TPU v7x, 32 devices: a whole 2x2x4 slice. The times are simulated.
32 devices in a mesh: sq: 32 (over z, y, x, core).
Axes of the slice: x: 2, y: 2, z: 4, core: 2. Of those that a mesh axis runs over, the one named last changes fastest.
Arguments:
- tokens: bfloat16 [1024, 2880], P('sq'), may hold values from -6 to 6
- norm_gain: float32 [2880], replicated, may hold values from 0.25 to 1.75
- expert_ids: int32 [1024, 4], P('sq'), may hold values from 0 to 7, all different within a row; in each aligned block of 32 rows (0 to 31, 32 to 63, ...) at most 17 rows name the same one
- combine_weight: float32 [1024, 4], P('sq'), may hold values from 0.05 to 0.6
- cotangent: bfloat16 [1024, 2880], P('sq'), may hold values from -6 to 6
- w_gate: bfloat16 [32, 2880, 720], P('sq'), may hold values from -0.109375 to 0.109375
- w_up: bfloat16 [32, 2880, 720], P('sq'), may hold values from -0.109375 to 0.109375
- w_down: bfloat16 [32, 720, 2880], P('sq'), may hold values from -0.109375 to 0.109375
Outputs:
- d_tokens: bfloat16 [1024, 2880], P('sq')
- grad_gate: bfloat16 [32, 2880, 720], P('sq')
- grad_up: bfloat16 [32, 2880, 720], P('sq')
- grad_down: bfloat16 [32, 720, 2880], P('sq')
Inputs may be any that keep to these rules, and one draw needn't show every extreme that they name: `expert_ids`: each row names 4 different experts; the rows of one device name any one expert at most 17 times, a bound that some block reaches.
All inputs are finite; a program needn't handle non-finite values.
Results may differ from a plain program's by a relative error of at most 0.0078.
Values may be sent and summed in bfloat16 or wider, within the bound.
No kernel may reach another device: no remote copies, remote signals or barrier semaphores. Data moves between devices by JAX's collectives and lax.ppermute only.
A program may use at most 128 MiB of HBM per device.

v0:
```python
import jax
import jax.numpy as jnp
from jax import lax
from jax.sharding import PartitionSpec as P

QUARTERS = 4


norm_eps = 1e-05
glu_alpha = 1.702


def contract_rows(left, right):
    return lax.dot_general(
        left, right, (((0,), (0,)), ((), ())), preferred_element_type=jnp.float32
    )


def contract_cols(left, right):
    return lax.dot_general(
        left, right, (((1,), (1,)), ((), ())), preferred_element_type=jnp.float32
    )


def local(tokens, norm_gain, expert_ids, combine_weight, cotangent, w_gate, w_up, w_down):
    devices = lax.axis_size("sq")
    tok_count, top_count = expert_ids.shape
    width = tokens.shape[1]
    expert_count = devices // QUARTERS
    slot_count = tok_count * top_count * QUARTERS // devices + 1
    pick_count = tok_count * top_count
    expert_slots = expert_count * slot_count
    token_f = tokens.astype(jnp.float32)
    rstd = lax.rsqrt(jnp.mean(token_f * token_f, axis=-1, keepdims=True) + norm_eps)
    normed = (token_f * rstd * norm_gain).astype(jnp.bfloat16)
    flat_ids = expert_ids.reshape(pick_count)
    onehot = (flat_ids[:, None] == jnp.arange(expert_count, dtype=jnp.int32)[None, :]).astype(
        jnp.float32
    )
    row_iota = lax.broadcasted_iota(jnp.int32, (pick_count, pick_count), 0)
    col_iota = lax.broadcasted_iota(jnp.int32, (pick_count, pick_count), 1)
    lower = (row_iota > col_iota).astype(jnp.float32)
    earlier = jnp.dot(lower, onehot, preferred_element_type=jnp.float32)
    slot = jnp.sum(earlier * onehot, axis=-1).astype(jnp.int32)
    position = flat_ids * slot_count + slot
    select = (position[:, None] == jnp.arange(expert_slots, dtype=jnp.int32)[None, :]).astype(
        jnp.float32
    )
    select = select.reshape(tok_count, top_count, expert_slots)
    token_select = jnp.sum(select, axis=1)
    weight_select = jnp.sum(select * combine_weight[:, :, None], axis=1)
    send_x = contract_rows(token_select.astype(jnp.bfloat16), normed).astype(jnp.bfloat16)
    send_dy = lax.dot_general(
        weight_select,
        cotangent.astype(jnp.float32),
        (((0,), (0,)), ((), ())),
        precision=lax.Precision.HIGHEST,
        preferred_element_type=jnp.float32,
    ).astype(jnp.bfloat16)
    rows_total = devices * slot_count

    def spread(buffer):
        shaped = buffer.reshape(expert_count, 1, slot_count, width)
        return jnp.broadcast_to(shaped, (expert_count, QUARTERS, slot_count, width)).reshape(
            devices, slot_count, width
        )

    got_x, got_dy = (
        lax.all_to_all(spread(send_x), "sq", split_axis=0, concat_axis=0, tiled=True),
        lax.all_to_all(spread(send_dy), "sq", split_axis=0, concat_axis=0, tiled=True),
    )
    x_in = got_x.reshape(rows_total, width)
    dy_e = got_dy.reshape(rows_total, width)
    gate_w = w_gate[0]
    up_w = w_up[0]
    down_w = w_down[0]
    gate = jnp.dot(x_in, gate_w, preferred_element_type=jnp.float32)
    up = jnp.dot(x_in, up_w, preferred_element_type=jnp.float32)
    sig = jax.nn.sigmoid(glu_alpha * gate)
    glu = gate * sig
    hid = (glu * (up + 1.0)).astype(jnp.bfloat16)
    d_hid = contract_cols(dy_e, down_w)
    d_up = (d_hid * glu).astype(jnp.bfloat16)
    d_gate = (d_hid * (up + 1.0) * (sig + glu_alpha * gate * sig * (1.0 - sig))).astype(
        jnp.bfloat16
    )
    partial_rows = (contract_cols(d_gate, gate_w) + contract_cols(d_up, up_w)).astype(jnp.bfloat16)
    grad_gate = contract_rows(x_in, d_gate).astype(jnp.bfloat16)[None]
    grad_up = contract_rows(x_in, d_up).astype(jnp.bfloat16)[None]
    grad_down = contract_rows(hid, dy_e).astype(jnp.bfloat16)[None]
    back = lax.all_to_all(
        partial_rows.reshape(devices, slot_count, width),
        "sq",
        split_axis=0,
        concat_axis=0,
        tiled=True,
    )
    summed = jnp.sum(
        back.reshape(expert_count, QUARTERS, slot_count, width).astype(jnp.float32), axis=1
    )
    d_rows = summed.astype(jnp.bfloat16).reshape(expert_slots, width)
    d_normed = jnp.dot(
        token_select.astype(jnp.bfloat16), d_rows, preferred_element_type=jnp.float32
    )
    scaled = d_normed * norm_gain
    mixed = jnp.mean(token_f * scaled, axis=-1, keepdims=True)
    d_tokens = (rstd * scaled - token_f * rstd * rstd * rstd * mixed).astype(jnp.bfloat16)
    return (d_tokens, grad_gate, grad_up, grad_down)


def solution(mesh):
    placed = (
        P("sq", None),
        P(),
        P("sq", None),
        P("sq", None),
        P("sq", None),
        P("sq", None, None),
        P("sq", None, None),
        P("sq", None, None),
    )
    return jax.shard_map(
        local,
        mesh=mesh,
        in_specs=placed,
        out_specs=(P("sq", None), P("sq", None, None), P("sq", None, None), P("sq", None, None)),
        check_vma=False,
    )
```

profile of v0, /device:TPU:0, one launch (start us, length us, event | category | flops | bytes accessed | tf_op | source)
XLA Modules:
  0.0 363.6 jit_solution(2204184415464816401)
XLA Ops:
  0.6 0.0 copy-start
  0.6 0.8 copy.24
  1.4 0.1 eq.29
  1.6 0.1 fusion.13
  1.7 0.1 convert_element_type.61
  1.8 0.1 copy.25
  1.9 0.7 multiply_add_fusion
  2.6 1.1 fusion.22
  3.7 0.8 convert_reduce_fusion
  4.5 1.4 convolution_convert_fusion.3
  5.9 0.3 broadcast_in_dim.16
  6.2 2.3 broadcast_in_dim.34
  8.5 7.4 %all-to-all-start.1 = ((bf16[32,17,2880]{2,1,0:T(8,128)(2,1)}), bf16[32,17,2880]{2,1,0:T(8,128)(2,1)}, u32[]{:S(2)}, u32[]{:S(2)}) async-start(bf16[32,17,2880]{2,1,0:T(8,128)(2,1)} %bitcast.40), calls=%async_computation.1 | async-start | bytes 9043968 | tf_op jit(solution)/shard_map/all_to_all | solution.py:69
  15.9 0.0 copy-done
  15.9 0.9 convolution_convert_fusion.4
  16.8 0.3 broadcast_in_dim.14
  17.1 99.8 %all-to-all-done.1 = bf16[32,17,2880]{2,1,0:T(8,128)(2,1)} async-done(((bf16[32,17,2880]{2,1,0:T(8,128)(2,1)}), bf16[32,17,2880]{2,1,0:T(8,128)(2,1)}, u32[]{:S(2)}, u32[]{:S(2)}) %all-to-all-start.1) | async-done | bytes 3133472 | tf_op jit(solution)/shard_map/all_to_all | solution.py:69
  116.9 2.4 broadcast_in_dim.15
  119.4 4.1 %all-to-all-start = ((bf16[32,17,2880]{2,1,0:T(8,128)(2,1)}), bf16[32,17,2880]{2,1,0:T(8,128)(2,1)}, u32[]{:S(2)}, u32[]{:S(2)}) async-start(bf16[32,17,2880]{2,1,0:T(8,128)(2,1)} %bitcast.41), calls=%async_computation | async-start | bytes 9043968 | tf_op jit(solution)/shard_map/all_to_all | solution.py:70
  123.5 3.9 %reshape.71 = bf16[544,2880]{1,0:T(8,128)(2,1)S(1)} reshape(bf16[32,17,2880]{2,1,0:T(8,128)(2,1)} %all-to-all-done.1) | data formatting | bytes 6266880 | tf_op jit(solution)/shard_map/reshape | solution.py:72
  127.4 6.2 %fusion.5 = f32[544,720]{1,0:T(8,128)} fusion(bf16[544,2880]{1,0:T(8,128)(2,1)S(1)} %reshape.71, bf16[1,2880,720]{1,2,0:T(8,128)(2,1)} %param.13), kind=kOutput, calls=%fused_computation.10 | convolution fusion | flops 2256076800 | bytes 8847360 | tf_op jit(solution)/shard_map/dot_general | solution.py:77
  133.6 6.2 %fusion.8 = f32[544,720]{1,0:T(8,128)} fusion(bf16[544,2880]{1,0:T(8,128)(2,1)S(1)} %reshape.71, bf16[1,2880,720]{1,2,0:T(8,128)(2,1)} %param.14), kind=kOutput, calls=%fused_computation.13 | convolution fusion | flops 2256076800 | bytes 8847360 | tf_op jit(solution)/shard_map/dot_general | solution.py:78
  139.8 84.7 %all-to-all-done = bf16[32,17,2880]{2,1,0:T(8,128)(2,1)} async-done(((bf16[32,17,2880]{2,1,0:T(8,128)(2,1)}), bf16[32,17,2880]{2,1,0:T(8,128)(2,1)}, u32[]{:S(2)}, u32[]{:S(2)}) %all-to-all-start) | async-done | bytes 3133472 | tf_op jit(solution)/shard_map/all_to_all | solution.py:70
  224.5 5.2 %reshape.69 = bf16[544,2880]{1,0:T(8,128)(2,1)} reshape(bf16[32,17,2880]{2,1,0:T(8,128)(2,1)} %all-to-all-done) | data formatting | bytes 6266880 | tf_op jit(solution)/shard_map/reshape | solution.py:73
  229.7 7.3 %multiply_convert_fusion.1 = (bf16[544,720]{1,0:T(8,128)(2,1)S(1)}, bf16[544,720]{1,0:T(8,128)(2,1)S(1)}) fusion(f32[544,720]{1,0:T(8,128)} %fusion.5, f32[544,720]{1,0:T(8,128)} %fusion.8, bf16[544,2880]{1,0:T(8,128)(2,1)} %reshape.69, bf16[1,720,2880]{2,1,0:T(8,128)(2,1)} %param.15), kind=kOutput, calls=%fused_computation.21 | convolution fusion | flops 2261952000 | bytes 11980800 | tf_op jit(solution)/shard_map/dot_general | solution.py:20
  237.1 0.0 copy-start.5
  237.1 0.0 copy-start.6
  237.1 5.2 %fusion.3 = f32[544,2880]{1,0:T(8,128)S(1)} fusion(bf16[544,720]{1,0:T(8,128)(2,1)S(1)} %get-tuple-element.7, bf16[1,2880,720]{1,2,0:T(8,128)(2,1)} %param.13), kind=kOutput, calls=%fused_computation.8 | convolution fusion | flops 2256076800 | bytes 11197440 | tf_op jit(solution)/shard_map/dot_general | solution.py:20
  242.3 0.0 copy-done.5
  242.3 0.0 copy-done.6
  242.3 6.4 %add_convert_fusion = bf16[544,2880]{1,0:T(8,128)(2,1)} fusion(f32[544,2880]{1,0:T(8,128)S(1)} %fusion.3, bf16[544,720]{1,0:T(8,128)(2,1)S(1)} %get-tuple-element.6, bf16[1,2880,720]{1,2,0:T(8,128)(2,1)} %param.14), kind=kOutput, calls=%fused_computation | convolution fusion | flops 2259210240 | bytes 14330880 | tf_op jit(solution)/shard_map/dot_general | solution.py:20
  248.7 5.1 %reshape.72 = bf16[32,17,2880]{2,1,0:T(8,128)(2,1)} reshape(bf16[544,2880]{1,0:T(8,128)(2,1)} %add_convert_fusion) | data formatting | bytes 6266880 | tf_op jit(solution)/shard_map/reshape | solution.py:92
  253.8 4.1 %all-to-all-start.2 = ((bf16[32,17,2880]{2,1,0:T(8,128)(2,1)}), bf16[32,17,2880]{2,1,0:T(8,128)(2,1)}, u32[]{:S(2)}, u32[]{:S(2)}) async-start(bf16[32,17,2880]{2,1,0:T(8,128)(2,1)} %reshape.72), calls=%async_computation.2 | async-start | bytes 9043968 | tf_op jit(solution)/shard_map/all_to_all | solution.py:91
  257.9 0.0 copy-start.7
  257.9 6.4 %fusion = bf16[1,2880,720]{1,2,0:T(8,128)(2,1)} fusion(bf16[544,2880]{1,0:T(8,128)(2,1)S(1)} %reshape.71, bf16[544,720]{1,0:T(8,128)(2,1)} %copy-done.5), kind=kOutput, calls=%fused_computation.5 | convolution fusion | flops 2258150400 | bytes 8064000 | tf_op jit(solution)/shard_map/dot_general | solution.py:14
  264.3 0.0 copy-done.7
  264.3 5.2 %fusion.1 = bf16[1,2880,720]{1,2,0:T(8,128)(2,1)} fusion(bf16[544,2880]{1,0:T(8,128)(2,1)S(1)} %reshape.71, bf16[544,720]{1,0:T(8,128)(2,1)S(1)} %copy-done.7), kind=kOutput, calls=%fused_computation.6 | convolution fusion | flops 2258150400 | bytes 8064000 | tf_op jit(solution)/shard_map/dot_general | solution.py:14
  269.5 0.0 copy-done.2
  269.5 0.0 copy-done.8
  269.6 0.0 copy-done.9
  269.6 5.4 %fusion.2 = bf16[1,720,2880]{2,1,0:T(8,128)(2,1)} fusion(bf16[544,2880]{1,0:T(8,128)(2,1)S(1)} %copy-done.2, f32[544,720]{1,0:T(8,128)S(1)} %copy-done.9, f32[544,720]{1,0:T(8,128)S(1)} %copy-done.8), kind=kOutput, calls=%fused_computation.7 | convolution fusion | flops 2261283840 | bytes 10414080 | tf_op jit(solution)/shard_map/dot_general | solution.py:14
  275.0 83.9 %all-to-all-done.2 = bf16[32,17,2880]{2,1,0:T(8,128)(2,1)} async-done(((bf16[32,17,2880]{2,1,0:T(8,128)(2,1)}), bf16[32,17,2880]{2,1,0:T(8,128)(2,1)}, u32[]{:S(2)}, u32[]{:S(2)}) %all-to-all-start.2) | async-done | bytes 3133472 | tf_op jit(solution)/shard_map/all_to_all | solution.py:91
  358.9 3.1 bitcast_reduce_fusion
  361.9 0.4 reshape.74
  362.3 0.0 copy-done.3
  362.3 0.0 copy-done.4
  362.4 0.4 fusion.23
  362.7 0.8 fusion.21
  (10 shorter events, 0.0 us)
Async XLA Ops:
  0.6 15.3 %copy-start = (bf16[32,2880]{1,0:T(8,128)(2,1)S(1)}, bf16[32,2880]{1,0:T(8,128)(2,1)}, u32[]{:S(2)}) copy-start(bf16[32,2880]{1,0:T(8,128)(2,1)} %param.12) | copy-start | bytes 552964
  8.5 108.4 %all-to-all-start.1 = ((bf16[32,17,2880]{2,1,0:T(8,128)(2,1)}), bf16[32,17,2880]{2,1,0:T(8,128)(2,1)}, u32[]{:S(2)}, u32[]{:S(2)}) async-start(bf16[32,17,2880]{2,1,0:T(8,128)(2,1)} %bitcast.40), calls=%async_computation.1 | async-start | bytes 9043968 | tf_op jit(solution)/shard_map/all_to_all | solution.py:69
  119.4 105.1 %all-to-all-start = ((bf16[32,17,2880]{2,1,0:T(8,128)(2,1)}), bf16[32,17,2880]{2,1,0:T(8,128)(2,1)}, u32[]{:S(2)}, u32[]{:S(2)}) async-start(bf16[32,17,2880]{2,1,0:T(8,128)(2,1)} %bitcast.41), calls=%async_computation | async-start | bytes 9043968 | tf_op jit(solution)/shard_map/all_to_all | solution.py:70
  237.1 5.2 %copy-start.5 = (bf16[544,720]{1,0:T(8,128)(2,1)}, bf16[544,720]{1,0:T(8,128)(2,1)S(1)}, u32[]{:S(2)}) copy-start(bf16[544,720]{1,0:T(8,128)(2,1)S(1)} %get-tuple-element.7) | copy-start | bytes 2350084
  237.1 5.2 %copy-start.6 = (bf16[544,720]{1,0:T(8,128)(2,1)}, bf16[544,720]{1,0:T(8,128)(2,1)S(1)}, u32[]{:S(2)}) copy-start(bf16[544,720]{1,0:T(8,128)(2,1)S(1)} %get-tuple-element.6) | copy-start | bytes 2350084
  253.8 105.0 %all-to-all-start.2 = ((bf16[32,17,2880]{2,1,0:T(8,128)(2,1)}), bf16[32,17,2880]{2,1,0:T(8,128)(2,1)}, u32[]{:S(2)}, u32[]{:S(2)}) async-start(bf16[32,17,2880]{2,1,0:T(8,128)(2,1)} %reshape.72), calls=%async_computation.2 | async-start | bytes 9043968 | tf_op jit(solution)/shard_map/all_to_all | solution.py:91
  257.9 6.4 %copy-start.7 = (bf16[544,720]{1,0:T(8,128)(2,1)S(1)}, bf16[544,720]{1,0:T(8,128)(2,1)}, u32[]{:S(2)}) copy-start(bf16[544,720]{1,0:T(8,128)(2,1)} %copy-done.6) | copy-start | bytes 2350084
  264.3 5.2 %copy-start.2 = (bf16[544,2880]{1,0:T(8,128)(2,1)S(1)}, bf16[544,2880]{1,0:T(8,128)(2,1)}, u32[]{:S(2)}) copy-start(bf16[544,2880]{1,0:T(8,128)(2,1)} %reshape.69) | copy-start | bytes 9400324
  264.3 5.2 %copy-start.8 = (f32[544,720]{1,0:T(8,128)S(1)}, f32[544,720]{1,0:T(8,128)}, u32[]{:S(2)}) copy-start(f32[544,720]{1,0:T(8,128)} %fusion.5) | copy-start | bytes 4700164
  264.3 5.2 %copy-start.9 = (f32[544,720]{1,0:T(8,128)S(1)}, f32[544,720]{1,0:T(8,128)}, u32[]{:S(2)}) copy-start(f32[544,720]{1,0:T(8,128)} %fusion.8) | copy-start | bytes 4700164
  275.0 87.4 %copy-start.3 = (bf16[32,2880]{1,0:T(8,128)(2,1)S(1)}, bf16[32,2880]{1,0:T(8,128)(2,1)}, u32[]{:S(2)}) copy-start(bf16[32,2880]{1,0:T(8,128)(2,1)} %param.8) | copy-start | bytes 552964
  275.0 87.4 %copy-start.4 = (f32[2880]{0:T(1024)S(1)}, f32[2880]{0:T(1024)}, u32[]{:S(2)}) copy-start(f32[2880]{0:T(1024)} %param.9) | copy-start | bytes 34564
  358.9 4.7 %copy-start.1 = (bf16[32,2880]{1,0:T(8,128)(2,1)S(1)}, bf16[32,2880]{1,0:T(8,128)(2,1)}, u32[]{:S(2)}) copy-start(bf16[32,2880]{1,0:T(8,128)(2,1)} %param.12) | copy-start | bytes 552964
where the time goes:
time: 364 us
  waiting for transfers between devices  268 us (74%)
  matrix products  51 us (14%)
  local copies, waits for them, and re-layouts  21.2 us (6%)
  starting transfers between devices  15.6 us (4%)
  other arithmetic  6.49 us (2%)
    all_to_all x1, waiting for transfers between devices, local(): lax.all_to_all(spread(send_x), 'sq', split_axis=0, concat_axis=0, tiled=T...  99.8 us
    all_to_all x1, waiting for transfers between devices, local(): lax.all_to_all(spread(send_dy), 'sq', split_axis=0, concat_axis=0, tiled=...  84.7 us
    all_to_all x1, waiting for transfers between devices, local(): lax.all_to_all(partial_rows.reshape(devices, slot_count, width), 'sq', sp...  83.9 us
    dot_general x3, matrix products, contract_cols(): lax.dot_general(left, right, (((1,), (1,)), ((), ())), preferred_element_...  18.9 us
    dot_general x4, matrix products, contract_rows(): lax.dot_general(left, right, (((0,), (0,)), ((), ())), preferred_element_...  18.4 us
    all_to_all x1, starting transfers between devices, local(): lax.all_to_all(spread(send_x), 'sq', split_axis=0, concat_axis=0, tiled=T...  7.41 us
  transfers between devices with their start and end apart: 3, of which 3 were waited for; matrix products, arithmetic and copies ran while one was open for 9% of the time, Pallas kernels for 0%

commit v1 on v0

v1 whole, which is shorter than its diff:
```python
import jax
import jax.numpy as jnp
from jax import lax
from jax.experimental.layout import Layout, with_layout_constraint
from jax.sharding import PartitionSpec as P

QUARTERS = 4
CORE, PAIR, SIDE = 1, 2, 4
TILE = 8

norm_eps = 1e-05
glu_alpha = 1.702


def contract_rows(left, right):
    return lax.dot_general(
        left, right, (((0,), (0,)), ((), ())), preferred_element_type=jnp.float32
    )


def contract_cols(left, right):
    return lax.dot_general(
        left, right, (((1,), (1,)), ((), ())), preferred_element_type=jnp.float32
    )


def row_major(value):
    return with_layout_constraint(value, Layout(major_to_minor=(0, 1)))


def behind(values, first):
    return lax.optimization_barrier((values, first))[0]


def three_parts(value):
    first = lax.reduce_precision(value, 8, 7)
    rest = value - first
    second = lax.reduce_precision(rest, 8, 7)
    return [part.astype(jnp.bfloat16) for part in (first, second, rest - second)]


def local(tokens, norm_gain, expert_ids, combine_weight, cotangent, w_gate, w_up, w_down):
    devices = lax.axis_size("sq")
    tok_count, top_count = expert_ids.shape
    width = tokens.shape[1]
    expert_count = devices // QUARTERS
    planes = expert_count // 2
    slot_count = tok_count * top_count * QUARTERS // devices + 1
    slots = -(-slot_count * planes // TILE) * TILE
    column = planes * tok_count
    kept = 2 * slots
    expert = lax.axis_index("sq") // QUARTERS
    plane = expert // 2

    def flip(value, bit):
        return lax.ppermute(row_major(value), "sq", [(i, i ^ bit) for i in range(devices)])

    def shift(value, by):
        step = by * 2 * QUARTERS
        pairs = [(i, (i + step) % devices) for i in range(devices)]
        return lax.ppermute(row_major(value), "sq", pairs)

    token_f = row_major(tokens).astype(jnp.float32)
    rstd = lax.rsqrt(jnp.mean(token_f * token_f, axis=-1, keepdims=True) + norm_eps)
    normed = (token_f * rstd * norm_gain).astype(jnp.bfloat16)

    picked = expert_ids[:, :, None] == jnp.arange(expert_count, dtype=jnp.int32)[None, None, :]
    weight = jnp.sum(jnp.where(picked, combine_weight[:, :, None], 0.0), axis=1)
    payload = row_major(jnp.concatenate([normed] + three_parts(weight), axis=1))

    lines = [
        [plane * 2 * QUARTERS + place for plane in range(planes)] for place in range(2 * QUARTERS)
    ]

    def gather_column(block):
        return row_major(
            lax.all_gather(block, "sq", axis=0, tiled=True, axis_index_groups=lines)
        )

    column_x = gather_column(payload)

    parts = column_x[:, width:].astype(jnp.float32).reshape(column, 3, expert_count)
    column_weight = parts[:, 0] + parts[:, 1] + parts[:, 2]
    slot_iota = lax.broadcasted_iota(jnp.int32, (slots, column), 0)
    earlier = lax.broadcasted_iota(jnp.int32, (column, column), 0) < lax.broadcasted_iota(
        jnp.int32, (column, column), 1
    )

    def choose(which):
        experts = jnp.arange(expert_count, dtype=jnp.int32)
        mine = jnp.sum(jnp.where(experts[None, :] == which, column_weight, 0.0), axis=1)
        mask = mine > 0.0
        slot = jnp.sum(jnp.where(earlier & mask[:, None], 1, 0), axis=0)
        hit = (slot_iota == slot[None, :]) & mask[None, :]
        row_weight = jnp.sum(jnp.where(hit, mine[None, :], 0.0), axis=1, keepdims=True)
        return hit.astype(jnp.bfloat16), row_weight

    own_select, own_weight = choose(expert)
    far_select, far_weight = choose(expert ^ 1)

    def rows_x(select):
        return jnp.dot(select, column_x[:, :width], preferred_element_type=jnp.float32).astype(
            jnp.bfloat16
        )

    own_x = rows_x(own_select)
    far_x = rows_x(far_select)
    side_x = flip(far_x, SIDE)
    pair_x = flip(own_x, PAIR)
    across_x = flip(far_x, PAIR | SIDE)
    column_cot = behind(gather_column(cotangent), (side_x, pair_x, across_x))

    def rows_dy(select, row_weight):
        rows = jnp.dot(select, column_cot, preferred_element_type=jnp.float32)
        return (rows * row_weight).astype(jnp.bfloat16)

    own_dy = rows_dy(own_select, own_weight)
    far_dy = rows_dy(far_select, far_weight)
    side_dy = flip(far_dy, SIDE)
    pair_dy = flip(own_dy, PAIR)

    def both_cores(first, second):
        rows = jnp.concatenate([first, second], axis=0)
        return jnp.concatenate([rows, flip(rows, CORE)], axis=0)

    gate_w = w_gate[0]
    up_w = w_up[0]
    down_w = w_down[0]

    def forward(x_in):
        gate = jnp.dot(x_in, gate_w, preferred_element_type=jnp.float32)
        up = jnp.dot(x_in, up_w, preferred_element_type=jnp.float32)
        return gate, up

    def hidden(gate, up, dy_e):
        sig = jax.nn.sigmoid(glu_alpha * gate)
        glu = gate * sig
        hid = (glu * (up + 1.0)).astype(jnp.bfloat16)
        d_hid = contract_cols(dy_e, down_w)
        d_up = (d_hid * glu).astype(jnp.bfloat16)
        d_gate = (d_hid * (up + 1.0) * (sig + glu_alpha * gate * sig * (1.0 - sig))).astype(
            jnp.bfloat16
        )
        return hid, d_gate, d_up

    def row_gradient(d_gate, d_up, first, last):
        return (
            contract_cols(d_gate, gate_w[first:last]) + contract_cols(d_up, up_w[first:last])
        ).astype(jnp.bfloat16)

    own_x, side_x, pair_x, across_x = behind((own_x, side_x, pair_x, across_x), (own_dy, far_dy))
    chip_x = both_cores(own_x, side_x)
    pair_x = both_cores(pair_x, across_x)
    chip_forward = forward(chip_x)
    side_dy, pair_dy = behind((side_dy, pair_dy), chip_forward)
    across_dy = flip(side_dy, PAIR)
    chip_dy = both_cores(own_dy, side_dy)
    pair_forward = forward(behind(pair_x, chip_dy))
    chip_hid, chip_d_gate, chip_d_up = hidden(*chip_forward, chip_dy)
    chip_rows = row_gradient(chip_d_gate, chip_d_up, 0, width)
    chip_sum = chip_rows[:kept].astype(jnp.float32) + flip(chip_rows[kept:], CORE).astype(
        jnp.float32
    )
    side_sum = flip(chip_sum[slots:].astype(jnp.bfloat16), SIDE)

    pair_core_dy = flip(pair_dy, CORE)
    across_dy = behind(across_dy, (chip_sum, pair_forward))
    pair_dy = jnp.concatenate([pair_dy, across_dy, pair_core_dy, flip(across_dy, CORE)], axis=0)
    pair_hid, pair_d_gate, pair_d_up = hidden(*pair_forward, pair_dy)

    cut = -(-width // 2 // 256) * 256
    spans = [(0, cut), (cut, width)]

    def core_sum(rows, from_core):
        total = rows[:kept].astype(jnp.float32) + from_core.astype(jnp.float32)
        return total.astype(jnp.bfloat16)

    def to_pair(rows):
        return flip(rows[:slots], PAIR), flip(rows[slots:], PAIR | SIDE)

    rows_first = row_gradient(pair_d_gate, pair_d_up, *spans[0])
    core_first = flip(rows_first[kept:], CORE)
    rows_second = row_gradient(*behind((pair_d_gate, pair_d_up), rows_first), *spans[1])
    core_second = flip(rows_second[kept:], CORE)
    sum_first = core_sum(rows_first, core_first)
    sent_first = to_pair(sum_first)

    x_in = jnp.concatenate([chip_x, pair_x], axis=0)
    dy_e = jnp.concatenate([chip_dy, pair_dy], axis=0)
    hid = jnp.concatenate([chip_hid, pair_hid], axis=0)
    d_gate = jnp.concatenate([chip_d_gate, pair_d_gate], axis=0)
    d_up = jnp.concatenate([chip_d_up, pair_d_up], axis=0)

    def to_column(span, from_pair, from_across):
        first, last = span
        own_rows = chip_sum[:slots, first:last] + from_pair.astype(jnp.float32)
        far_rows = side_sum[:, first:last].astype(jnp.float32) + from_across.astype(jnp.float32)
        return row_major(
            contract_rows(own_select, own_rows.astype(jnp.bfloat16))
            + contract_rows(far_select, far_rows.astype(jnp.bfloat16))
        )

    def to_tokens(d_column):
        blocks = d_column.reshape(planes, tok_count, d_column.shape[1])
        total = lax.dynamic_index_in_dim(blocks, plane, 0, False)
        got = []
        for s in range(1, planes):
            block = lax.dynamic_index_in_dim(blocks, (plane + s) % planes, 0, False)
            got.append(shift(block.astype(jnp.bfloat16), s))
        return total, got

    def added(total, got):
        for block in got:
            total = total + block.astype(jnp.float32)
        return total

    def weight_gradient(left, right, first):
        return contract_rows(*behind((left, right), first)).astype(jnp.bfloat16)

    sum_second = core_sum(*behind((rows_second, core_second), sum_first))
    sent_second = to_pair(sum_second)
    grad_gate = weight_gradient(x_in, d_gate, (sum_second, chip_sum))
    d_column = to_column(spans[0], *behind(sent_first, grad_gate))
    first_half = to_tokens(d_column)
    grad_up = weight_gradient(x_in, d_up, d_column)
    first_half = added(*behind(first_half, grad_up))
    second_half = to_tokens(to_column(spans[1], *behind(sent_second, first_half)))
    grad_down = weight_gradient(hid, dy_e, first_half)
    second_half = added(*behind(second_half, grad_down))
    grads = [grad[None] for grad in (grad_gate, grad_up, grad_down)]
    d_normed = jnp.concatenate([first_half, second_half], axis=1)

    scaled = d_normed * norm_gain
    mixed = jnp.mean(token_f * scaled, axis=-1, keepdims=True)
    d_tokens = (rstd * scaled - token_f * rstd * rstd * rstd * mixed).astype(jnp.bfloat16)
    return (d_tokens, *grads)


def solution(mesh):
    placed = (
        P("sq", None),
        P(),
        P("sq", None),
        P("sq", None),
        P("sq", None),
        P("sq", None, None),
        P("sq", None, None),
        P("sq", None, None),
    )
    return jax.shard_map(
        local,
        mesh=mesh,
        in_specs=placed,
        out_specs=(P("sq", None), P("sq", None, None), P("sq", None, None), P("sq", None, None)),
        check_vma=False,
    )
```

time: 364 us -> 117 us (0.32)
  waiting for transfers between devices: 268 us -> 9.84 us
  blocking collectives: 0 us -> 38.2 us
  local copies, waits for them, and re-layouts: 21.2 us -> 1.93 us
  matrix products: 51 us -> 37 us
  starting transfers between devices: 15.6 us -> 23.1 us
    all_to_all x3 -> x0, waiting for transfers between devices: 268 us -> none  [the longest x1 99.8 us: local(): lax.all_to_all(spread(send_x), 'sq', split_axis=0, concat_axis=0, tiled=T...]
    all_gather x0 -> x2, blocking collectives: none -> 38.2 us  [gather_column(): lax.all_gather(block, 'sq', axis=0, tiled=True, axis_index_groups=lines)]
    ppermute x0 -> x25, starting transfers between devices: none -> 23.1 us  [the longest x19 15.1 us: flip(): lax.ppermute(row_major(value), 'sq', [(i, i ^ bit) for i in range(devices)])]
    all_to_all x3 -> x0, starting transfers between devices: 15.6 us -> none  [the longest x1 7.41 us: local(): lax.all_to_all(spread(send_x), 'sq', split_axis=0, concat_axis=0, tiled=T...]
    reshape x4 -> x1, local copies, waits for them, and re-layouts: 14.6 us -> 0.05 us  [local(): column_x[:, width:].astype(jnp.float32).reshape(column, 3, expert_count)]
    ppermute x0 -> x25, waiting for transfers between devices: none -> 9.84 us  [the longest x19 8.64 us: flip(): lax.ppermute(row_major(value), 'sq', [(i, i ^ bit) for i in range(devices)])]
    dot_general x3 -> x8, matrix products: 18.9 us -> 10.3 us  [contract_cols(): lax.dot_general(left, right, (((1,), (1,)), ((), ())), preferred_element_...]
    broadcast_in_dim x4 -> x0, local copies, waits for them, and re-layouts: 5.4 us -> none  [spread(): jnp.broadcast_to(shaped, (expert_count, QUARTERS, slot_count, width))]
  transfers between devices with their start and end apart: 3 -> 25, of which waited for: 3 -> 7; matrix products, arithmetic and copies ran while one was open for 9% -> 33% of each run, Pallas kernels for 0% -> 0%
where the time goes in v1:
time: 117 us
  blocking collectives  38.2 us (33%)
  matrix products  37 us (32%)
  starting transfers between devices  23.1 us (20%)
  waiting for transfers between devices  9.84 us (8%)
  other arithmetic  5.75 us (5%)
  local copies, waits for them, and re-layouts  1.93 us (2%)
  between operations  1.35 us (1%)
    all_gather x2, blocking collectives, gather_column(): lax.all_gather(block, 'sq', axis=0, tiled=True, axis_index_groups=lines)  38.2 us
    dot_general x7, matrix products, contract_rows(): lax.dot_general(left, right, (((0,), (0,)), ((), ())), preferred_element_...  16.8 us
    ppermute x19, starting transfers between devices, flip(): lax.ppermute(row_major(value), 'sq', [(i, i ^ bit) for i in range(devices)])  15.1 us
    dot_general x8, matrix products, contract_cols(): lax.dot_general(left, right, (((1,), (1,)), ((), ())), preferred_element_...  10.3 us
    ppermute x19, waiting for transfers between devices, flip(): lax.ppermute(row_major(value), 'sq', [(i, i ^ bit) for i in range(devices)])  8.64 us
    ppermute x6, starting transfers between devices, shift(): return lax.ppermute(row_major(value), 'sq', pairs)  8.05 us
    dot_general x2, matrix products, forward(): gate = jnp.dot(x_in, gate_w, preferred_element_type=jnp.float32)  5.54 us
    dot_general x2, matrix products, forward(): up = jnp.dot(x_in, up_w, preferred_element_type=jnp.float32)  3.26 us
  transfers between devices with their start and end apart: 25, of which 7 were waited for; matrix products, arithmetic and copies ran while one was open for 33% of the time, Pallas kernels for 0%

profile of v1, /device:TPU:0, one launch (start us, length us, event | category | flops | bytes accessed | tf_op | source)
XLA Modules:
  0.0 117.2 jit_solution(6260189874429159662)
XLA Ops:
  0.6 0.7 select_reduce_fusion.4
  1.6 1.1 fusion.56
  2.7 1.0 fusion.51
  3.8 20.9 %all_gather.6 = bf16[128,2904]{1,0:T(8,128)(2,1)S(1)} all-gather(bf16[32,2904]{1,0:T(8,128)(2,1)S(1)} %concatenate.47), channel_id=1, replica_groups={{0,8,16,24},{1,9,17,25},{2,10,18,26},{3,11,19,27},{4,12,20,28},{5,13,21..., dimensions={0}, use_global_device_ids=true | all-gather | bytes 929280 | tf_op jit(solution)/shard_map/all_gather | solution.py:77
  25.4 1.6 %collective-permute-start = (bf16[72,2880]{1,0:T(8,128)(2,1)S(1)}, bf16[72,2880]{1,0:T(8,128)(2,1)S(1)}, u32[]{:S(2)}, u32[]{:S(2)}) collective-permute-start(bf16[72,2880]{1,0:T(8,128)(2,1)S(1)} %convolution_convert_fusion.4), channel_id=1, source_target_pairs={{0,4},{1,5},{2,6},{3,7},{4,0},{5,1},{6,2},{7,3},{8,12},{9,13},{10,... | collective-permute-start | bytes 1244168 | tf_op jit(solution)/shard_map/ppermute | solution.py:56
  27.0 1.4 %collective-permute-start.2 = (bf16[72,2880]{1,0:T(8,128)(2,1)S(1)}, bf16[72,2880]{1,0:T(8,128)(2,1)S(1)}, u32[]{:S(2)}, u32[]{:S(2)}) collective-permute-start(bf16[72,2880]{1,0:T(8,128)(2,1)S(1)} %convolution_convert_fusion.4), channel_id=1, source_target_pairs={{0,6},{1,7},{2,4},{3,5},{4,2},{5,3},{6,0},{7,1},{8,14},{9,15},{10,... | collective-permute-start | bytes 1244168 | tf_op jit(solution)/shard_map/ppermute | solution.py:56
  28.8 0.6 collective-permute-start.1
  29.7 17.3 %all_gather.7 = bf16[128,2880]{1,0:T(8,128)(2,1)S(1)} all-gather(bf16[32,2880]{1,0:T(8,128)(2,1)S(1)} %copy-done.1), channel_id=1, replica_groups={{0,8,16,24},{1,9,17,25},{2,10,18,26},{3,11,19,27},{4,12,20,28},{5,13,21..., dimensions={0}, use_global_device_ids=true | all-gather | bytes 921600 | tf_op jit(solution)/shard_map/all_gather | solution.py:77
  47.5 1.6 %collective-permute-start.3 = (bf16[72,2880]{1,0:T(8,128)(2,1)S(1)}, bf16[72,2880]{1,0:T(8,128)(2,1)S(1)}, u32[]{:S(2)}, u32[]{:S(2)}) collective-permute-start(bf16[72,2880]{1,0:T(8,128)(2,1)S(1)} %fusion.23), channel_id=1, source_target_pairs={{0,4},{1,5},{2,6},{3,7},{4,0},{5,1},{6,2},{7,3},{8,12},{9,13},{10,... | collective-permute-start | bytes 1244168 | tf_op jit(solution)/shard_map/ppermute | solution.py:56
  49.1 1.5 %collective-permute-start.4 = (bf16[72,2880]{1,0:T(8,128)(2,1)S(1)}, bf16[72,2880]{1,0:T(8,128)(2,1)S(1)}, u32[]{:S(2)}, u32[]{:S(2)}) collective-permute-start(bf16[72,2880]{1,0:T(8,128)(2,1)S(1)} %get-tuple-element.94), channel_id=1, source_target_pairs={{0,2},{1,3},{2,0},{3,1},{4,6},{5,7},{6,4},{7,5},{8,10},{9,11},{10,... | collective-permute-start | bytes 1244168 | tf_op jit(solution)/shard_map/ppermute | solution.py:56
  50.8 0.6 collective-permute-start.9
  51.5 1.6 %collective-permute-done.5 = bf16[144,2880]{1,0:T(8,128)(2,1)S(1)} collective-permute-done((bf16[144,2880]{1,0:T(8,128)(2,1)S(1)}, bf16[144,2880]{1,0:T(8,128)(2,1)S(1)}, u32[]{:S(2)}, u32[]{:S(2)}) %collective-permute-start.5) | collective-permute-done | bytes 829472 | tf_op jit(solution)/shard_map/ppermute | solution.py:56
  53.4 3.9 %fusion.14 = f32[288,720]{1,0:T(8,128)S(1)} fusion(bf16[288,2880]{1,0:T(8,128)(2,1)S(1)} %get-tuple-element.75, bf16[1,2880,720]{1,2,0:T(8,128)(2,1)} %param.13), kind=kOutput, calls=%fused_computation.17 | convolution fusion | flops 1194393600 | bytes 6635520 | tf_op jit(solution)/shard_map/dot_general | solution.py:131
  57.3 1.6 %fusion.8 = f32[288,720]{1,0:T(8,128)S(1)} fusion(bf16[288,2880]{1,0:T(8,128)(2,1)S(1)} %get-tuple-element.75, bf16[1,2880,720]{1,2,0:T(8,128)(2,1)S(1)} %bitcast.86), kind=kOutput, calls=%fused_computation.11 | convolution fusion | flops 1194393600 | bytes 6635520 | tf_op jit(solution)/shard_map/dot_general | solution.py:132
  59.0 0.6 collective-permute-start.8
  59.9 1.6 %fusion.10 = f32[288,720]{1,0:T(8,128)S(1)} fusion(bf16[288,2880]{1,0:T(8,128)(2,1)S(1)} %pad_maximum_fusion.1, bf16[1,2880,720]{1,2,0:T(8,128)(2,1)S(1)} %bitcast.95), kind=kOutput, calls=%fused_computation.13 | convolution fusion | flops 1194393600 | bytes 6635520 | tf_op jit(solution)/shard_map/dot_general | solution.py:131
  61.5 0.6 collective-permute-start.10
  62.3 1.6 %fusion.4 = f32[288,720]{1,0:T(8,128)S(1)} fusion(bf16[288,2880]{1,0:T(8,128)(2,1)S(1)} %pad_maximum_fusion.1, bf16[1,2880,720]{1,2,0:T(8,128)(2,1)S(1)} %bitcast.86), kind=kOutput, calls=%fused_computation.7 | convolution fusion | flops 1194393600 | bytes 6635520 | tf_op jit(solution)/shard_map/dot_general | solution.py:132
  64.0 0.4 slice-done.2
  64.4 1.8 %multiply_convert_fusion.1 = (bf16[288,720]{1,0:T(8,128)(2,1)S(1)}, bf16[288,720]{1,0:T(8,128)(2,1)S(1)}, bf16[288,720]{1,0:T(8,128)(2,1)S(1)}) fusion(f32[288,720]{1,0:T(8,128)S(1)} %fusion.8, f32[288,720]{1,0:T(8,128)S(1)} %fusion.14, bf16[1,720,2880]{2,1,0:T(8,128)(2,1)S(1)} %bitcast.93, bf16[144,2880]{1,0:T(8,128)(2,1)S(1)} %collective-permute-done.6, ...), kind=kOutput, calls=%fused_computation.57 | convolution fusion | flops 1202895360 | bytes 8709120 | tf_op jit(solution)/shard_map/dot_general | solution.py:22
  66.2 1.6 %fusion.6 = f32[288,2880]{1,0:T(8,128)S(1)} fusion(bf16[288,720]{1,0:T(8,128)(2,1)S(1)} %get-tuple-element.70, bf16[1,2880,720]{1,2,0:T(8,128)(2,1)S(1)} %bitcast.86), kind=kOutput, calls=%fused_computation.9 | convolution fusion | flops 1194393600 | bytes 7879680 | tf_op jit(solution)/shard_map/dot_general | solution.py:22
  67.8 1.6 %fusion.19 = bf16[288,2880]{1,0:T(8,128)(2,1)S(1)} fusion(f32[288,2880]{1,0:T(8,128)S(1)} %fusion.6, bf16[288,720]{1,0:T(8,128)(2,1)S(1)} %get-tuple-element.69, bf16[1,2880,720]{1,2,0:T(8,128)(2,1)S(1)} %bitcast.95), kind=kOutput, calls=%fused_computation.20 | convolution fusion | flops 1196052480 | bytes 9538560 | tf_op jit(solution)/shard_map/dot_general | solution.py:22
  69.7 2.2 %collective-permute-done.7 = bf16[144,2880]{1,0:T(8,128)(2,1)S(1)} collective-permute-done((bf16[144,2880]{1,0:T(8,128)(2,1)S(1)}, bf16[144,2880]{1,0:T(8,128)(2,1)S(1)}, u32[]{:S(2)}, u32[]{:S(2)}) %collective-permute-start.7) | collective-permute-done | bytes 829472 | tf_op jit(solution)/shard_map/ppermute | solution.py:56
  72.5 0.6 collective-permute-start.16
  73.2 0.9 collective-permute-done.11
  74.1 1.8 %multiply_convert_fusion = (bf16[288,720]{1,0:T(8,128)(2,1)S(1)}, bf16[288,720]{1,0:T(8,128)(2,1)S(1)}, bf16[288,720]{1,0:T(8,128)(2,1)S(1)}) fusion(f32[288,720]{1,0:T(8,128)S(1)} %fusion.4, f32[288,720]{1,0:T(8,128)S(1)} %fusion.10, bf16[1,720,2880]{2,1,0:T(8,128)(2,1)S(1)} %bitcast.93, bf16[72,2880]{1,0:T(8,128)(2,1)S(1)} %collective-permute-done.11, ...), kind=kOutput, calls=%fused_computation.56 | convolution fusion | flops 1204554240 | bytes 8709120 | tf_op jit(solution)/shard_map/dot_general | solution.py:22
  76.0 0.8 fusion.27
  76.9 0.9 fusion.24
  78.1 0.8 fusion.32
  78.9 0.9 fusion.25
  79.9 0.4 collective-permute-start.15
  80.6 1.1 collective-permute-done.15
  81.8 1.6 %collective-permute-start.13 = (bf16[72,1536]{1,0:T(8,128)(2,1)S(1)}, bf16[72,1536]{1,0:T(8,128)(2,1)S(1)}, u32[]{:S(2)}, u32[]{:S(2)}) collective-permute-start(bf16[72,1536]{1,0:T(8,128)(2,1)S(1)} %get-tuple-element.83), channel_id=1, source_target_pairs={{0,2},{1,3},{2,0},{3,1},{4,6},{5,7},{6,4},{7,5},{8,10},{9,11},{10,... | collective-permute-start | bytes 663560 | tf_op jit(solution)/shard_map/ppermute | solution.py:56
  83.4 0.6 collective-permute-start.14
  84.0 1.5 %collective-permute-start.20 = (bf16[72,1344]{1,0:T(8,128)(2,1)S(1)}, bf16[72,1344]{1,0:T(8,128)(2,1)S(1)}, u32[]{:S(2)}, u32[]{:S(2)}) collective-permute-start(bf16[72,1344]{1,0:T(8,128)(2,1)S(1)} %get-tuple-element.89), channel_id=1, source_target_pairs={{0,2},{1,3},{2,0},{3,1},{4,6},{5,7},{6,4},{7,5},{8,10},{9,11},{10,... | collective-permute-start | bytes 580616 | tf_op jit(solution)/shard_map/ppermute | solution.py:56
  85.5 1.4 %collective-permute-start.21 = (bf16[72,1344]{1,0:T(8,128)(2,1)S(1)}, bf16[72,1344]{1,0:T(8,128)(2,1)S(1)}, u32[]{:S(2)}, u32[]{:S(2)}) collective-permute-start(bf16[72,1344]{1,0:T(8,128)(2,1)S(1)} %get-tuple-element.88), channel_id=1, source_target_pairs={{0,6},{1,7},{2,4},{3,5},{4,2},{5,3},{6,0},{7,1},{8,14},{9,15},{10,... | collective-permute-start | bytes 580616 | tf_op jit(solution)/shard_map/ppermute | solution.py:56
  86.9 5.2 %convolution_convert_fusion.2 = bf16[2880,720]{0,1:T(8,128)(2,1)} fusion(bf16[576,2880]{1,0:T(8,128)(2,1)S(1)} %constant_dynamic-update-slice_fusion.3, bf16[576,720]{1,0:T(8,128)(2,1)S(1)} %pad_maximum_fusion.2), kind=kOutput, calls=%fused_computation.2 | convolution fusion | flops 2390860800 | bytes 8294400 | tf_op jit(solution)/shard_map/dot_general | solution.py:16
  92.1 2.9 %collective-permute-done.14 = bf16[72,1536]{1,0:T(8,128)(2,1)S(1)} collective-permute-done((bf16[72,1536]{1,0:T(8,128)(2,1)S(1)}, bf16[72,1536]{1,0:T(8,128)(2,1)S(1)}, u32[]{:S(2)}, u32[]{:S(2)}) %collective-permute-start.14) | collective-permute-done | bytes 221216 | tf_op jit(solution)/shard_map/ppermute | solution.py:56
  95.7 2.1 %collective-permute-start.18 = (bf16[32,1536]{1,0:T(8,128)(2,1)S(1)}, bf16[32,1536]{1,0:T(8,128)(2,1)S(1)}, u32[]{:S(2)}, u32[]{:S(2)}) collective-permute-start(bf16[32,1536]{1,0:T(8,128)(2,1)S(1)} %get-tuple-element.77), channel_id=1, source_target_pairs={{0,16},{1,17},{2,18},{3,19},{4,20},{5,21},{6,22},{7,23},{8,24},{9,... | collective-permute-start | bytes 294920 | tf_op jit(solution)/shard_map/ppermute | solution.py:61
  97.8 1.8 %collective-permute-start.19 = (bf16[32,1536]{1,0:T(8,128)(2,1)S(1)}, bf16[32,1536]{1,0:T(8,128)(2,1)S(1)}, u32[]{:S(2)}, u32[]{:S(2)}) collective-permute-start(bf16[32,1536]{1,0:T(8,128)(2,1)S(1)} %get-tuple-element.76), channel_id=1, source_target_pairs={{0,24},{1,25},{2,26},{3,27},{4,28},{5,29},{6,30},{7,31},{8,0},{9,1... | collective-permute-start | bytes 294920 | tf_op jit(solution)/shard_map/ppermute | solution.py:61
  99.5 5.2 %convolution_convert_fusion.1 = bf16[2880,720]{0,1:T(8,128)(2,1)} fusion(bf16[576,2880]{1,0:T(8,128)(2,1)S(1)} %constant_dynamic-update-slice_fusion.3, bf16[576,720]{1,0:T(8,128)(2,1)S(1)} %pad_maximum_fusion.3), kind=kOutput, calls=%fused_computation.1 | convolution fusion | flops 2390860800 | bytes 8294400 | tf_op jit(solution)/shard_map/dot_general | solution.py:16
  104.8 0.8 collective-permute-done.18
  106.4 1.7 %collective-permute-start.22 = (bf16[32,1344]{1,0:T(8,128)(2,1)S(1)}, bf16[32,1344]{1,0:T(8,128)(2,1)S(1)}, u32[]{:S(2)}, u32[]{:S(2)}) collective-permute-start(bf16[32,1344]{1,0:T(8,128)(2,1)S(1)} %get-tuple-element.81), channel_id=1, source_target_pairs={{0,8},{1,9},{2,10},{3,11},{4,12},{5,13},{6,14},{7,15},{8,16},{9,17... | collective-permute-start | bytes 258056 | tf_op jit(solution)/shard_map/ppermute | solution.py:61
  108.1 1.6 %collective-permute-start.23 = (bf16[32,1344]{1,0:T(8,128)(2,1)S(1)}, bf16[32,1344]{1,0:T(8,128)(2,1)S(1)}, u32[]{:S(2)}, u32[]{:S(2)}) collective-permute-start(bf16[32,1344]{1,0:T(8,128)(2,1)S(1)} %get-tuple-element.80), channel_id=1, source_target_pairs={{0,16},{1,17},{2,18},{3,19},{4,20},{5,21},{6,22},{7,23},{8,24},{9,... | collective-permute-start | bytes 258056 | tf_op jit(solution)/shard_map/ppermute | solution.py:61
  109.7 0.9 collective-permute-start.24
  110.5 5.2 %convolution_convert_fusion = bf16[720,2880]{1,0:T(8,128)(2,1)} fusion(bf16[576,720]{1,0:T(8,128)(2,1)S(1)} %pad_maximum_fusion.4, bf16[576,2880]{1,0:T(8,128)(2,1)S(1)} %constant_dynamic-update-slice_fusion.9), kind=kOutput, calls=%fused_computation | convolution fusion | flops 2390860800 | bytes 8294400 | tf_op jit(solution)/shard_map/dot_general | solution.py:16
  115.7 0.4 collective-permute-done.23
  116.3 0.8 fusion.55
  (104 shorter events, 6.7 us)
Async XLA Ops:
  0.6 29.1 %copy-start.1 = (bf16[32,2880]{1,0:T(8,128)(2,1)S(1)}, bf16[32,2880]{1,0:T(8,128)(2,1)}, u32[]{:S(2)}) copy-start(bf16[32,2880]{1,0:T(8,128)(2,1)} %param.12) | copy-start | bytes 552964
  25.4 21.6 %collective-permute-start = (bf16[72,2880]{1,0:T(8,128)(2,1)S(1)}, bf16[72,2880]{1,0:T(8,128)(2,1)S(1)}, u32[]{:S(2)}, u32[]{:S(2)}) collective-permute-start(bf16[72,2880]{1,0:T(8,128)(2,1)S(1)} %convolution_convert_fusion.4), channel_id=1, source_target_pairs={{0,4},{1,5},{2,6},{3,7},{4,0},{5,1},{6,2},{7,3},{8,12},{9,13},{10,... | collective-permute-start | bytes 1244168 | tf_op jit(solution)/shard_map/ppermute | solution.py:56
  27.0 20.0 %collective-permute-start.2 = (bf16[72,2880]{1,0:T(8,128)(2,1)S(1)}, bf16[72,2880]{1,0:T(8,128)(2,1)S(1)}, u32[]{:S(2)}, u32[]{:S(2)}) collective-permute-start(bf16[72,2880]{1,0:T(8,128)(2,1)S(1)} %convolution_convert_fusion.4), channel_id=1, source_target_pairs={{0,6},{1,7},{2,4},{3,5},{4,2},{5,3},{6,0},{7,1},{8,14},{9,15},{10,... | collective-permute-start | bytes 1244168 | tf_op jit(solution)/shard_map/ppermute | solution.py:56
  28.8 18.2 %collective-permute-start.1 = (bf16[72,2880]{1,0:T(8,128)(2,1)S(1)}, bf16[72,2880]{1,0:T(8,128)(2,1)S(1)}, u32[]{:S(2)}, u32[]{:S(2)}) collective-permute-start(bf16[72,2880]{1,0:T(8,128)(2,1)S(1)} %convolution_convert_fusion.3), channel_id=1, source_target_pairs={{0,2},{1,3},{2,0},{3,1},{4,6},{5,7},{6,4},{7,5},{8,10},{9,11},{10,... | collective-permute-start | bytes 1244168 | tf_op jit(solution)/shard_map/ppermute | solution.py:56
  47.5 11.4 %collective-permute-start.3 = (bf16[72,2880]{1,0:T(8,128)(2,1)S(1)}, bf16[72,2880]{1,0:T(8,128)(2,1)S(1)}, u32[]{:S(2)}, u32[]{:S(2)}) collective-permute-start(bf16[72,2880]{1,0:T(8,128)(2,1)S(1)} %fusion.23), channel_id=1, source_target_pairs={{0,4},{1,5},{2,6},{3,7},{4,0},{5,1},{6,2},{7,3},{8,12},{9,13},{10,... | collective-permute-start | bytes 1244168 | tf_op jit(solution)/shard_map/ppermute | solution.py:56
  49.1 9.9 %collective-permute-start.4 = (bf16[72,2880]{1,0:T(8,128)(2,1)S(1)}, bf16[72,2880]{1,0:T(8,128)(2,1)S(1)}, u32[]{:S(2)}, u32[]{:S(2)}) collective-permute-start(bf16[72,2880]{1,0:T(8,128)(2,1)S(1)} %get-tuple-element.94), channel_id=1, source_target_pairs={{0,2},{1,3},{2,0},{3,1},{4,6},{5,7},{6,4},{7,5},{8,10},{9,11},{10,... | collective-permute-start | bytes 1244168 | tf_op jit(solution)/shard_map/ppermute | solution.py:56
  50.7 2.4 %collective-permute-start.5 = (bf16[144,2880]{1,0:T(8,128)(2,1)S(1)}, bf16[144,2880]{1,0:T(8,128)(2,1)S(1)}, u32[]{:S(2)}, u32[]{:S(2)}) collective-permute-start(bf16[144,2880]{1,0:T(8,128)(2,1)S(1)} %pad_maximum_fusion.5), channel_id=1, source_target_pairs={{0,1},{1,0},{2,3},{3,2},{4,5},{5,4},{6,7},{7,6},{8,9},{9,8},{10,11... | collective-permute-start | bytes 2488328 | tf_op jit(solution)/shard_map/ppermute | solution.py:56
  50.8 8.9 %collective-permute-start.9 = (bf16[144,2880]{1,0:T(8,128)(2,1)S(1)}, bf16[144,2880]{1,0:T(8,128)(2,1)S(1)}, u32[]{:S(2)}, u32[]{:S(2)}) collective-permute-start(bf16[144,2880]{1,0:T(8,128)(2,1)S(1)} %pad_maximum_fusion.7), channel_id=1, source_target_pairs={{0,1},{1,0},{2,3},{3,2},{4,5},{5,4},{6,7},{7,6},{8,9},{9,8},{10,11... | collective-permute-start | bytes 2488328 | tf_op jit(solution)/shard_map/ppermute | solution.py:56
  53.1 4.2 %slice-start = ((s8[4239360]{0:T(1024)(128)(4,1)}), s8[4194304]{0:T(1024)(128)(4,1)S(1)}, s32[]{:S(2)}) async-start(s8[4239360]{0:T(1024)(128)(4,1)} %bitcast.85), calls=%async_computation | async-start | bytes 8388608
  53.3 4.0 %slice-start.1 = ((s8[4239360]{0:T(1024)(128)(4,1)}), s8[45056]{0:T(1024)(128)(4,1)S(1)}, s32[]{:S(2)}) async-start(s8[4239360]{0:T(1024)(128)(4,1)} %bitcast.85), calls=%async_computation.1 | async-start | bytes 90112
  53.4 6.5 %slice-start.4 = ((s8[4239360]{0:T(1024)(128)(4,1)}), s8[4194304]{0:T(1024)(128)(4,1)S(1)}, s32[]{:S(2)}) async-start(s8[4239360]{0:T(1024)(128)(4,1)} %bitcast.94), calls=%async_computation.4 | async-start | bytes 8388608
  57.3 2.6 %slice-start.5 = ((s8[4239360]{0:T(1024)(128)(4,1)}), s8[45056]{0:T(1024)(128)(4,1)S(1)}, s32[]{:S(2)}) async-start(s8[4239360]{0:T(1024)(128)(4,1)} %bitcast.94), calls=%async_computation.5 | async-start | bytes 90112
  59.0 13.2 %collective-permute-start.8 = (bf16[72,2880]{1,0:T(8,128)(2,1)S(1)}, bf16[72,2880]{1,0:T(8,128)(2,1)S(1)}, u32[]{:S(2)}, u32[]{:S(2)}) collective-permute-start(bf16[72,2880]{1,0:T(8,128)(2,1)S(1)} %collective-permute-done.3), channel_id=1, source_target_pairs={{0,2},{1,3},{2,0},{3,1},{4,6},{5,7},{6,4},{7,5},{8,10},{9,11},{10,... | collective-permute-start | bytes 1244168 | tf_op jit(solution)/shard_map/ppermute | solution.py:56
  59.7 4.3 %collective-permute-start.6 = (bf16[144,2880]{1,0:T(8,128)(2,1)S(1)}, bf16[144,2880]{1,0:T(8,128)(2,1)S(1)}, u32[]{:S(2)}, u32[]{:S(2)}) collective-permute-start(bf16[144,2880]{1,0:T(8,128)(2,1)S(1)} %pad_maximum_fusion.6), channel_id=1, source_target_pairs={{0,1},{1,0},{2,3},{3,2},{4,5},{5,4},{6,7},{7,6},{8,9},{9,8},{10,11... | collective-permute-start | bytes 2488328 | tf_op jit(solution)/shard_map/ppermute | solution.py:56
  61.5 11.6 %collective-permute-start.10 = (bf16[72,2880]{1,0:T(8,128)(2,1)S(1)}, bf16[72,2880]{1,0:T(8,128)(2,1)S(1)}, u32[]{:S(2)}, u32[]{:S(2)}) collective-permute-start(bf16[72,2880]{1,0:T(8,128)(2,1)S(1)} %collective-permute-done.4), channel_id=1, source_target_pairs={{0,1},{1,0},{2,3},{3,2},{4,5},{5,4},{6,7},{7,6},{8,9},{9,8},{10,11... | collective-permute-start | bytes 1244168 | tf_op jit(solution)/shard_map/ppermute | solution.py:56
  62.2 2.2 %slice-start.2 = ((s8[4239360]{0:T(1024)(128)(4,1)}), s8[4194304]{0:T(1024)(128)(4,1)S(1)}, s32[]{:S(2)}) async-start(s8[4239360]{0:T(1024)(128)(4,1)} %bitcast.92), calls=%async_computation.2 | async-start | bytes 8388608
  62.3 2.1 %slice-start.3 = ((s8[4239360]{0:T(1024)(128)(4,1)}), s8[45056]{0:T(1024)(128)(4,1)S(1)}, s32[]{:S(2)}) async-start(s8[4239360]{0:T(1024)(128)(4,1)} %bitcast.92), calls=%async_computation.3 | async-start | bytes 90112
  69.4 2.4 %collective-permute-start.7 = (bf16[144,2880]{1,0:T(8,128)(2,1)S(1)}, bf16[144,2880]{1,0:T(8,128)(2,1)S(1)}, u32[]{:S(2)}, u32[]{:S(2)}) collective-permute-start(bf16[144,2880]{1,0:T(8,128)(2,1)S(1)} %slice.120), channel_id=1, source_target_pairs={{0,1},{1,0},{2,3},{3,2},{4,5},{5,4},{6,7},{7,6},{8,9},{9,8},{10,11... | collective-permute-start | bytes 2488328 | tf_op jit(solution)/shard_map/ppermute | solution.py:56
  72.2 1.8 %collective-permute-start.11 = (bf16[72,2880]{1,0:T(8,128)(2,1)S(1)}, bf16[72,2880]{1,0:T(8,128)(2,1)S(1)}, u32[]{:S(2)}, u32[]{:S(2)}) collective-permute-start(bf16[72,2880]{1,0:T(8,128)(2,1)S(1)} %collective-permute-done.8), channel_id=1, source_target_pairs={{0,1},{1,0},{2,3},{3,2},{4,5},{5,4},{6,7},{7,6},{8,9},{9,8},{10,11... | collective-permute-start | bytes 1244168 | tf_op jit(solution)/shard_map/ppermute | solution.py:56
  72.5 22.8 %collective-permute-start.16 = (bf16[72,2880]{1,0:T(8,128)(2,1)S(1)}, bf16[72,2880]{1,0:T(8,128)(2,1)S(1)}, u32[]{:S(2)}, u32[]{:S(2)}) collective-permute-start(bf16[72,2880]{1,0:T(8,128)(2,1)S(1)} %slice.193), channel_id=1, source_target_pairs={{0,4},{1,5},{2,6},{3,7},{4,0},{5,1},{6,2},{7,3},{8,12},{9,13},{10,... | collective-permute-start | bytes 1244168 | tf_op jit(solution)/shard_map/ppermute | solution.py:56
  77.9 2.5 %collective-permute-start.12 = (bf16[144,1536]{1,0:T(8,128)(2,1)S(1)}, bf16[144,1536]{1,0:T(8,128)(2,1)S(1)}, u32[]{:S(2)}, u32[]{:S(2)}) collective-permute-start(bf16[144,1536]{1,0:T(8,128)(2,1)S(1)} %slice.123), channel_id=1, source_target_pairs={{0,1},{1,0},{2,3},{3,2},{4,5},{5,4},{6,7},{7,6},{8,9},{9,8},{10,11... | collective-permute-start | bytes 1327112 | tf_op jit(solution)/shard_map/ppermute | solution.py:56
  79.9 1.8 %collective-permute-start.15 = (bf16[144,1344]{1,0:T(8,128)(2,1)S(1)}, bf16[144,1344]{1,0:T(8,128)(2,1)S(1)}, u32[]{:S(2)}, u32[]{:S(2)}) collective-permute-start(bf16[144,1344]{1,0:T(8,128)(2,1)S(1)} %slice.126), channel_id=1, source_target_pairs={{0,1},{1,0},{2,3},{3,2},{4,5},{5,4},{6,7},{7,6},{8,9},{9,8},{10,11... | collective-permute-start | bytes 1161224 | tf_op jit(solution)/shard_map/ppermute | solution.py:56
  81.8 10.2 %collective-permute-start.13 = (bf16[72,1536]{1,0:T(8,128)(2,1)S(1)}, bf16[72,1536]{1,0:T(8,128)(2,1)S(1)}, u32[]{:S(2)}, u32[]{:S(2)}) collective-permute-start(bf16[72,1536]{1,0:T(8,128)(2,1)S(1)} %get-tuple-element.83), channel_id=1, source_target_pairs={{0,2},{1,3},{2,0},{3,1},{4,6},{5,7},{6,4},{7,5},{8,10},{9,11},{10,... | collective-permute-start | bytes 663560 | tf_op jit(solution)/shard_map/ppermute | solution.py:56
  83.4 11.6 %collective-permute-start.14 = (bf16[72,1536]{1,0:T(8,128)(2,1)S(1)}, bf16[72,1536]{1,0:T(8,128)(2,1)S(1)}, u32[]{:S(2)}, u32[]{:S(2)}) collective-permute-start(bf16[72,1536]{1,0:T(8,128)(2,1)S(1)} %get-tuple-element.82), channel_id=1, source_target_pairs={{0,6},{1,7},{2,4},{3,5},{4,2},{5,3},{6,0},{7,1},{8,14},{9,15},{10,... | collective-permute-start | bytes 663560 | tf_op jit(solution)/shard_map/ppermute | solution.py:56
  84.0 21.6 %collective-permute-start.20 = (bf16[72,1344]{1,0:T(8,128)(2,1)S(1)}, bf16[72,1344]{1,0:T(8,128)(2,1)S(1)}, u32[]{:S(2)}, u32[]{:S(2)}) collective-permute-start(bf16[72,1344]{1,0:T(8,128)(2,1)S(1)} %get-tuple-element.89), channel_id=1, source_target_pairs={{0,2},{1,3},{2,0},{3,1},{4,6},{5,7},{6,4},{7,5},{8,10},{9,11},{10,... | collective-permute-start | bytes 580616 | tf_op jit(solution)/shard_map/ppermute | solution.py:56
  85.5 20.2 %collective-permute-start.21 = (bf16[72,1344]{1,0:T(8,128)(2,1)S(1)}, bf16[72,1344]{1,0:T(8,128)(2,1)S(1)}, u32[]{:S(2)}, u32[]{:S(2)}) collective-permute-start(bf16[72,1344]{1,0:T(8,128)(2,1)S(1)} %get-tuple-element.88), channel_id=1, source_target_pairs={{0,6},{1,7},{2,4},{3,5},{4,2},{5,3},{6,0},{7,1},{8,14},{9,15},{10,... | collective-permute-start | bytes 580616 | tf_op jit(solution)/shard_map/ppermute | solution.py:56
  95.7 9.1 %collective-permute-start.17 = (bf16[32,1536]{1,0:T(8,128)(2,1)S(1)}, bf16[32,1536]{1,0:T(8,128)(2,1)S(1)}, u32[]{:S(2)}, u32[]{:S(2)}) collective-permute-start(bf16[32,1536]{1,0:T(8,128)(2,1)S(1)} %get-tuple-element.78), channel_id=1, source_target_pairs={{0,8},{1,9},{2,10},{3,11},{4,12},{5,13},{6,14},{7,15},{8,16},{9,17... | collective-permute-start | bytes 294920 | tf_op jit(solution)/shard_map/ppermute | solution.py:61
  95.7 9.9 %collective-permute-start.18 = (bf16[32,1536]{1,0:T(8,128)(2,1)S(1)}, bf16[32,1536]{1,0:T(8,128)(2,1)S(1)}, u32[]{:S(2)}, u32[]{:S(2)}) collective-permute-start(bf16[32,1536]{1,0:T(8,128)(2,1)S(1)} %get-tuple-element.77), channel_id=1, source_target_pairs={{0,16},{1,17},{2,18},{3,19},{4,20},{5,21},{6,22},{7,23},{8,24},{9,... | collective-permute-start | bytes 294920 | tf_op jit(solution)/shard_map/ppermute | solution.py:61
  97.8 7.8 %collective-permute-start.19 = (bf16[32,1536]{1,0:T(8,128)(2,1)S(1)}, bf16[32,1536]{1,0:T(8,128)(2,1)S(1)}, u32[]{:S(2)}, u32[]{:S(2)}) collective-permute-start(bf16[32,1536]{1,0:T(8,128)(2,1)S(1)} %get-tuple-element.76), channel_id=1, source_target_pairs={{0,24},{1,25},{2,26},{3,27},{4,28},{5,29},{6,30},{7,31},{8,0},{9,1... | collective-permute-start | bytes 294920 | tf_op jit(solution)/shard_map/ppermute | solution.py:61
  106.4 9.4 %collective-permute-start.22 = (bf16[32,1344]{1,0:T(8,128)(2,1)S(1)}, bf16[32,1344]{1,0:T(8,128)(2,1)S(1)}, u32[]{:S(2)}, u32[]{:S(2)}) collective-permute-start(bf16[32,1344]{1,0:T(8,128)(2,1)S(1)} %get-tuple-element.81), channel_id=1, source_target_pairs={{0,8},{1,9},{2,10},{3,11},{4,12},{5,13},{6,14},{7,15},{8,16},{9,17... | collective-permute-start | bytes 258056 | tf_op jit(solution)/shard_map/ppermute | solution.py:61
  108.1 8.0 %collective-permute-start.23 = (bf16[32,1344]{1,0:T(8,128)(2,1)S(1)}, bf16[32,1344]{1,0:T(8,128)(2,1)S(1)}, u32[]{:S(2)}, u32[]{:S(2)}) collective-permute-start(bf16[32,1344]{1,0:T(8,128)(2,1)S(1)} %get-tuple-element.80), channel_id=1, source_target_pairs={{0,16},{1,17},{2,18},{3,19},{4,20},{5,21},{6,22},{7,23},{8,24},{9,... | collective-permute-start | bytes 258056 | tf_op jit(solution)/shard_map/ppermute | solution.py:61
  109.7 6.5 %copy-start = (bf16[32,2880]{1,0:T(8,128)(2,1)S(1)}, bf16[32,2880]{1,0:T(8,128)(2,1)}, u32[]{:S(2)}) copy-start(bf16[32,2880]{1,0:T(8,128)(2,1)} %param.8) | copy-start | bytes 552964
  109.7 6.5 %copy-start.2 = (f32[2880]{0:T(1024)S(1)}, f32[2880]{0:T(1024)}, u32[]{:S(2)}) copy-start(f32[2880]{0:T(1024)} %param.9) | copy-start | bytes 34564
  109.7 6.4 %collective-permute-start.24 = (bf16[32,1344]{1,0:T(8,128)(2,1)S(1)}, bf16[32,1344]{1,0:T(8,128)(2,1)S(1)}, u32[]{:S(2)}, u32[]{:S(2)}) collective-permute-start(bf16[32,1344]{1,0:T(8,128)(2,1)S(1)} %get-tuple-element.79), channel_id=1, source_target_pairs={{0,24},{1,25},{2,26},{3,27},{4,28},{5,29},{6,30},{7,31},{8,0},{9,1... | collective-permute-start | bytes 258056 | tf_op jit(solution)/shard_map/ppermute | solution.py:61

commit v2 on v1

--- a/solution.py
+++ b/solution.py
@@ -1,12 +1,15 @@
 import jax
 import jax.numpy as jnp
 from jax import lax
+from jax.experimental import pallas as pl
 from jax.experimental.layout import Layout, with_layout_constraint
+from jax.experimental.pallas import tpu as pltpu
 from jax.sharding import PartitionSpec as P
 
 QUARTERS = 4
 CORE, PAIR, SIDE = 1, 2, 4
 TILE = 8
+PRODUCT_COLUMNS = 768
 
 norm_eps = 1e-05
 glu_alpha = 1.702
@@ -30,6 +33,67 @@
 
 def behind(values, first):
     return lax.optimization_barrier((values, first))[0]
+
+
+def fast_copy_kernel(weight_ref, out_ref, done):
+    copy = pltpu.make_async_copy(weight_ref, out_ref, done)
+    copy.start()
+    copy.wait()
+
+
+def fast_copy(weight):
+    return pl.pallas_call(
+        fast_copy_kernel,
+        in_specs=[pl.BlockSpec(memory_space=pl.ANY)],
+        out_specs=pl.BlockSpec(memory_space=pltpu.VMEM),
+        out_shape=jax.ShapeDtypeStruct(weight.shape, weight.dtype),
+        scratch_shapes=[pltpu.SemaphoreType.DMA],
+        cost_estimate=pl.CostEstimate(
+            flops=0, bytes_accessed=4 * weight.size, transcendentals=0
+        ),
+        compiler_params=pltpu.CompilerParams(vmem_limit_bytes=8 * 1024 * 1024),
+    )(weight)
+
+
+def product_kernel(left_ref, right_ref, out_ref, turned_ref, result_ref, sent):
+    turned_ref[...] = left_ref[...].T
+    width = right_ref.shape[1]
+    copies = []
+    for number, first in enumerate(range(0, width, PRODUCT_COLUMNS)):
+        columns = slice(first, min(first + PRODUCT_COLUMNS, width))
+        result_ref[:, columns] = jnp.dot(
+            turned_ref[...], right_ref[:, columns], preferred_element_type=jnp.float32
+        ).astype(result_ref.dtype)
+        copies.append(
+            pltpu.make_async_copy(
+                result_ref.at[:, columns], out_ref.at[:, columns], sent.at[number]
+            )
+        )
+        copies[-1].start()
+    for copy in copies:
+        copy.wait()
+
+
+def weight_product(left, right):
+    rows, hidden = left.shape
+    width = right.shape[1]
+    return pl.pallas_call(
+        product_kernel,
+        in_specs=[pl.BlockSpec(memory_space=pltpu.VMEM)] * 2,
+        out_specs=pl.BlockSpec(memory_space=pl.ANY),
+        out_shape=jax.ShapeDtypeStruct((hidden, width), jnp.bfloat16),
+        scratch_shapes=[
+            pltpu.VMEM((hidden, rows), jnp.bfloat16),
+            pltpu.VMEM((hidden, width), jnp.bfloat16),
+            pltpu.SemaphoreType.DMA((-(-width // PRODUCT_COLUMNS),)),
+        ],
+        cost_estimate=pl.CostEstimate(
+            flops=2 * rows * hidden * width,
+            bytes_accessed=2 * (rows * hidden + rows * width + hidden * width),
+            transcendentals=0,
+        ),
+        compiler_params=pltpu.CompilerParams(vmem_limit_bytes=24 * 1024 * 1024),
+    )(left, right)
 
 
 def three_parts(value):
@@ -123,9 +187,9 @@
         rows = jnp.concatenate([first, second], axis=0)
         return jnp.concatenate([rows, flip(rows, CORE)], axis=0)
 
-    gate_w = w_gate[0]
+    gate_w = fast_copy(behind(w_gate[0], (own_dy, far_dy)).T).T
     up_w = w_up[0]
-    down_w = w_down[0]
+    down_w = fast_copy(behind(w_down[0], gate_w))
 
     def forward(x_in):
         gate = jnp.dot(x_in, gate_w, preferred_element_type=jnp.float32)
@@ -164,7 +228,7 @@
     side_sum = flip(chip_sum[slots:].astype(jnp.bfloat16), SIDE)
 
     pair_core_dy = flip(pair_dy, CORE)
-    across_dy = behind(across_dy, (chip_sum, pair_forward))
+    across_dy = behind(across_dy, (chip_rows, pair_forward))
     pair_dy = jnp.concatenate([pair_dy, across_dy, pair_core_dy, flip(across_dy, CORE)], axis=0)
     pair_hid, pair_d_gate, pair_d_up = hidden(*pair_forward, pair_dy)
 
@@ -178,7 +242,7 @@
     def to_pair(rows):
         return flip(rows[:slots], PAIR), flip(rows[slots:], PAIR | SIDE)
 
-    rows_first = row_gradient(pair_d_gate, pair_d_up, *spans[0])
+    rows_first = row_gradient(*behind((pair_d_gate, pair_d_up), chip_sum), *spans[0])
     core_first = flip(rows_first[kept:], CORE)
     rows_second = row_gradient(*behind((pair_d_gate, pair_d_up), rows_first), *spans[1])
     core_second = flip(rows_second[kept:], CORE)
@@ -214,20 +278,20 @@
             total = total + block.astype(jnp.float32)
         return total
 
-    def weight_gradient(left, right, first):
-        return contract_rows(*behind((left, right), first)).astype(jnp.bfloat16)
-
-    sum_second = core_sum(*behind((rows_second, core_second), sum_first))
+    def weight_gradient(hidden_rows, model_rows, first):
+        return weight_product(*behind((hidden_rows, model_rows), first))
+
+    grad_gate = weight_gradient(d_gate, x_in, (sum_first, rows_second, chip_sum))
+    sum_second = core_sum(*behind((rows_second, core_second), grad_gate))
     sent_second = to_pair(sum_second)
-    grad_gate = weight_gradient(x_in, d_gate, (sum_second, chip_sum))
     d_column = to_column(spans[0], *behind(sent_first, grad_gate))
     first_half = to_tokens(d_column)
-    grad_up = weight_gradient(x_in, d_up, d_column)
+    grad_up = weight_gradient(d_up, x_in, d_column)
     first_half = added(*behind(first_half, grad_up))
     second_half = to_tokens(to_column(spans[1], *behind(sent_second, first_half)))
     grad_down = weight_gradient(hid, dy_e, first_half)
     second_half = added(*behind(second_half, grad_down))
-    grads = [grad[None] for grad in (grad_gate, grad_up, grad_down)]
+    grads = [grad_gate.T[None], grad_up.T[None], grad_down[None]]
     d_normed = jnp.concatenate([first_half, second_half], axis=1)
 
     scaled = d_normed * norm_gain

time: 117 us -> 117 us (level)
  matrix products: 37 us -> 19.7 us
  Pallas kernels: 0 us -> 14.9 us
    dot_general x7 -> x4, matrix products: 16.8 us -> 1.26 us  [contract_rows(): lax.dot_general(left, right, (((0,), (0,)), ((), ())), preferred_element_...]
    pallas_call x0 -> x5, Pallas kernels: none -> 14.9 us  [the longest x3 14 us: weight_product(): pl.pallas_call(product_kernel, in_specs=[pl.BlockSpec(memory_space=pltpu....]
    dot_general x2, matrix products: 5.54 us -> 3.29 us  [forward(): gate = jnp.dot(x_in, gate_w, preferred_element_type=jnp.float32)]
    ppermute x6, waiting for transfers between devices: 1.21 us -> 2.76 us  [shift(): return lax.ppermute(row_major(value), 'sq', pairs)]
    ppermute x19, waiting for transfers between devices: 8.64 us -> 7.31 us  [flip(): lax.ppermute(row_major(value), 'sq', [(i, i ^ bit) for i in range(devices)])]
  transfers between devices with their start and end apart: 25 -> 25, of which waited for: 7 -> 6; matrix products, arithmetic and copies ran while one was open for 33% -> 16% of each run, Pallas kernels for 0% -> 13%
where the time goes in v2:
time: 117 us
  blocking collectives  38.3 us (33%)
  starting transfers between devices  23.7 us (20%)
  matrix products  19.7 us (17%)
  Pallas kernels  14.9 us (13%)
  waiting for transfers between devices  10.1 us (9%)
  other arithmetic  5.56 us (5%)
  local copies, waits for them, and re-layouts  2.98 us (3%)
  between operations  1.37 us (1%)
    all_gather x2, blocking collectives, gather_column(): lax.all_gather(block, 'sq', axis=0, tiled=True, axis_index_groups=lines)  38.3 us
    ppermute x19, starting transfers between devices, flip(): lax.ppermute(row_major(value), 'sq', [(i, i ^ bit) for i in range(devices)])  15.7 us
    pallas_call x3, Pallas kernels, weight_product(): pl.pallas_call(product_kernel, in_specs=[pl.BlockSpec(memory_space=pltpu....  14 us
    dot_general x8, matrix products, contract_cols(): lax.dot_general(left, right, (((1,), (1,)), ((), ())), preferred_element_...  10.7 us
    ppermute x6, starting transfers between devices, shift(): return lax.ppermute(row_major(value), 'sq', pairs)  8.06 us
    ppermute x19, waiting for transfers between devices, flip(): lax.ppermute(row_major(value), 'sq', [(i, i ^ bit) for i in range(devices)])  7.31 us
    dot_general x2, matrix products, forward(): up = jnp.dot(x_in, up_w, preferred_element_type=jnp.float32)  3.3 us
    dot_general x2, matrix products, forward(): gate = jnp.dot(x_in, gate_w, preferred_element_type=jnp.float32)  3.29 us
  transfers between devices with their start and end apart: 25, of which 6 were waited for; matrix products, arithmetic and copies ran while one was open for 16% of the time, Pallas kernels for 13%

profile of v2, /device:TPU:0, one launch (start us, length us, event | category | flops | bytes accessed | tf_op | source)
XLA Modules:
  0.0 116.6 jit_solution(1212858062868206895)
XLA Ops:
  0.6 0.7 select_reduce_fusion.4
  1.6 1.1 fusion.45
  2.7 1.0 fusion.40
  3.8 20.9 %all_gather.6 = bf16[128,2904]{1,0:T(8,128)(2,1)S(1)} all-gather(bf16[32,2904]{1,0:T(8,128)(2,1)S(1)} %concatenate.47), channel_id=1, replica_groups={{0,8,16,24},{1,9,17,25},{2,10,18,26},{3,11,19,27},{4,12,20,28},{5,13,21..., dimensions={0}, use_global_device_ids=true | all-gather | bytes 929280 | tf_op jit(solution)/shard_map/all_gather | solution.py:141
  25.4 1.6 %collective-permute-start = (bf16[72,2880]{1,0:T(8,128)(2,1)S(1)}, bf16[72,2880]{1,0:T(8,128)(2,1)S(1)}, u32[]{:S(2)}, u32[]{:S(2)}) collective-permute-start(bf16[72,2880]{1,0:T(8,128)(2,1)S(1)} %convolution_convert_fusion.1), channel_id=1, source_target_pairs={{0,4},{1,5},{2,6},{3,7},{4,0},{5,1},{6,2},{7,3},{8,12},{9,13},{10,... | collective-permute-start | bytes 1244168 | tf_op jit(solution)/shard_map/ppermute | solution.py:120
  26.9 1.4 %collective-permute-start.2 = (bf16[72,2880]{1,0:T(8,128)(2,1)S(1)}, bf16[72,2880]{1,0:T(8,128)(2,1)S(1)}, u32[]{:S(2)}, u32[]{:S(2)}) collective-permute-start(bf16[72,2880]{1,0:T(8,128)(2,1)S(1)} %convolution_convert_fusion.1), channel_id=1, source_target_pairs={{0,6},{1,7},{2,4},{3,5},{4,2},{5,3},{6,0},{7,1},{8,14},{9,15},{10,... | collective-permute-start | bytes 1244168 | tf_op jit(solution)/shard_map/ppermute | solution.py:120
  28.8 0.6 collective-permute-start.1
  29.7 17.4 %all_gather.7 = bf16[128,2880]{1,0:T(8,128)(2,1)S(1)} all-gather(bf16[32,2880]{1,0:T(8,128)(2,1)S(1)} %copy-done.2), channel_id=1, replica_groups={{0,8,16,24},{1,9,17,25},{2,10,18,26},{3,11,19,27},{4,12,20,28},{5,13,21..., dimensions={0}, use_global_device_ids=true | all-gather | bytes 921600 | tf_op jit(solution)/shard_map/all_gather | solution.py:141
  47.7 1.6 %collective-permute-start.3 = (bf16[72,2880]{1,0:T(8,128)(2,1)S(1)}, bf16[72,2880]{1,0:T(8,128)(2,1)S(1)}, u32[]{:S(2)}, u32[]{:S(2)}) collective-permute-start(bf16[72,2880]{1,0:T(8,128)(2,1)S(1)} %fusion.13), channel_id=1, source_target_pairs={{0,4},{1,5},{2,6},{3,7},{4,0},{5,1},{6,2},{7,3},{8,12},{9,13},{10,... | collective-permute-start | bytes 1244168 | tf_op jit(solution)/shard_map/ppermute | solution.py:120
  49.3 1.5 %collective-permute-start.4 = (bf16[72,2880]{1,0:T(8,128)(2,1)S(1)}, bf16[72,2880]{1,0:T(8,128)(2,1)S(1)}, u32[]{:S(2)}, u32[]{:S(2)}) collective-permute-start(bf16[72,2880]{1,0:T(8,128)(2,1)S(1)} %get-tuple-element.102), channel_id=1, source_target_pairs={{0,2},{1,3},{2,0},{3,1},{4,6},{5,7},{6,4},{7,5},{8,10},{9,11},{10,... | collective-permute-start | bytes 1244168 | tf_op jit(solution)/shard_map/ppermute | solution.py:120
  51.4 0.5 collective-permute-start.9
  51.9 1.2 %slice-done = s8[4194304]{0:T(1024)(128)(4,1)S(1)} async-done(((s8[4239360]{0:T(1024)(128)(4,1)}), s8[4194304]{0:T(1024)(128)(4,1)S(1)}, s32[]{:S(2)}) %slice-start) | async-done | bytes 4194328
  53.1 0.5 shard_map.112
  54.1 1.6 %fusion.93 = f32[288,720]{1,0:T(8,128)S(1)} fusion(bf16[288,2880]{1,0:T(8,128)(2,1)S(1)} %get-tuple-element.83, bf16[720,2880]{1,0:T(8,128)(2,1)S(1)} %shard_map.111), kind=kOutput, calls=%fused_computation.163 | convolution fusion | flops 1194393600 | bytes 6635520 | tf_op jit(solution)/shard_map/dot_general | solution.py:195
  56.0 1.6 %fusion.4 = f32[288,720]{1,0:T(8,128)S(1)} fusion(bf16[288,2880]{1,0:T(8,128)(2,1)S(1)} %get-tuple-element.83, bf16[1,2880,720]{1,2,0:T(8,128)(2,1)S(1)} %bitcast.81), kind=kOutput, calls=%fused_computation.4 | convolution fusion | flops 1194393600 | bytes 6635520 | tf_op jit(solution)/shard_map/dot_general | solution.py:196
  57.7 1.2 %collective-permute-start.8 = (bf16[72,2880]{1,0:T(8,128)(2,1)S(1)}, bf16[72,2880]{1,0:T(8,128)(2,1)S(1)}, u32[]{:S(2)}, u32[]{:S(2)}) collective-permute-start(bf16[72,2880]{1,0:T(8,128)(2,1)S(1)} %collective-permute-done.3), channel_id=1, source_target_pairs={{0,2},{1,3},{2,0},{3,1},{4,6},{5,7},{6,4},{7,5},{8,10},{9,11},{10,... | collective-permute-start | bytes 1244168 | tf_op jit(solution)/shard_map/ppermute | solution.py:120
  59.2 1.6 %fusion.95 = f32[288,720]{1,0:T(8,128)S(1)} fusion(bf16[288,2880]{1,0:T(8,128)(2,1)S(1)} %pad_maximum_fusion.1, bf16[720,2880]{1,0:T(8,128)(2,1)S(1)} %shard_map.111), kind=kOutput, calls=%fused_computation.165 | convolution fusion | flops 1194393600 | bytes 6635520 | tf_op jit(solution)/shard_map/dot_general | solution.py:195
  60.8 0.6 collective-permute-start.10
  61.6 1.7 %fusion = f32[288,720]{1,0:T(8,128)S(1)} fusion(bf16[288,2880]{1,0:T(8,128)(2,1)S(1)} %pad_maximum_fusion.1, bf16[1,2880,720]{1,2,0:T(8,128)(2,1)S(1)} %bitcast.81), kind=kOutput, calls=%fused_computation | convolution fusion | flops 1194393600 | bytes 6635520 | tf_op jit(solution)/shard_map/dot_general | solution.py:196
  63.3 1.9 %multiply_convert_fusion.1 = (bf16[288,720]{1,0:T(8,128)(2,1)S(1)}, bf16[288,720]{1,0:T(8,128)(2,1)S(1)}, bf16[288,720]{1,0:T(8,128)(2,1)S(1)}) fusion(f32[288,720]{1,0:T(8,128)S(1)} %fusion.4, f32[288,720]{1,0:T(8,128)S(1)} %fusion.93, bf16[720,2880]{1,0:T(8,128)(2,1)S(1)} %shard_map.112, bf16[144,2880]{1,0:T(8,128)(2,1)S(1)} %collective-permute-done.6, ...), kind=kOutput, calls=%fused_computation.43 | convolution fusion | flops 1202895360 | bytes 8709120 | tf_op jit(solution)/shard_map/dot_general | solution.py:25
  65.2 1.6 %fusion.94 = f32[288,2880]{1,0:T(8,128)S(1)} fusion(bf16[288,720]{1,0:T(8,128)(2,1)S(1)} %get-tuple-element.77, bf16[720,2880]{1,0:T(8,128)(2,1)S(1)} %shard_map.111), kind=kOutput, calls=%fused_computation.164 | convolution fusion | flops 1194393600 | bytes 7879680 | tf_op jit(solution)/shard_map/dot_general | solution.py:25
  66.7 1.6 %fusion.9 = bf16[288,2880]{1,0:T(8,128)(2,1)S(1)} fusion(f32[288,2880]{1,0:T(8,128)S(1)} %fusion.94, bf16[288,720]{1,0:T(8,128)(2,1)S(1)} %get-tuple-element.78, bf16[1,2880,720]{1,2,0:T(8,128)(2,1)S(1)} %bitcast.81), kind=kOutput, calls=%fused_computation.7 | convolution fusion | flops 1196052480 | bytes 9538560 | tf_op jit(solution)/shard_map/dot_general | solution.py:25
  68.5 1.4 %collective-permute-done.8 = bf16[72,2880]{1,0:T(8,128)(2,1)S(1)} collective-permute-done((bf16[72,2880]{1,0:T(8,128)(2,1)S(1)}, bf16[72,2880]{1,0:T(8,128)(2,1)S(1)}, u32[]{:S(2)}, u32[]{:S(2)}) %collective-permute-start.8) | collective-permute-done | bytes 414752 | tf_op jit(solution)/shard_map/ppermute | solution.py:120
  70.0 0.6 collective-permute-start.7
  70.7 1.0 collective-permute-done.11
  71.7 2.1 %multiply_convert_fusion = (bf16[288,720]{1,0:T(8,128)(2,1)S(1)}, bf16[288,720]{1,0:T(8,128)(2,1)S(1)}, bf16[288,720]{1,0:T(8,128)(2,1)S(1)}) fusion(f32[288,720]{1,0:T(8,128)S(1)} %fusion, f32[288,720]{1,0:T(8,128)S(1)} %fusion.95, bf16[720,2880]{1,0:T(8,128)(2,1)S(1)} %shard_map.112, bf16[72,2880]{1,0:T(8,128)(2,1)S(1)} %collective-permute-done.11, ...), kind=kOutput, calls=%fused_computation.42 | convolution fusion | flops 1204554240 | bytes 8709120 | tf_op jit(solution)/shard_map/dot_general | solution.py:25
  74.3 0.9 fusion.16
  75.2 0.9 fusion.14
  76.3 0.8 fusion.20
  77.3 0.6 collective-permute-start.15
  77.9 0.9 fusion.15
  79.1 0.6 collective-permute-start.13
  79.7 2.5 %collective-permute-start.14 = (bf16[72,1536]{1,0:T(8,128)(2,1)S(1)}, bf16[72,1536]{1,0:T(8,128)(2,1)S(1)}, u32[]{:S(2)}, u32[]{:S(2)}) collective-permute-start(bf16[72,1536]{1,0:T(8,128)(2,1)S(1)} %get-tuple-element.90), channel_id=1, source_target_pairs={{0,6},{1,7},{2,4},{3,5},{4,2},{5,3},{6,0},{7,1},{8,14},{9,15},{10,... | collective-permute-start | bytes 663560 | tf_op jit(solution)/shard_map/ppermute | solution.py:120
  82.1 4.7 %shard_map.113 = bf16[720,2880]{1,0:T(8,128)(2,1)} custom-call(bf16[576,720]{1,0:T(8,128)(2,1)S(1)} %pad_maximum_fusion.2.left_ref, bf16[576,2880]{1,0:T(8,128)(2,1)S(1)} %constant_dynamic-update-slice_fusion.3.right_ref), custom_call_target="tpu_custom_call" | custom-call | flops 2388787200 | bytes 8294400 | tf_op jit(solution)/shard_map/pallas_call | solution.py:80
  87.0 0.6 collective-permute-start.20
  87.5 1.4 %collective-permute-start.21 = (bf16[72,1344]{1,0:T(8,128)(2,1)S(1)}, bf16[72,1344]{1,0:T(8,128)(2,1)S(1)}, u32[]{:S(2)}, u32[]{:S(2)}) collective-permute-start(bf16[72,1344]{1,0:T(8,128)(2,1)S(1)} %get-tuple-element.96), channel_id=1, source_target_pairs={{0,6},{1,7},{2,4},{3,5},{4,2},{5,3},{6,0},{7,1},{8,14},{9,15},{10,... | collective-permute-start | bytes 580616 | tf_op jit(solution)/shard_map/ppermute | solution.py:120
  89.0 4.1 %collective-permute-done.14 = bf16[72,1536]{1,0:T(8,128)(2,1)S(1)} collective-permute-done((bf16[72,1536]{1,0:T(8,128)(2,1)S(1)}, bf16[72,1536]{1,0:T(8,128)(2,1)S(1)}, u32[]{:S(2)}, u32[]{:S(2)}) %collective-permute-start.14) | collective-permute-done | bytes 221216 | tf_op jit(solution)/shard_map/ppermute | solution.py:120
  93.4 0.7 collective-permute-done.15
  94.6 2.0 %collective-permute-start.17 = (bf16[32,1536]{1,0:T(8,128)(2,1)S(1)}, bf16[32,1536]{1,0:T(8,128)(2,1)S(1)}, u32[]{:S(2)}, u32[]{:S(2)}) collective-permute-start(bf16[32,1536]{1,0:T(8,128)(2,1)S(1)} %get-tuple-element.85), channel_id=1, source_target_pairs={{0,16},{1,17},{2,18},{3,19},{4,20},{5,21},{6,22},{7,23},{8,24},{9,... | collective-permute-start | bytes 294920 | tf_op jit(solution)/shard_map/ppermute | solution.py:125
  96.6 1.8 %collective-permute-start.18 = (bf16[32,1536]{1,0:T(8,128)(2,1)S(1)}, bf16[32,1536]{1,0:T(8,128)(2,1)S(1)}, u32[]{:S(2)}, u32[]{:S(2)}) collective-permute-start(bf16[32,1536]{1,0:T(8,128)(2,1)S(1)} %get-tuple-element.84), channel_id=1, source_target_pairs={{0,24},{1,25},{2,26},{3,27},{4,28},{5,29},{6,30},{7,31},{8,0},{9,1... | collective-permute-start | bytes 294920 | tf_op jit(solution)/shard_map/ppermute | solution.py:125
  98.4 4.7 %shard_map.114 = bf16[720,2880]{1,0:T(8,128)(2,1)} custom-call(bf16[576,720]{1,0:T(8,128)(2,1)S(1)} %pad_maximum_fusion.3.left_ref, bf16[576,2880]{1,0:T(8,128)(2,1)S(1)} %constant_dynamic-update-slice_fusion.3.right_ref), custom_call_target="tpu_custom_call" | custom-call | flops 2388787200 | bytes 8294400 | tf_op jit(solution)/shard_map/pallas_call | solution.py:80
  103.1 1.9 %collective-permute-done.17 = bf16[32,1536]{1,0:T(8,128)(2,1)S(1)} collective-permute-done((bf16[32,1536]{1,0:T(8,128)(2,1)S(1)}, bf16[32,1536]{1,0:T(8,128)(2,1)S(1)}, u32[]{:S(2)}, u32[]{:S(2)}) %collective-permute-start.17) | collective-permute-done | bytes 98336 | tf_op jit(solution)/shard_map/ppermute | solution.py:125
  105.8 1.7 %collective-permute-start.22 = (bf16[32,1344]{1,0:T(8,128)(2,1)S(1)}, bf16[32,1344]{1,0:T(8,128)(2,1)S(1)}, u32[]{:S(2)}, u32[]{:S(2)}) collective-permute-start(bf16[32,1344]{1,0:T(8,128)(2,1)S(1)} %get-tuple-element.89), channel_id=1, source_target_pairs={{0,8},{1,9},{2,10},{3,11},{4,12},{5,13},{6,14},{7,15},{8,16},{9,17... | collective-permute-start | bytes 258056 | tf_op jit(solution)/shard_map/ppermute | solution.py:125
  107.5 1.1 collective-permute-start.23
  108.6 1.3 %collective-permute-start.24 = (bf16[32,1344]{1,0:T(8,128)(2,1)S(1)}, bf16[32,1344]{1,0:T(8,128)(2,1)S(1)}, u32[]{:S(2)}, u32[]{:S(2)}) collective-permute-start(bf16[32,1344]{1,0:T(8,128)(2,1)S(1)} %get-tuple-element.87), channel_id=1, source_target_pairs={{0,24},{1,25},{2,26},{3,27},{4,28},{5,29},{6,30},{7,31},{8,0},{9,1... | collective-permute-start | bytes 258056 | tf_op jit(solution)/shard_map/ppermute | solution.py:125
  110.0 4.7 %shard_map.115 = bf16[720,2880]{1,0:T(8,128)(2,1)} custom-call(bf16[576,720]{1,0:T(8,128)(2,1)S(1)} %pad_maximum_fusion.4.left_ref, bf16[576,2880]{1,0:T(8,128)(2,1)S(1)} %constant_dynamic-update-slice_fusion.9.right_ref), custom_call_target="tpu_custom_call" | custom-call | flops 2388787200 | bytes 8294400 | tf_op jit(solution)/shard_map/pallas_call | solution.py:80
  114.7 0.9 collective-permute-done.23
  115.8 0.8 fusion.44
  (103 shorter events, 7.0 us)
Async XLA Ops:
  0.6 29.1 %copy-start.2 = (bf16[32,2880]{1,0:T(8,128)(2,1)S(1)}, bf16[32,2880]{1,0:T(8,128)(2,1)}, u32[]{:S(2)}) copy-start(bf16[32,2880]{1,0:T(8,128)(2,1)} %param.12) | copy-start | bytes 552964
  25.4 21.7 %collective-permute-start = (bf16[72,2880]{1,0:T(8,128)(2,1)S(1)}, bf16[72,2880]{1,0:T(8,128)(2,1)S(1)}, u32[]{:S(2)}, u32[]{:S(2)}) collective-permute-start(bf16[72,2880]{1,0:T(8,128)(2,1)S(1)} %convolution_convert_fusion.1), channel_id=1, source_target_pairs={{0,4},{1,5},{2,6},{3,7},{4,0},{5,1},{6,2},{7,3},{8,12},{9,13},{10,... | collective-permute-start | bytes 1244168 | tf_op jit(solution)/shard_map/ppermute | solution.py:120
  26.9 20.2 %collective-permute-start.2 = (bf16[72,2880]{1,0:T(8,128)(2,1)S(1)}, bf16[72,2880]{1,0:T(8,128)(2,1)S(1)}, u32[]{:S(2)}, u32[]{:S(2)}) collective-permute-start(bf16[72,2880]{1,0:T(8,128)(2,1)S(1)} %convolution_convert_fusion.1), channel_id=1, source_target_pairs={{0,6},{1,7},{2,4},{3,5},{4,2},{5,3},{6,0},{7,1},{8,14},{9,15},{10,... | collective-permute-start | bytes 1244168 | tf_op jit(solution)/shard_map/ppermute | solution.py:120
  28.8 18.3 %collective-permute-start.1 = (bf16[72,2880]{1,0:T(8,128)(2,1)S(1)}, bf16[72,2880]{1,0:T(8,128)(2,1)S(1)}, u32[]{:S(2)}, u32[]{:S(2)}) collective-permute-start(bf16[72,2880]{1,0:T(8,128)(2,1)S(1)} %convolution_convert_fusion), channel_id=1, source_target_pairs={{0,2},{1,3},{2,0},{3,1},{4,6},{5,7},{6,4},{7,5},{8,10},{9,11},{10,... | collective-permute-start | bytes 1244168 | tf_op jit(solution)/shard_map/ppermute | solution.py:120
  29.7 21.3 %copy-start = (bf16[1,2880,720]{1,2,0:T(8,128)(2,1)S(1)}, bf16[1,2880,720]{1,2,0:T(8,128)(2,1)}, u32[]{:S(2)}) copy-start(bf16[1,2880,720]{1,2,0:T(8,128)(2,1)} %param.13) | copy-start | bytes 12441604
  47.7 10.0 %collective-permute-start.3 = (bf16[72,2880]{1,0:T(8,128)(2,1)S(1)}, bf16[72,2880]{1,0:T(8,128)(2,1)S(1)}, u32[]{:S(2)}, u32[]{:S(2)}) collective-permute-start(bf16[72,2880]{1,0:T(8,128)(2,1)S(1)} %fusion.13), channel_id=1, source_target_pairs={{0,4},{1,5},{2,6},{3,7},{4,0},{5,1},{6,2},{7,3},{8,12},{9,13},{10,... | collective-permute-start | bytes 1244168 | tf_op jit(solution)/shard_map/ppermute | solution.py:120
  49.3 8.4 %collective-permute-start.4 = (bf16[72,2880]{1,0:T(8,128)(2,1)S(1)}, bf16[72,2880]{1,0:T(8,128)(2,1)S(1)}, u32[]{:S(2)}, u32[]{:S(2)}) collective-permute-start(bf16[72,2880]{1,0:T(8,128)(2,1)S(1)} %get-tuple-element.102), channel_id=1, source_target_pairs={{0,2},{1,3},{2,0},{3,1},{4,6},{5,7},{6,4},{7,5},{8,10},{9,11},{10,... | collective-permute-start | bytes 1244168 | tf_op jit(solution)/shard_map/ppermute | solution.py:120
  50.8 3.0 %collective-permute-start.5 = (bf16[144,2880]{1,0:T(8,128)(2,1)S(1)}, bf16[144,2880]{1,0:T(8,128)(2,1)S(1)}, u32[]{:S(2)}, u32[]{:S(2)}) collective-permute-start(bf16[144,2880]{1,0:T(8,128)(2,1)S(1)} %pad_maximum_fusion.5), channel_id=1, source_target_pairs={{0,1},{1,0},{2,3},{3,2},{4,5},{5,4},{6,7},{7,6},{8,9},{9,8},{10,11... | collective-permute-start | bytes 2488328 | tf_op jit(solution)/shard_map/ppermute | solution.py:120
  50.9 2.2 %slice-start = ((s8[4239360]{0:T(1024)(128)(4,1)}), s8[4194304]{0:T(1024)(128)(4,1)S(1)}, s32[]{:S(2)}) async-start(s8[4239360]{0:T(1024)(128)(4,1)} %bitcast.73), calls=%async_computation | async-start | bytes 8388608
  51.0 2.1 %slice-start.1 = ((s8[4239360]{0:T(1024)(128)(4,1)}), s8[45056]{0:T(1024)(128)(4,1)S(1)}, s32[]{:S(2)}) async-start(s8[4239360]{0:T(1024)(128)(4,1)} %bitcast.73), calls=%async_computation.1 | async-start | bytes 90112
  51.4 7.6 %collective-permute-start.9 = (bf16[144,2880]{1,0:T(8,128)(2,1)S(1)}, bf16[144,2880]{1,0:T(8,128)(2,1)S(1)}, u32[]{:S(2)}, u32[]{:S(2)}) collective-permute-start(bf16[144,2880]{1,0:T(8,128)(2,1)S(1)} %pad_maximum_fusion.7), channel_id=1, source_target_pairs={{0,1},{1,0},{2,3},{3,2},{4,5},{5,4},{6,7},{7,6},{8,9},{9,8},{10,11... | collective-permute-start | bytes 2488328 | tf_op jit(solution)/shard_map/ppermute | solution.py:120
  53.8 2.2 %slice-start.2 = ((s8[4239360]{0:T(1024)(128)(4,1)}), s8[4194304]{0:T(1024)(128)(4,1)S(1)}, s32[]{:S(2)}) async-start(s8[4239360]{0:T(1024)(128)(4,1)} %bitcast.80), calls=%async_computation.2 | async-start | bytes 8388608
  54.1 2.0 %slice-start.3 = ((s8[4239360]{0:T(1024)(128)(4,1)}), s8[45056]{0:T(1024)(128)(4,1)S(1)}, s32[]{:S(2)}) async-start(s8[4239360]{0:T(1024)(128)(4,1)} %bitcast.80), calls=%async_computation.3 | async-start | bytes 90112
  57.7 12.2 %collective-permute-start.8 = (bf16[72,2880]{1,0:T(8,128)(2,1)S(1)}, bf16[72,2880]{1,0:T(8,128)(2,1)S(1)}, u32[]{:S(2)}, u32[]{:S(2)}) collective-permute-start(bf16[72,2880]{1,0:T(8,128)(2,1)S(1)} %collective-permute-done.3), channel_id=1, source_target_pairs={{0,2},{1,3},{2,0},{3,1},{4,6},{5,7},{6,4},{7,5},{8,10},{9,11},{10,... | collective-permute-start | bytes 1244168 | tf_op jit(solution)/shard_map/ppermute | solution.py:120
  58.9 4.3 %collective-permute-start.6 = (bf16[144,2880]{1,0:T(8,128)(2,1)S(1)}, bf16[144,2880]{1,0:T(8,128)(2,1)S(1)}, u32[]{:S(2)}, u32[]{:S(2)}) collective-permute-start(bf16[144,2880]{1,0:T(8,128)(2,1)S(1)} %pad_maximum_fusion.6), channel_id=1, source_target_pairs={{0,1},{1,0},{2,3},{3,2},{4,5},{5,4},{6,7},{7,6},{8,9},{9,8},{10,11... | collective-permute-start | bytes 2488328 | tf_op jit(solution)/shard_map/ppermute | solution.py:120
  60.8 9.8 %collective-permute-start.10 = (bf16[72,2880]{1,0:T(8,128)(2,1)S(1)}, bf16[72,2880]{1,0:T(8,128)(2,1)S(1)}, u32[]{:S(2)}, u32[]{:S(2)}) collective-permute-start(bf16[72,2880]{1,0:T(8,128)(2,1)S(1)} %collective-permute-done.4), channel_id=1, source_target_pairs={{0,1},{1,0},{2,3},{3,2},{4,5},{5,4},{6,7},{7,6},{8,9},{9,8},{10,11... | collective-permute-start | bytes 1244168 | tf_op jit(solution)/shard_map/ppermute | solution.py:120
  69.9 1.8 %collective-permute-start.11 = (bf16[72,2880]{1,0:T(8,128)(2,1)S(1)}, bf16[72,2880]{1,0:T(8,128)(2,1)S(1)}, u32[]{:S(2)}, u32[]{:S(2)}) collective-permute-start(bf16[72,2880]{1,0:T(8,128)(2,1)S(1)} %collective-permute-done.8), channel_id=1, source_target_pairs={{0,1},{1,0},{2,3},{3,2},{4,5},{5,4},{6,7},{7,6},{8,9},{9,8},{10,11... | collective-permute-start | bytes 1244168 | tf_op jit(solution)/shard_map/ppermute | solution.py:120
  70.0 4.1 %collective-permute-start.7 = (bf16[144,2880]{1,0:T(8,128)(2,1)S(1)}, bf16[144,2880]{1,0:T(8,128)(2,1)S(1)}, u32[]{:S(2)}, u32[]{:S(2)}) collective-permute-start(bf16[144,2880]{1,0:T(8,128)(2,1)S(1)} %slice.112), channel_id=1, source_target_pairs={{0,1},{1,0},{2,3},{3,2},{4,5},{5,4},{6,7},{7,6},{8,9},{9,8},{10,11... | collective-permute-start | bytes 2488328 | tf_op jit(solution)/shard_map/ppermute | solution.py:120
  76.2 2.7 %collective-permute-start.12 = (bf16[144,1536]{1,0:T(8,128)(2,1)S(1)}, bf16[144,1536]{1,0:T(8,128)(2,1)S(1)}, u32[]{:S(2)}, u32[]{:S(2)}) collective-permute-start(bf16[144,1536]{1,0:T(8,128)(2,1)S(1)} %slice.116), channel_id=1, source_target_pairs={{0,1},{1,0},{2,3},{3,2},{4,5},{5,4},{6,7},{7,6},{8,9},{9,8},{10,11... | collective-permute-start | bytes 1327112 | tf_op jit(solution)/shard_map/ppermute | solution.py:120
  77.3 16.9 %collective-permute-start.15 = (bf16[72,2880]{1,0:T(8,128)(2,1)S(1)}, bf16[72,2880]{1,0:T(8,128)(2,1)S(1)}, u32[]{:S(2)}, u32[]{:S(2)}) collective-permute-start(bf16[72,2880]{1,0:T(8,128)(2,1)S(1)} %slice.183), channel_id=1, source_target_pairs={{0,4},{1,5},{2,6},{3,7},{4,0},{5,1},{6,2},{7,3},{8,12},{9,13},{10,... | collective-permute-start | bytes 1244168 | tf_op jit(solution)/shard_map/ppermute | solution.py:120
  78.8 8.0 %collective-permute-start.19 = (bf16[144,1344]{1,0:T(8,128)(2,1)S(1)}, bf16[144,1344]{1,0:T(8,128)(2,1)S(1)}, u32[]{:S(2)}, u32[]{:S(2)}) collective-permute-start(bf16[144,1344]{1,0:T(8,128)(2,1)S(1)} %slice.123), channel_id=1, source_target_pairs={{0,1},{1,0},{2,3},{3,2},{4,5},{5,4},{6,7},{7,6},{8,9},{9,8},{10,11... | collective-permute-start | bytes 1161224 | tf_op jit(solution)/shard_map/ppermute | solution.py:120
  79.1 9.9 %collective-permute-start.13 = (bf16[72,1536]{1,0:T(8,128)(2,1)S(1)}, bf16[72,1536]{1,0:T(8,128)(2,1)S(1)}, u32[]{:S(2)}, u32[]{:S(2)}) collective-permute-start(bf16[72,1536]{1,0:T(8,128)(2,1)S(1)} %get-tuple-element.91), channel_id=1, source_target_pairs={{0,2},{1,3},{2,0},{3,1},{4,6},{5,7},{6,4},{7,5},{8,10},{9,11},{10,... | collective-permute-start | bytes 663560 | tf_op jit(solution)/shard_map/ppermute | solution.py:120
  79.7 13.5 %collective-permute-start.14 = (bf16[72,1536]{1,0:T(8,128)(2,1)S(1)}, bf16[72,1536]{1,0:T(8,128)(2,1)S(1)}, u32[]{:S(2)}, u32[]{:S(2)}) collective-permute-start(bf16[72,1536]{1,0:T(8,128)(2,1)S(1)} %get-tuple-element.90), channel_id=1, source_target_pairs={{0,6},{1,7},{2,4},{3,5},{4,2},{5,3},{6,0},{7,1},{8,14},{9,15},{10,... | collective-permute-start | bytes 663560 | tf_op jit(solution)/shard_map/ppermute | solution.py:120
  87.0 18.0 %collective-permute-start.20 = (bf16[72,1344]{1,0:T(8,128)(2,1)S(1)}, bf16[72,1344]{1,0:T(8,128)(2,1)S(1)}, u32[]{:S(2)}, u32[]{:S(2)}) collective-permute-start(bf16[72,1344]{1,0:T(8,128)(2,1)S(1)} %get-tuple-element.97), channel_id=1, source_target_pairs={{0,2},{1,3},{2,0},{3,1},{4,6},{5,7},{6,4},{7,5},{8,10},{9,11},{10,... | collective-permute-start | bytes 580616 | tf_op jit(solution)/shard_map/ppermute | solution.py:120
  87.5 17.5 %collective-permute-start.21 = (bf16[72,1344]{1,0:T(8,128)(2,1)S(1)}, bf16[72,1344]{1,0:T(8,128)(2,1)S(1)}, u32[]{:S(2)}, u32[]{:S(2)}) collective-permute-start(bf16[72,1344]{1,0:T(8,128)(2,1)S(1)} %get-tuple-element.96), channel_id=1, source_target_pairs={{0,6},{1,7},{2,4},{3,5},{4,2},{5,3},{6,0},{7,1},{8,14},{9,15},{10,... | collective-permute-start | bytes 580616 | tf_op jit(solution)/shard_map/ppermute | solution.py:120
  94.5 8.6 %collective-permute-start.16 = (bf16[32,1536]{1,0:T(8,128)(2,1)S(1)}, bf16[32,1536]{1,0:T(8,128)(2,1)S(1)}, u32[]{:S(2)}, u32[]{:S(2)}) collective-permute-start(bf16[32,1536]{1,0:T(8,128)(2,1)S(1)} %get-tuple-element.86), channel_id=1, source_target_pairs={{0,8},{1,9},{2,10},{3,11},{4,12},{5,13},{6,14},{7,15},{8,16},{9,17... | collective-permute-start | bytes 294920 | tf_op jit(solution)/shard_map/ppermute | solution.py:125
  94.6 10.4 %collective-permute-start.17 = (bf16[32,1536]{1,0:T(8,128)(2,1)S(1)}, bf16[32,1536]{1,0:T(8,128)(2,1)S(1)}, u32[]{:S(2)}, u32[]{:S(2)}) collective-permute-start(bf16[32,1536]{1,0:T(8,128)(2,1)S(1)} %get-tuple-element.85), channel_id=1, source_target_pairs={{0,16},{1,17},{2,18},{3,19},{4,20},{5,21},{6,22},{7,23},{8,24},{9,... | collective-permute-start | bytes 294920 | tf_op jit(solution)/shard_map/ppermute | solution.py:125
  96.6 8.4 %collective-permute-start.18 = (bf16[32,1536]{1,0:T(8,128)(2,1)S(1)}, bf16[32,1536]{1,0:T(8,128)(2,1)S(1)}, u32[]{:S(2)}, u32[]{:S(2)}) collective-permute-start(bf16[32,1536]{1,0:T(8,128)(2,1)S(1)} %get-tuple-element.84), channel_id=1, source_target_pairs={{0,24},{1,25},{2,26},{3,27},{4,28},{5,29},{6,30},{7,31},{8,0},{9,1... | collective-permute-start | bytes 294920 | tf_op jit(solution)/shard_map/ppermute | solution.py:125
  105.8 8.9 %collective-permute-start.22 = (bf16[32,1344]{1,0:T(8,128)(2,1)S(1)}, bf16[32,1344]{1,0:T(8,128)(2,1)S(1)}, u32[]{:S(2)}, u32[]{:S(2)}) collective-permute-start(bf16[32,1344]{1,0:T(8,128)(2,1)S(1)} %get-tuple-element.89), channel_id=1, source_target_pairs={{0,8},{1,9},{2,10},{3,11},{4,12},{5,13},{6,14},{7,15},{8,16},{9,17... | collective-permute-start | bytes 258056 | tf_op jit(solution)/shard_map/ppermute | solution.py:125
  107.5 8.0 %collective-permute-start.23 = (bf16[32,1344]{1,0:T(8,128)(2,1)S(1)}, bf16[32,1344]{1,0:T(8,128)(2,1)S(1)}, u32[]{:S(2)}, u32[]{:S(2)}) collective-permute-start(bf16[32,1344]{1,0:T(8,128)(2,1)S(1)} %get-tuple-element.88), channel_id=1, source_target_pairs={{0,16},{1,17},{2,18},{3,19},{4,20},{5,21},{6,22},{7,23},{8,24},{9,... | collective-permute-start | bytes 258056 | tf_op jit(solution)/shard_map/ppermute | solution.py:125
  108.6 7.0 %copy-start.1 = (bf16[32,2880]{1,0:T(8,128)(2,1)S(1)}, bf16[32,2880]{1,0:T(8,128)(2,1)}, u32[]{:S(2)}) copy-start(bf16[32,2880]{1,0:T(8,128)(2,1)} %param.8) | copy-start | bytes 552964
  108.6 7.0 %copy-start.3 = (f32[2880]{0:T(1024)S(1)}, f32[2880]{0:T(1024)}, u32[]{:S(2)}) copy-start(f32[2880]{0:T(1024)} %param.9) | copy-start | bytes 34564
  108.6 6.9 %collective-permute-start.24 = (bf16[32,1344]{1,0:T(8,128)(2,1)S(1)}, bf16[32,1344]{1,0:T(8,128)(2,1)S(1)}, u32[]{:S(2)}, u32[]{:S(2)}) collective-permute-start(bf16[32,1344]{1,0:T(8,128)(2,1)S(1)} %get-tuple-element.87), channel_id=1, source_target_pairs={{0,24},{1,25},{2,26},{3,27},{4,28},{5,29},{6,30},{7,31},{8,0},{9,1... | collective-permute-start | bytes 258056 | tf_op jit(solution)/shard_map/ppermute | solution.py:125

commit v3 on v2

--- a/solution.py
+++ b/solution.py
@@ -96,11 +96,49 @@
     )(left, right)
 
 
-def three_parts(value):
-    first = lax.reduce_precision(value, 8, 7)
-    rest = value - first
-    second = lax.reduce_precision(rest, 8, 7)
-    return [part.astype(jnp.bfloat16) for part in (first, second, rest - second)]
+def payload_kernel(tokens_ref, gain_ref, ids_ref, weight_ref, out_ref, rstd_ref):
+    tok_count, width = tokens_ref.shape
+    top_count = ids_ref.shape[0]
+    expert_count = (out_ref.shape[1] - width) // 3
+    token_f = tokens_ref[...].astype(jnp.float32)
+    rstd = lax.rsqrt(jnp.mean(token_f * token_f, axis=-1, keepdims=True) + norm_eps)
+    rstd_ref[...] = rstd
+    out_ref[:, :width] = (token_f * rstd * gain_ref[...]).astype(jnp.bfloat16)
+    experts = lax.broadcasted_iota(jnp.int32, (expert_count, tok_count), 0)
+    weight = jnp.zeros((expert_count, tok_count), jnp.float32)
+    for k in range(top_count):
+        weight += jnp.where(ids_ref[k : k + 1, :] == experts, weight_ref[k : k + 1, :], 0.0)
+    parts = []
+    for _ in range(3):
+        parts.append(weight.astype(jnp.bfloat16))
+        weight = weight - parts[-1].astype(jnp.float32)
+    parts = jnp.concatenate([part.astype(jnp.float32) for part in parts], axis=0)
+    row = lax.broadcasted_iota(jnp.int32, (3 * expert_count, 3 * expert_count), 0)
+    col = lax.broadcasted_iota(jnp.int32, (3 * expert_count, 3 * expert_count), 1)
+    unit = (row == col).astype(jnp.bfloat16)
+    turned = lax.dot_general(
+        parts.astype(jnp.bfloat16),
+        unit,
+        (((0,), (0,)), ((), ())),
+        preferred_element_type=jnp.float32,
+    )
+    out_ref[:, width:] = turned.astype(jnp.bfloat16)
+
+
+def make_payload(tokens, norm_gain, expert_ids, combine_weight, expert_count):
+    tok_count, width = tokens.shape
+    return pl.pallas_call(
+        payload_kernel,
+        in_specs=[pl.BlockSpec(memory_space=pltpu.VMEM)] * 4,
+        out_specs=[pl.BlockSpec(memory_space=pltpu.VMEM)] * 2,
+        out_shape=[
+            jax.ShapeDtypeStruct((tok_count, width + 3 * expert_count), jnp.bfloat16),
+            jax.ShapeDtypeStruct((tok_count, 1), jnp.float32),
+        ],
+        cost_estimate=pl.CostEstimate(
+            flops=4 * tok_count * width, bytes_accessed=4 * tok_count * width, transcendentals=0
+        ),
+    )(tokens, norm_gain[None, :], expert_ids.T, combine_weight.T)
 
 
 def local(tokens, norm_gain, expert_ids, combine_weight, cotangent, w_gate, w_up, w_down):
@@ -124,13 +162,7 @@
         pairs = [(i, (i + step) % devices) for i in range(devices)]
         return lax.ppermute(row_major(value), "sq", pairs)
 
-    token_f = row_major(tokens).astype(jnp.float32)
-    rstd = lax.rsqrt(jnp.mean(token_f * token_f, axis=-1, keepdims=True) + norm_eps)
-    normed = (token_f * rstd * norm_gain).astype(jnp.bfloat16)
-
-    picked = expert_ids[:, :, None] == jnp.arange(expert_count, dtype=jnp.int32)[None, None, :]
-    weight = jnp.sum(jnp.where(picked, combine_weight[:, :, None], 0.0), axis=1)
-    payload = row_major(jnp.concatenate([normed] + three_parts(weight), axis=1))
+    payload, rstd = make_payload(tokens, norm_gain, expert_ids, combine_weight, expert_count)
 
     lines = [
         [plane * 2 * QUARTERS + place for plane in range(planes)] for place in range(2 * QUARTERS)
@@ -189,7 +221,6 @@
 
     gate_w = fast_copy(behind(w_gate[0], (own_dy, far_dy)).T).T
     up_w = w_up[0]
-    down_w = fast_copy(behind(w_down[0], gate_w))
 
     def forward(x_in):
         gate = jnp.dot(x_in, gate_w, preferred_element_type=jnp.float32)
@@ -216,6 +247,7 @@
     chip_x = both_cores(own_x, side_x)
     pair_x = both_cores(pair_x, across_x)
     chip_forward = forward(chip_x)
+    down_w = fast_copy(behind(w_down[0], chip_forward))
     side_dy, pair_dy = behind((side_dy, pair_dy), chip_forward)
     across_dy = flip(side_dy, PAIR)
     chip_dy = both_cores(own_dy, side_dy)
@@ -232,7 +264,7 @@
     pair_dy = jnp.concatenate([pair_dy, across_dy, pair_core_dy, flip(across_dy, CORE)], axis=0)
     pair_hid, pair_d_gate, pair_d_up = hidden(*pair_forward, pair_dy)
 
-    cut = -(-width // 2 // 256) * 256
+    cut = width // 2 // 256 * 256
     spans = [(0, cut), (cut, width)]
 
     def core_sum(rows, from_core):
@@ -294,6 +326,7 @@
     grads = [grad_gate.T[None], grad_up.T[None], grad_down[None]]
     d_normed = jnp.concatenate([first_half, second_half], axis=1)
 
+    token_f = row_major(tokens).astype(jnp.float32)
     scaled = d_normed * norm_gain
     mixed = jnp.mean(token_f * scaled, axis=-1, keepdims=True)
     d_tokens = (rstd * scaled - token_f * rstd * rstd * rstd * mixed).astype(jnp.bfloat16)

time: 117 us -> 122 us (1.043)
  waiting for transfers between devices: 10.1 us -> 16.3 us
  other arithmetic: 5.56 us -> 2.77 us
  Pallas kernels: 14.9 us -> 17 us
  starting transfers between devices: 23.7 us -> 21.9 us
  matrix products: 19.7 us -> 21.1 us
    ppermute x6, waiting for transfers between devices: 2.76 us -> 7.23 us  [shift(): return lax.ppermute(row_major(value), 'sq', pairs)]
    ppermute x6, starting transfers between devices: 8.06 us -> 6.08 us  [shift(): return lax.ppermute(row_major(value), 'sq', pairs)]
    pallas_call x0 -> x1, Pallas kernels: none -> 1.88 us  [make_payload(): pl.pallas_call(payload_kernel, in_specs=[pl.BlockSpec(memory_space=pltpu....]
    dot_general x2, matrix products: 3.29 us -> 5.14 us  [forward(): gate = jnp.dot(x_in, gate_w, preferred_element_type=jnp.float32)]
    reduce_sum x2 -> x0, other arithmetic: 1.81 us -> none  [the longest x1 1.07 us: local(): jnp.mean(token_f * token_f, axis=-1, keepdims=True) + norm_eps]
    ppermute x19, waiting for transfers between devices: 7.31 us -> 9.05 us  [flip(): lax.ppermute(row_major(value), 'sq', [(i, i ^ bit) for i in range(devices)])]
    broadcast_in_dim x0 -> x1, local copies, waits for them, and re-layouts: none -> 1.37 us  [make_payload(): norm_gain[None, :]]
  transfers between devices with their start and end apart: 25 -> 25, of which waited for: 6 -> 7; matrix products, arithmetic and copies ran while one was open for 16% -> 17% of each run, Pallas kernels for 13% -> 12%
where the time goes in v3:
time: 122 us
  blocking collectives  38.6 us (32%)
  starting transfers between devices  21.9 us (18%)
  matrix products  21.1 us (17%)
  Pallas kernels  17 us (14%)
  waiting for transfers between devices  16.3 us (13%)
  local copies, waits for them, and re-layouts  2.89 us (2%)
  other arithmetic  2.77 us (2%)
  between operations  1.36 us (1%)
    all_gather x2, blocking collectives, gather_column(): lax.all_gather(block, 'sq', axis=0, tiled=True, axis_index_groups=lines)  38.6 us
    ppermute x19, starting transfers between devices, flip(): lax.ppermute(row_major(value), 'sq', [(i, i ^ bit) for i in range(devices)])  15.8 us
    pallas_call x3, Pallas kernels, weight_product(): pl.pallas_call(product_kernel, in_specs=[pl.BlockSpec(memory_space=pltpu....  14.2 us
    dot_general x8, matrix products, contract_cols(): lax.dot_general(left, right, (((1,), (1,)), ((), ())), preferred_element_...  10.5 us
    ppermute x19, waiting for transfers between devices, flip(): lax.ppermute(row_major(value), 'sq', [(i, i ^ bit) for i in range(devices)])  9.05 us
    ppermute x6, waiting for transfers between devices, shift(): return lax.ppermute(row_major(value), 'sq', pairs)  7.23 us
    ppermute x6, starting transfers between devices, shift(): return lax.ppermute(row_major(value), 'sq', pairs)  6.08 us
    dot_general x2, matrix products, forward(): gate = jnp.dot(x_in, gate_w, preferred_element_type=jnp.float32)  5.14 us
  transfers between devices with their start and end apart: 25, of which 7 were waited for; matrix products, arithmetic and copies ran while one was open for 17% of the time, Pallas kernels for 12%

profile of v3, /device:TPU:0, one launch (start us, length us, event | category | flops | bytes accessed | tf_op | source)
XLA Modules:
  0.0 122.0 jit_solution(6419457006468898105)
XLA Ops:
  0.7 1.4 %broadcast_in_dim.72.gain_ref = f32[1,2880]{1,0:T(1,128)} reshape(f32[2880]{0:T(1024)} %param.9) | data formatting | bytes 23040 | tf_op jit(solution)/shard_map/broadcast_in_dim | solution.py:141
  2.0 1.9 %shard_map.111 = (bf16[32,2904]{1,0:T(8,128)(2,1)}, f32[32,1]{1,0:T(8,128)}) custom-call(bf16[32,2880]{1,0:T(8,128)(2,1)} %tokens_ref.1, f32[1,2880]{1,0:T(1,128)} %broadcast_in_dim.72.gain_ref, s32[4,32]{1,0:T(4,128)} %bitcast.85, f32[4,32]{1,0:T(4,128)} %bitcast.86), custom_call_target="tpu_custom_call" | custom-call | flops 368640 | bytes 368640 | tf_op jit(solution)/shard_map/pallas_call | solution.py:130
  3.9 21.3 %all_gather.6 = bf16[128,2904]{1,0:T(8,128)(2,1)S(1)} all-gather(bf16[32,2904]{1,0:T(8,128)(2,1)} %get-tuple-element.42), channel_id=1, replica_groups={{0,8,16,24},{1,9,17,25},{2,10,18,26},{3,11,19,27},{4,12,20,28},{5,13,21..., dimensions={0}, use_global_device_ids=true | all-gather | bytes 929280 | tf_op jit(solution)/shard_map/all_gather | solution.py:173
  25.8 1.6 %collective-permute-start = (bf16[72,2880]{1,0:T(8,128)(2,1)S(1)}, bf16[72,2880]{1,0:T(8,128)(2,1)S(1)}, u32[]{:S(2)}, u32[]{:S(2)}) collective-permute-start(bf16[72,2880]{1,0:T(8,128)(2,1)S(1)} %convolution_convert_fusion.1), channel_id=1, source_target_pairs={{0,4},{1,5},{2,6},{3,7},{4,0},{5,1},{6,2},{7,3},{8,12},{9,13},{10,... | collective-permute-start | bytes 1244168 | tf_op jit(solution)/shard_map/ppermute | solution.py:158
  27.4 1.4 %collective-permute-start.2 = (bf16[72,2880]{1,0:T(8,128)(2,1)S(1)}, bf16[72,2880]{1,0:T(8,128)(2,1)S(1)}, u32[]{:S(2)}, u32[]{:S(2)}) collective-permute-start(bf16[72,2880]{1,0:T(8,128)(2,1)S(1)} %convolution_convert_fusion.1), channel_id=1, source_target_pairs={{0,6},{1,7},{2,4},{3,5},{4,2},{5,3},{6,0},{7,1},{8,14},{9,15},{10,... | collective-permute-start | bytes 1244168 | tf_op jit(solution)/shard_map/ppermute | solution.py:158
  29.2 0.6 collective-permute-start.1
  30.3 17.4 %all_gather.7 = bf16[128,2880]{1,0:T(8,128)(2,1)S(1)} all-gather(bf16[32,2880]{1,0:T(8,128)(2,1)S(1)} %copy-done.2), channel_id=1, replica_groups={{0,8,16,24},{1,9,17,25},{2,10,18,26},{3,11,19,27},{4,12,20,28},{5,13,21..., dimensions={0}, use_global_device_ids=true | all-gather | bytes 921600 | tf_op jit(solution)/shard_map/all_gather | solution.py:173
  48.0 1.6 %collective-permute-start.3 = (bf16[72,2880]{1,0:T(8,128)(2,1)S(1)}, bf16[72,2880]{1,0:T(8,128)(2,1)S(1)}, u32[]{:S(2)}, u32[]{:S(2)}) collective-permute-start(bf16[72,2880]{1,0:T(8,128)(2,1)S(1)} %fusion.13), channel_id=1, source_target_pairs={{0,4},{1,5},{2,6},{3,7},{4,0},{5,1},{6,2},{7,3},{8,12},{9,13},{10,... | collective-permute-start | bytes 1244168 | tf_op jit(solution)/shard_map/ppermute | solution.py:158
  49.8 1.6 %collective-permute-start.4 = (bf16[72,2880]{1,0:T(8,128)(2,1)S(1)}, bf16[72,2880]{1,0:T(8,128)(2,1)S(1)}, u32[]{:S(2)}, u32[]{:S(2)}) collective-permute-start(bf16[72,2880]{1,0:T(8,128)(2,1)S(1)} %get-tuple-element.103), channel_id=1, source_target_pairs={{0,2},{1,3},{2,0},{3,1},{4,6},{5,7},{6,4},{7,5},{8,10},{9,11},{10,... | collective-permute-start | bytes 1244168 | tf_op jit(solution)/shard_map/ppermute | solution.py:158
  51.6 0.6 collective-permute-start.9
  52.7 1.2 collective-permute-done.5
  54.4 1.6 %fusion.4 = f32[288,720]{1,0:T(8,128)S(1)} fusion(bf16[288,2880]{1,0:T(8,128)(2,1)S(1)} %get-tuple-element.90, bf16[1,2880,720]{1,2,0:T(8,128)(2,1)S(1)} %bitcast.83), kind=kOutput, calls=%fused_computation.4 | convolution fusion | flops 1194393600 | bytes 6635520 | tf_op jit(solution)/shard_map/dot_general | solution.py:227
  56.0 2.6 %fusion.89 = f32[288,720]{1,0:T(8,128)} fusion(bf16[288,2880]{1,0:T(8,128)(2,1)S(1)} %get-tuple-element.90, bf16[720,2880]{1,0:T(8,128)(2,1)S(1)} %shard_map.112), kind=kOutput, calls=%fused_computation.153 | convolution fusion | flops 1194393600 | bytes 6635520 | tf_op jit(solution)/shard_map/dot_general | solution.py:226
  58.5 1.0 collective-permute-start.8
  59.7 1.6 %fusion = f32[288,720]{1,0:T(8,128)S(1)} fusion(bf16[288,2880]{1,0:T(8,128)(2,1)S(1)} %pad_maximum_fusion.1, bf16[1,2880,720]{1,2,0:T(8,128)(2,1)S(1)} %bitcast.83), kind=kOutput, calls=%fused_computation | convolution fusion | flops 1194393600 | bytes 6635520 | tf_op jit(solution)/shard_map/dot_general | solution.py:227
  61.5 0.5 collective-permute-start.6
  62.0 0.5 shard_map.113
  62.7 2.6 %fusion.91 = f32[288,720]{1,0:T(8,128)} fusion(bf16[288,2880]{1,0:T(8,128)(2,1)S(1)} %pad_maximum_fusion.1, bf16[720,2880]{1,0:T(8,128)(2,1)S(1)} %shard_map.112), kind=kOutput, calls=%fused_computation.155 | convolution fusion | flops 1194393600 | bytes 6635520 | tf_op jit(solution)/shard_map/dot_general | solution.py:226
  65.3 1.9 %multiply_convert_fusion.1 = (bf16[288,720]{1,0:T(8,128)(2,1)S(1)}, bf16[288,720]{1,0:T(8,128)(2,1)S(1)}, bf16[288,720]{1,0:T(8,128)(2,1)S(1)}) fusion(f32[288,720]{1,0:T(8,128)S(1)} %fusion.4, f32[288,720]{1,0:T(8,128)S(1)} %copy-done.5, bf16[720,2880]{1,0:T(8,128)(2,1)S(1)} %shard_map.113, bf16[144,2880]{1,0:T(8,128)(2,1)S(1)} %collective-permute-done.6, ...), kind=kOutput, calls=%fused_computation.44 | convolution fusion | flops 1202895360 | bytes 8709120 | tf_op jit(solution)/shard_map/dot_general | solution.py:25
  67.2 1.6 %fusion.90 = f32[288,2880]{1,0:T(8,128)S(1)} fusion(bf16[288,720]{1,0:T(8,128)(2,1)S(1)} %get-tuple-element.81, bf16[720,2880]{1,0:T(8,128)(2,1)S(1)} %shard_map.112), kind=kOutput, calls=%fused_computation.154 | convolution fusion | flops 1194393600 | bytes 7879680 | tf_op jit(solution)/shard_map/dot_general | solution.py:25
  68.7 1.6 %fusion.9 = bf16[288,2880]{1,0:T(8,128)(2,1)S(1)} fusion(f32[288,2880]{1,0:T(8,128)S(1)} %fusion.90, bf16[288,720]{1,0:T(8,128)(2,1)S(1)} %get-tuple-element.82, bf16[1,2880,720]{1,2,0:T(8,128)(2,1)S(1)} %bitcast.83), kind=kOutput, calls=%fused_computation.7 | convolution fusion | flops 1196052480 | bytes 9538560 | tf_op jit(solution)/shard_map/dot_general | solution.py:25
  70.8 0.5 collective-permute-start.7
  71.3 1.0 collective-permute-done.11
  72.4 1.9 %multiply_convert_fusion = (bf16[288,720]{1,0:T(8,128)(2,1)S(1)}, bf16[288,720]{1,0:T(8,128)(2,1)S(1)}, bf16[288,720]{1,0:T(8,128)(2,1)S(1)}) fusion(f32[288,720]{1,0:T(8,128)S(1)} %fusion, f32[288,720]{1,0:T(8,128)S(1)} %copy-done.6, bf16[720,2880]{1,0:T(8,128)(2,1)S(1)} %shard_map.113, bf16[72,2880]{1,0:T(8,128)(2,1)S(1)} %collective-permute-done.11, ...), kind=kOutput, calls=%fused_computation.43 | convolution fusion | flops 1204554240 | bytes 8709120 | tf_op jit(solution)/shard_map/dot_general | solution.py:25
  74.9 0.7 fusion.20
  75.6 0.7 fusion.14
  76.4 0.5 collective-permute-start.15
  76.9 1.0 fusion.16
  78.0 1.0 fusion.15
  79.1 0.6 collective-permute-start.19
  79.8 2.1 %collective-permute-start.14 = (bf16[72,1280]{1,0:T(8,128)(2,1)S(1)}, bf16[72,1280]{1,0:T(8,128)(2,1)S(1)}, u32[]{:S(2)}, u32[]{:S(2)}) collective-permute-start(bf16[72,1280]{1,0:T(8,128)(2,1)S(1)} %get-tuple-element.100), channel_id=1, source_target_pairs={{0,6},{1,7},{2,4},{3,5},{4,2},{5,3},{6,0},{7,1},{8,14},{9,15},{10,... | collective-permute-start | bytes 552968 | tf_op jit(solution)/shard_map/ppermute | solution.py:158
  81.9 1.0 collective-permute-start.13
  82.9 4.9 %shard_map.114 = bf16[720,2880]{1,0:T(8,128)(2,1)} custom-call(bf16[576,720]{1,0:T(8,128)(2,1)S(1)} %pad_maximum_fusion.2.left_ref, bf16[576,2880]{1,0:T(8,128)(2,1)S(1)} %constant_dynamic-update-slice_fusion.3.right_ref), custom_call_target="tpu_custom_call" | custom-call | flops 2388787200 | bytes 8294400 | tf_op jit(solution)/shard_map/pallas_call | solution.py:80
  88.0 1.0 collective-permute-start.21
  89.0 1.0 collective-permute-start.20
  90.0 2.4 %collective-permute-done.13 = bf16[72,1280]{1,0:T(8,128)(2,1)S(1)} collective-permute-done((bf16[72,1280]{1,0:T(8,128)(2,1)S(1)}, bf16[72,1280]{1,0:T(8,128)(2,1)S(1)}, u32[]{:S(2)}, u32[]{:S(2)}) %collective-permute-start.13) | collective-permute-done | bytes 184352 | tf_op jit(solution)/shard_map/ppermute | solution.py:158
  92.6 4.4 %collective-permute-done.15 = bf16[72,2880]{1,0:T(8,128)(2,1)S(1)} collective-permute-done((bf16[72,2880]{1,0:T(8,128)(2,1)S(1)}, bf16[72,2880]{1,0:T(8,128)(2,1)S(1)}, u32[]{:S(2)}, u32[]{:S(2)}) %collective-permute-start.15) | collective-permute-done | bytes 414752 | tf_op jit(solution)/shard_map/ppermute | solution.py:158
  97.4 1.5 %collective-permute-start.18 = (bf16[32,1280]{1,0:T(8,128)(2,1)S(1)}, bf16[32,1280]{1,0:T(8,128)(2,1)S(1)}, u32[]{:S(2)}, u32[]{:S(2)}) collective-permute-start(bf16[32,1280]{1,0:T(8,128)(2,1)S(1)} %get-tuple-element.91), channel_id=1, source_target_pairs={{0,24},{1,25},{2,26},{3,27},{4,28},{5,29},{6,30},{7,31},{8,0},{9,1... | collective-permute-start | bytes 245768 | tf_op jit(solution)/shard_map/ppermute | solution.py:163
  98.9 1.4 %collective-permute-start.16 = (bf16[32,1280]{1,0:T(8,128)(2,1)S(1)}, bf16[32,1280]{1,0:T(8,128)(2,1)S(1)}, u32[]{:S(2)}, u32[]{:S(2)}) collective-permute-start(bf16[32,1280]{1,0:T(8,128)(2,1)S(1)} %get-tuple-element.93), channel_id=1, source_target_pairs={{0,8},{1,9},{2,10},{3,11},{4,12},{5,13},{6,14},{7,15},{8,16},{9,17... | collective-permute-start | bytes 245768 | tf_op jit(solution)/shard_map/ppermute | solution.py:163
  100.3 4.7 %shard_map.115 = bf16[720,2880]{1,0:T(8,128)(2,1)} custom-call(bf16[576,720]{1,0:T(8,128)(2,1)S(1)} %pad_maximum_fusion.3.left_ref, bf16[576,2880]{1,0:T(8,128)(2,1)S(1)} %constant_dynamic-update-slice_fusion.3.right_ref), custom_call_target="tpu_custom_call" | custom-call | flops 2388787200 | bytes 8294400 | tf_op jit(solution)/shard_map/pallas_call | solution.py:80
  104.9 1.0 collective-permute-done.17
  106.0 4.7 %shard_map.116 = bf16[720,2880]{1,0:T(8,128)(2,1)} custom-call(bf16[576,720]{1,0:T(8,128)(2,1)S(1)} %pad_maximum_fusion.4.left_ref, bf16[576,2880]{1,0:T(8,128)(2,1)S(1)} %constant_dynamic-update-slice_fusion.9.right_ref), custom_call_target="tpu_custom_call" | custom-call | flops 2388787200 | bytes 8294400 | tf_op jit(solution)/shard_map/pallas_call | solution.py:80
  111.5 1.5 %collective-permute-start.24 = (bf16[32,1600]{1,0:T(8,128)(2,1)S(1)}, bf16[32,1600]{1,0:T(8,128)(2,1)S(1)}, u32[]{:S(2)}, u32[]{:S(2)}) collective-permute-start(bf16[32,1600]{1,0:T(8,128)(2,1)S(1)} %get-tuple-element.86), channel_id=1, source_target_pairs={{0,24},{1,25},{2,26},{3,27},{4,28},{5,29},{6,30},{7,31},{8,0},{9,1... | collective-permute-start | bytes 307208 | tf_op jit(solution)/shard_map/ppermute | solution.py:163
  113.0 1.1 collective-permute-start.23
  114.1 0.6 collective-permute-start.22
  114.7 1.5 %collective-permute-done.24 = bf16[32,1600]{1,0:T(8,128)(2,1)S(1)} collective-permute-done((bf16[32,1600]{1,0:T(8,128)(2,1)S(1)}, bf16[32,1600]{1,0:T(8,128)(2,1)S(1)}, u32[]{:S(2)}, u32[]{:S(2)}) %collective-permute-start.24) | collective-permute-done | bytes 102432 | tf_op jit(solution)/shard_map/ppermute | solution.py:163
  116.2 4.6 %collective-permute-done.23 = bf16[32,1600]{1,0:T(8,128)(2,1)S(1)} collective-permute-done((bf16[32,1600]{1,0:T(8,128)(2,1)S(1)}, bf16[32,1600]{1,0:T(8,128)(2,1)S(1)}, u32[]{:S(2)}, u32[]{:S(2)}) %collective-permute-start.23) | collective-permute-done | bytes 102432 | tf_op jit(solution)/shard_map/ppermute | solution.py:163
  121.1 0.8 fusion.41
  (103 shorter events, 6.6 us)
Async XLA Ops:
  0.6 29.6 %copy-start.2 = (bf16[32,2880]{1,0:T(8,128)(2,1)S(1)}, bf16[32,2880]{1,0:T(8,128)(2,1)}, u32[]{:S(2)}) copy-start(bf16[32,2880]{1,0:T(8,128)(2,1)} %param.12) | copy-start | bytes 552964
  3.9 26.1 %copy-start.4 = (f32[32,1]{1,0:T(8,128)S(1)}, f32[32,1]{1,0:T(8,128)}, u32[]{:S(2)}) copy-start(f32[32,1]{1,0:T(8,128)} %get-tuple-element.41) | copy-start | bytes 388
  25.8 21.9 %collective-permute-start = (bf16[72,2880]{1,0:T(8,128)(2,1)S(1)}, bf16[72,2880]{1,0:T(8,128)(2,1)S(1)}, u32[]{:S(2)}, u32[]{:S(2)}) collective-permute-start(bf16[72,2880]{1,0:T(8,128)(2,1)S(1)} %convolution_convert_fusion.1), channel_id=1, source_target_pairs={{0,4},{1,5},{2,6},{3,7},{4,0},{5,1},{6,2},{7,3},{8,12},{9,13},{10,... | collective-permute-start | bytes 1244168 | tf_op jit(solution)/shard_map/ppermute | solution.py:158
  27.4 20.3 %collective-permute-start.2 = (bf16[72,2880]{1,0:T(8,128)(2,1)S(1)}, bf16[72,2880]{1,0:T(8,128)(2,1)S(1)}, u32[]{:S(2)}, u32[]{:S(2)}) collective-permute-start(bf16[72,2880]{1,0:T(8,128)(2,1)S(1)} %convolution_convert_fusion.1), channel_id=1, source_target_pairs={{0,6},{1,7},{2,4},{3,5},{4,2},{5,3},{6,0},{7,1},{8,14},{9,15},{10,... | collective-permute-start | bytes 1244168 | tf_op jit(solution)/shard_map/ppermute | solution.py:158
  29.2 18.5 %collective-permute-start.1 = (bf16[72,2880]{1,0:T(8,128)(2,1)S(1)}, bf16[72,2880]{1,0:T(8,128)(2,1)S(1)}, u32[]{:S(2)}, u32[]{:S(2)}) collective-permute-start(bf16[72,2880]{1,0:T(8,128)(2,1)S(1)} %convolution_convert_fusion), channel_id=1, source_target_pairs={{0,2},{1,3},{2,0},{3,1},{4,6},{5,7},{6,4},{7,5},{8,10},{9,11},{10,... | collective-permute-start | bytes 1244168 | tf_op jit(solution)/shard_map/ppermute | solution.py:158
  30.3 21.9 %copy-start = (bf16[1,2880,720]{1,2,0:T(8,128)(2,1)S(1)}, bf16[1,2880,720]{1,2,0:T(8,128)(2,1)}, u32[]{:S(2)}) copy-start(bf16[1,2880,720]{1,2,0:T(8,128)(2,1)} %param.13) | copy-start | bytes 12441604
  48.0 10.6 %collective-permute-start.3 = (bf16[72,2880]{1,0:T(8,128)(2,1)S(1)}, bf16[72,2880]{1,0:T(8,128)(2,1)S(1)}, u32[]{:S(2)}, u32[]{:S(2)}) collective-permute-start(bf16[72,2880]{1,0:T(8,128)(2,1)S(1)} %fusion.13), channel_id=1, source_target_pairs={{0,4},{1,5},{2,6},{3,7},{4,0},{5,1},{6,2},{7,3},{8,12},{9,13},{10,... | collective-permute-start | bytes 1244168 | tf_op jit(solution)/shard_map/ppermute | solution.py:158
  49.8 8.7 %collective-permute-start.4 = (bf16[72,2880]{1,0:T(8,128)(2,1)S(1)}, bf16[72,2880]{1,0:T(8,128)(2,1)S(1)}, u32[]{:S(2)}, u32[]{:S(2)}) collective-permute-start(bf16[72,2880]{1,0:T(8,128)(2,1)S(1)} %get-tuple-element.103), channel_id=1, source_target_pairs={{0,2},{1,3},{2,0},{3,1},{4,6},{5,7},{6,4},{7,5},{8,10},{9,11},{10,... | collective-permute-start | bytes 1244168 | tf_op jit(solution)/shard_map/ppermute | solution.py:158
  51.5 2.4 %collective-permute-start.5 = (bf16[144,2880]{1,0:T(8,128)(2,1)S(1)}, bf16[144,2880]{1,0:T(8,128)(2,1)S(1)}, u32[]{:S(2)}, u32[]{:S(2)}) collective-permute-start(bf16[144,2880]{1,0:T(8,128)(2,1)S(1)} %pad_maximum_fusion.5), channel_id=1, source_target_pairs={{0,1},{1,0},{2,3},{3,2},{4,5},{5,4},{6,7},{7,6},{8,9},{9,8},{10,11... | collective-permute-start | bytes 2488328 | tf_op jit(solution)/shard_map/ppermute | solution.py:158
  51.6 8.0 %collective-permute-start.9 = (bf16[144,2880]{1,0:T(8,128)(2,1)S(1)}, bf16[144,2880]{1,0:T(8,128)(2,1)S(1)}, u32[]{:S(2)}, u32[]{:S(2)}) collective-permute-start(bf16[144,2880]{1,0:T(8,128)(2,1)S(1)} %pad_maximum_fusion.7), channel_id=1, source_target_pairs={{0,1},{1,0},{2,3},{3,2},{4,5},{5,4},{6,7},{7,6},{8,9},{9,8},{10,11... | collective-permute-start | bytes 2488328 | tf_op jit(solution)/shard_map/ppermute | solution.py:158
  52.2 2.2 %slice-start.2 = ((s8[4239360]{0:T(1024)(128)(4,1)}), s8[4194304]{0:T(1024)(128)(4,1)S(1)}, s32[]{:S(2)}) async-start(s8[4239360]{0:T(1024)(128)(4,1)} %bitcast.82), calls=%async_computation.2 | async-start | bytes 8388608
  52.2 2.2 %slice-start.3 = ((s8[4239360]{0:T(1024)(128)(4,1)}), s8[45056]{0:T(1024)(128)(4,1)S(1)}, s32[]{:S(2)}) async-start(s8[4239360]{0:T(1024)(128)(4,1)} %bitcast.82), calls=%async_computation.3 | async-start | bytes 90112
  58.5 12.0 %collective-permute-start.8 = (bf16[72,2880]{1,0:T(8,128)(2,1)S(1)}, bf16[72,2880]{1,0:T(8,128)(2,1)S(1)}, u32[]{:S(2)}, u32[]{:S(2)}) collective-permute-start(bf16[72,2880]{1,0:T(8,128)(2,1)S(1)} %collective-permute-done.3), channel_id=1, source_target_pairs={{0,2},{1,3},{2,0},{3,1},{4,6},{5,7},{6,4},{7,5},{8,10},{9,11},{10,... | collective-permute-start | bytes 1244168 | tf_op jit(solution)/shard_map/ppermute | solution.py:158
  59.6 2.4 %slice-start = ((s8[4239360]{0:T(1024)(128)(4,1)}), s8[4194304]{0:T(1024)(128)(4,1)S(1)}, s32[]{:S(2)}) async-start(s8[4239360]{0:T(1024)(128)(4,1)} %bitcast.75), calls=%async_computation | async-start | bytes 8388608
  59.7 2.3 %slice-start.1 = ((s8[4239360]{0:T(1024)(128)(4,1)}), s8[45056]{0:T(1024)(128)(4,1)S(1)}, s32[]{:S(2)}) async-start(s8[4239360]{0:T(1024)(128)(4,1)} %bitcast.75), calls=%async_computation.1 | async-start | bytes 90112
  61.4 9.9 %collective-permute-start.10 = (bf16[72,2880]{1,0:T(8,128)(2,1)S(1)}, bf16[72,2880]{1,0:T(8,128)(2,1)S(1)}, u32[]{:S(2)}, u32[]{:S(2)}) collective-permute-start(bf16[72,2880]{1,0:T(8,128)(2,1)S(1)} %collective-permute-done.4), channel_id=1, source_target_pairs={{0,1},{1,0},{2,3},{3,2},{4,5},{5,4},{6,7},{7,6},{8,9},{9,8},{10,11... | collective-permute-start | bytes 1244168 | tf_op jit(solution)/shard_map/ppermute | solution.py:158
  61.5 3.8 %collective-permute-start.6 = (bf16[144,2880]{1,0:T(8,128)(2,1)S(1)}, bf16[144,2880]{1,0:T(8,128)(2,1)S(1)}, u32[]{:S(2)}, u32[]{:S(2)}) collective-permute-start(bf16[144,2880]{1,0:T(8,128)(2,1)S(1)} %pad_maximum_fusion.6), channel_id=1, source_target_pairs={{0,1},{1,0},{2,3},{3,2},{4,5},{5,4},{6,7},{7,6},{8,9},{9,8},{10,11... | collective-permute-start | bytes 2488328 | tf_op jit(solution)/shard_map/ppermute | solution.py:158
  62.7 2.6 %copy-start.5 = (f32[288,720]{1,0:T(8,128)S(1)}, f32[288,720]{1,0:T(8,128)}, u32[]{:S(2)}) copy-start(f32[288,720]{1,0:T(8,128)} %fusion.89) | copy-start | bytes 2488324
  70.4 2.0 %copy-start.6 = (f32[288,720]{1,0:T(8,128)S(1)}, f32[288,720]{1,0:T(8,128)}, u32[]{:S(2)}) copy-start(f32[288,720]{1,0:T(8,128)} %fusion.91) | copy-start | bytes 2488324
  70.5 1.8 %collective-permute-start.11 = (bf16[72,2880]{1,0:T(8,128)(2,1)S(1)}, bf16[72,2880]{1,0:T(8,128)(2,1)S(1)}, u32[]{:S(2)}, u32[]{:S(2)}) collective-permute-start(bf16[72,2880]{1,0:T(8,128)(2,1)S(1)} %collective-permute-done.8), channel_id=1, source_target_pairs={{0,1},{1,0},{2,3},{3,2},{4,5},{5,4},{6,7},{7,6},{8,9},{9,8},{10,11... | collective-permute-start | bytes 1244168 | tf_op jit(solution)/shard_map/ppermute | solution.py:158
  70.8 3.8 %collective-permute-start.7 = (bf16[144,2880]{1,0:T(8,128)(2,1)S(1)}, bf16[144,2880]{1,0:T(8,128)(2,1)S(1)}, u32[]{:S(2)}, u32[]{:S(2)}) collective-permute-start(bf16[144,2880]{1,0:T(8,128)(2,1)S(1)} %slice.112), channel_id=1, source_target_pairs={{0,1},{1,0},{2,3},{3,2},{4,5},{5,4},{6,7},{7,6},{8,9},{9,8},{10,11... | collective-permute-start | bytes 2488328 | tf_op jit(solution)/shard_map/ppermute | solution.py:158
  76.4 20.6 %collective-permute-start.15 = (bf16[72,2880]{1,0:T(8,128)(2,1)S(1)}, bf16[72,2880]{1,0:T(8,128)(2,1)S(1)}, u32[]{:S(2)}, u32[]{:S(2)}) collective-permute-start(bf16[72,2880]{1,0:T(8,128)(2,1)S(1)} %slice.183), channel_id=1, source_target_pairs={{0,4},{1,5},{2,6},{3,7},{4,0},{5,1},{6,2},{7,3},{8,12},{9,13},{10,... | collective-permute-start | bytes 1244168 | tf_op jit(solution)/shard_map/ppermute | solution.py:158
  77.9 1.8 %collective-permute-start.12 = (bf16[144,1280]{1,0:T(8,128)(2,1)S(1)}, bf16[144,1280]{1,0:T(8,128)(2,1)S(1)}, u32[]{:S(2)}, u32[]{:S(2)}) collective-permute-start(bf16[144,1280]{1,0:T(8,128)(2,1)S(1)} %slice.116), channel_id=1, source_target_pairs={{0,1},{1,0},{2,3},{3,2},{4,5},{5,4},{6,7},{7,6},{8,9},{9,8},{10,11... | collective-permute-start | bytes 1105928 | tf_op jit(solution)/shard_map/ppermute | solution.py:158
  79.1 8.7 %collective-permute-start.19 = (bf16[144,1600]{1,0:T(8,128)(2,1)S(1)}, bf16[144,1600]{1,0:T(8,128)(2,1)S(1)}, u32[]{:S(2)}, u32[]{:S(2)}) collective-permute-start(bf16[144,1600]{1,0:T(8,128)(2,1)S(1)} %slice.123), channel_id=1, source_target_pairs={{0,1},{1,0},{2,3},{3,2},{4,5},{5,4},{6,7},{7,6},{8,9},{9,8},{10,11... | collective-permute-start | bytes 1382408 | tf_op jit(solution)/shard_map/ppermute | solution.py:158
  79.8 10.2 %collective-permute-start.14 = (bf16[72,1280]{1,0:T(8,128)(2,1)S(1)}, bf16[72,1280]{1,0:T(8,128)(2,1)S(1)}, u32[]{:S(2)}, u32[]{:S(2)}) collective-permute-start(bf16[72,1280]{1,0:T(8,128)(2,1)S(1)} %get-tuple-element.100), channel_id=1, source_target_pairs={{0,6},{1,7},{2,4},{3,5},{4,2},{5,3},{6,0},{7,1},{8,14},{9,15},{10,... | collective-permute-start | bytes 552968 | tf_op jit(solution)/shard_map/ppermute | solution.py:158
  81.9 10.4 %collective-permute-start.13 = (bf16[72,1280]{1,0:T(8,128)(2,1)S(1)}, bf16[72,1280]{1,0:T(8,128)(2,1)S(1)}, u32[]{:S(2)}, u32[]{:S(2)}) collective-permute-start(bf16[72,1280]{1,0:T(8,128)(2,1)S(1)} %get-tuple-element.101), channel_id=1, source_target_pairs={{0,2},{1,3},{2,0},{3,1},{4,6},{5,7},{6,4},{7,5},{8,10},{9,11},{10,... | collective-permute-start | bytes 552968 | tf_op jit(solution)/shard_map/ppermute | solution.py:158
  88.0 22.8 %collective-permute-start.21 = (bf16[72,1600]{1,0:T(8,128)(2,1)S(1)}, bf16[72,1600]{1,0:T(8,128)(2,1)S(1)}, u32[]{:S(2)}, u32[]{:S(2)}) collective-permute-start(bf16[72,1600]{1,0:T(8,128)(2,1)S(1)} %get-tuple-element.94), channel_id=1, source_target_pairs={{0,6},{1,7},{2,4},{3,5},{4,2},{5,3},{6,0},{7,1},{8,14},{9,15},{10,... | collective-permute-start | bytes 691208 | tf_op jit(solution)/shard_map/ppermute | solution.py:158
  89.0 21.7 %collective-permute-start.20 = (bf16[72,1600]{1,0:T(8,128)(2,1)S(1)}, bf16[72,1600]{1,0:T(8,128)(2,1)S(1)}, u32[]{:S(2)}, u32[]{:S(2)}) collective-permute-start(bf16[72,1600]{1,0:T(8,128)(2,1)S(1)} %get-tuple-element.95), channel_id=1, source_target_pairs={{0,2},{1,3},{2,0},{3,1},{4,6},{5,7},{6,4},{7,5},{8,10},{9,11},{10,... | collective-permute-start | bytes 691208 | tf_op jit(solution)/shard_map/ppermute | solution.py:158
  97.4 7.6 %collective-permute-start.18 = (bf16[32,1280]{1,0:T(8,128)(2,1)S(1)}, bf16[32,1280]{1,0:T(8,128)(2,1)S(1)}, u32[]{:S(2)}, u32[]{:S(2)}) collective-permute-start(bf16[32,1280]{1,0:T(8,128)(2,1)S(1)} %get-tuple-element.91), channel_id=1, source_target_pairs={{0,24},{1,25},{2,26},{3,27},{4,28},{5,29},{6,30},{7,31},{8,0},{9,1... | collective-permute-start | bytes 245768 | tf_op jit(solution)/shard_map/ppermute | solution.py:163
  98.9 7.1 %collective-permute-start.17 = (bf16[32,1280]{1,0:T(8,128)(2,1)S(1)}, bf16[32,1280]{1,0:T(8,128)(2,1)S(1)}, u32[]{:S(2)}, u32[]{:S(2)}) collective-permute-start(bf16[32,1280]{1,0:T(8,128)(2,1)S(1)} %get-tuple-element.92), channel_id=1, source_target_pairs={{0,16},{1,17},{2,18},{3,19},{4,20},{5,21},{6,22},{7,23},{8,24},{9,... | collective-permute-start | bytes 245768 | tf_op jit(solution)/shard_map/ppermute | solution.py:163
  98.9 7.1 %collective-permute-start.16 = (bf16[32,1280]{1,0:T(8,128)(2,1)S(1)}, bf16[32,1280]{1,0:T(8,128)(2,1)S(1)}, u32[]{:S(2)}, u32[]{:S(2)}) collective-permute-start(bf16[32,1280]{1,0:T(8,128)(2,1)S(1)} %get-tuple-element.93), channel_id=1, source_target_pairs={{0,8},{1,9},{2,10},{3,11},{4,12},{5,13},{6,14},{7,15},{8,16},{9,17... | collective-permute-start | bytes 245768 | tf_op jit(solution)/shard_map/ppermute | solution.py:163
  110.7 10.2 %copy-start.1 = (bf16[32,2880]{1,0:T(8,128)(2,1)S(1)}, bf16[32,2880]{1,0:T(8,128)(2,1)}, u32[]{:S(2)}) copy-start(bf16[32,2880]{1,0:T(8,128)(2,1)} %tokens_ref.1) | copy-start | bytes 552964
  110.7 10.2 %copy-start.3 = (f32[2880]{0:T(1024)S(1)}, f32[2880]{0:T(1024)}, u32[]{:S(2)}) copy-start(f32[2880]{0:T(1024)} %param.9) | copy-start | bytes 34564
  111.5 4.8 %collective-permute-start.24 = (bf16[32,1600]{1,0:T(8,128)(2,1)S(1)}, bf16[32,1600]{1,0:T(8,128)(2,1)S(1)}, u32[]{:S(2)}, u32[]{:S(2)}) collective-permute-start(bf16[32,1600]{1,0:T(8,128)(2,1)S(1)} %get-tuple-element.86), channel_id=1, source_target_pairs={{0,24},{1,25},{2,26},{3,27},{4,28},{5,29},{6,30},{7,31},{8,0},{9,1... | collective-permute-start | bytes 307208 | tf_op jit(solution)/shard_map/ppermute | solution.py:163
  113.0 7.9 %collective-permute-start.23 = (bf16[32,1600]{1,0:T(8,128)(2,1)S(1)}, bf16[32,1600]{1,0:T(8,128)(2,1)S(1)}, u32[]{:S(2)}, u32[]{:S(2)}) collective-permute-start(bf16[32,1600]{1,0:T(8,128)(2,1)S(1)} %get-tuple-element.87), channel_id=1, source_target_pairs={{0,16},{1,17},{2,18},{3,19},{4,20},{5,21},{6,22},{7,23},{8,24},{9,... | collective-permute-start | bytes 307208 | tf_op jit(solution)/shard_map/ppermute | solution.py:163
  114.1 6.8 %collective-permute-start.22 = (bf16[32,1600]{1,0:T(8,128)(2,1)S(1)}, bf16[32,1600]{1,0:T(8,128)(2,1)S(1)}, u32[]{:S(2)}, u32[]{:S(2)}) collective-permute-start(bf16[32,1600]{1,0:T(8,128)(2,1)S(1)} %get-tuple-element.88), channel_id=1, source_target_pairs={{0,8},{1,9},{2,10},{3,11},{4,12},{5,13},{6,14},{7,15},{8,16},{9,17... | collective-permute-start | bytes 307208 | tf_op jit(solution)/shard_map/ppermute | solution.py:163

commit v4 on v2

--- a/solution.py
+++ b/solution.py
@@ -182,6 +182,7 @@
     far_dy = rows_dy(far_select, far_weight)
     side_dy = flip(far_dy, SIDE)
     pair_dy = flip(own_dy, PAIR)
+    across_dy = flip(far_dy, PAIR | SIDE)
 
     def both_cores(first, second):
         rows = jnp.concatenate([first, second], axis=0)
@@ -189,7 +190,6 @@
 
     gate_w = fast_copy(behind(w_gate[0], (own_dy, far_dy)).T).T
     up_w = w_up[0]
-    down_w = fast_copy(behind(w_down[0], gate_w))
 
     def forward(x_in):
         gate = jnp.dot(x_in, gate_w, preferred_element_type=jnp.float32)
@@ -212,14 +212,16 @@
             contract_cols(d_gate, gate_w[first:last]) + contract_cols(d_up, up_w[first:last])
         ).astype(jnp.bfloat16)
 
-    own_x, side_x, pair_x, across_x = behind((own_x, side_x, pair_x, across_x), (own_dy, far_dy))
-    chip_x = both_cores(own_x, side_x)
+    chip_x = behind(both_cores(own_x, side_x), (own_dy, far_dy))
     pair_x = both_cores(pair_x, across_x)
     chip_forward = forward(chip_x)
-    side_dy, pair_dy = behind((side_dy, pair_dy), chip_forward)
-    across_dy = flip(side_dy, PAIR)
+    down_w = fast_copy(behind(w_down[0], chip_forward))
+    pair_forward = forward(behind(pair_x, chip_forward))
+    side_dy, pair_dy, across_dy = behind(
+        (side_dy, pair_dy, across_dy), (chip_forward, pair_forward)
+    )
     chip_dy = both_cores(own_dy, side_dy)
-    pair_forward = forward(behind(pair_x, chip_dy))
+    pair_dy = both_cores(pair_dy, across_dy)
     chip_hid, chip_d_gate, chip_d_up = hidden(*chip_forward, chip_dy)
     chip_rows = row_gradient(chip_d_gate, chip_d_up, 0, width)
     chip_sum = chip_rows[:kept].astype(jnp.float32) + flip(chip_rows[kept:], CORE).astype(
@@ -227,10 +229,7 @@
     )
     side_sum = flip(chip_sum[slots:].astype(jnp.bfloat16), SIDE)
 
-    pair_core_dy = flip(pair_dy, CORE)
-    across_dy = behind(across_dy, (chip_rows, pair_forward))
-    pair_dy = jnp.concatenate([pair_dy, across_dy, pair_core_dy, flip(across_dy, CORE)], axis=0)
-    pair_hid, pair_d_gate, pair_d_up = hidden(*pair_forward, pair_dy)
+    pair_hid, pair_d_gate, pair_d_up = hidden(*pair_forward, behind(pair_dy, chip_rows))
 
     cut = -(-width // 2 // 256) * 256
     spans = [(0, cut), (cut, width)]
@@ -288,8 +287,9 @@
     first_half = to_tokens(d_column)
     grad_up = weight_gradient(d_up, x_in, d_column)
     first_half = added(*behind(first_half, grad_up))
-    second_half = to_tokens(to_column(spans[1], *behind(sent_second, first_half)))
-    grad_down = weight_gradient(hid, dy_e, first_half)
+    d_column = to_column(spans[1], *behind(sent_second, first_half))
+    second_half = to_tokens(d_column)
+    grad_down = weight_gradient(hid, dy_e, d_column)
     second_half = added(*behind(second_half, grad_down))
     grads = [grad_gate.T[None], grad_up.T[None], grad_down[None]]
     d_normed = jnp.concatenate([first_half, second_half], axis=1)

time: 117 us -> 125 us (1.068)
  waiting for transfers between devices: 10.1 us -> 20 us
  local copies, waits for them, and re-layouts: 2.98 us -> 1.68 us
    ppermute x19 -> x18, waiting for transfers between devices: 7.31 us -> 17.2 us  [flip(): lax.ppermute(row_major(value), 'sq', [(i, i ^ bit) for i in range(devices)])]
    unnamed x26 -> x23, local copies, waits for them, and re-layouts: 2.19 us -> 0.83 us
    ppermute x19 -> x18, starting transfers between devices: 15.7 us -> 15.2 us  [flip(): lax.ppermute(row_major(value), 'sq', [(i, i ^ bit) for i in range(devices)])]
  transfers between devices with their start and end apart: 25 -> 24, of which waited for: 6 -> 8; matrix products, arithmetic and copies ran while one was open for 16% -> 13% of each run, Pallas kernels for 13% -> 12%
where the time goes in v4:
time: 125 us
  blocking collectives  38.3 us (31%)
  starting transfers between devices  23.3 us (19%)
  waiting for transfers between devices  20 us (16%)
  matrix products  19.3 us (15%)
  Pallas kernels  15.1 us (12%)
  other arithmetic  5.88 us (5%)
  local copies, waits for them, and re-layouts  1.68 us (1%)
  between operations  1.38 us (1%)
    all_gather x2, blocking collectives, gather_column(): lax.all_gather(block, 'sq', axis=0, tiled=True, axis_index_groups=lines)  38.3 us
    ppermute x18, waiting for transfers between devices, flip(): lax.ppermute(row_major(value), 'sq', [(i, i ^ bit) for i in range(devices)])  17.2 us
    ppermute x18, starting transfers between devices, flip(): lax.ppermute(row_major(value), 'sq', [(i, i ^ bit) for i in range(devices)])  15.2 us
    pallas_call x3, Pallas kernels, weight_product(): pl.pallas_call(product_kernel, in_specs=[pl.BlockSpec(memory_space=pltpu....  14.2 us
    dot_general x8, matrix products, contract_cols(): lax.dot_general(left, right, (((1,), (1,)), ((), ())), preferred_element_...  10.4 us
    ppermute x6, starting transfers between devices, shift(): return lax.ppermute(row_major(value), 'sq', pairs)  8.06 us
    dot_general x2, matrix products, forward(): gate = jnp.dot(x_in, gate_w, preferred_element_type=jnp.float32)  3.29 us
    dot_general x2, matrix products, forward(): up = jnp.dot(x_in, up_w, preferred_element_type=jnp.float32)  3.25 us
  transfers between devices with their start and end apart: 24, of which 8 were waited for; matrix products, arithmetic and copies ran while one was open for 13% of the time, Pallas kernels for 12%

profile of v4, /device:TPU:0, one launch (start us, length us, event | category | flops | bytes accessed | tf_op | source)
XLA Modules:
  0.0 124.9 jit_solution(13015104672185607037)
XLA Ops:
  0.6 0.7 select_reduce_fusion.4
  1.6 1.1 fusion.43
  2.7 1.0 fusion.38
  3.8 20.9 %all_gather.6 = bf16[128,2904]{1,0:T(8,128)(2,1)S(1)} all-gather(bf16[32,2904]{1,0:T(8,128)(2,1)S(1)} %concatenate.51), channel_id=1, replica_groups={{0,8,16,24},{1,9,17,25},{2,10,18,26},{3,11,19,27},{4,12,20,28},{5,13,21..., dimensions={0}, use_global_device_ids=true | all-gather | bytes 929280 | tf_op jit(solution)/shard_map/all_gather | solution.py:141
  25.4 1.6 %collective-permute-start = (bf16[72,2880]{1,0:T(8,128)(2,1)S(1)}, bf16[72,2880]{1,0:T(8,128)(2,1)S(1)}, u32[]{:S(2)}, u32[]{:S(2)}) collective-permute-start(bf16[72,2880]{1,0:T(8,128)(2,1)S(1)} %convolution_convert_fusion.1), channel_id=1, source_target_pairs={{0,4},{1,5},{2,6},{3,7},{4,0},{5,1},{6,2},{7,3},{8,12},{9,13},{10,... | collective-permute-start | bytes 1244168 | tf_op jit(solution)/shard_map/ppermute | solution.py:120
  26.9 1.4 %collective-permute-start.2 = (bf16[72,2880]{1,0:T(8,128)(2,1)S(1)}, bf16[72,2880]{1,0:T(8,128)(2,1)S(1)}, u32[]{:S(2)}, u32[]{:S(2)}) collective-permute-start(bf16[72,2880]{1,0:T(8,128)(2,1)S(1)} %convolution_convert_fusion.1), channel_id=1, source_target_pairs={{0,6},{1,7},{2,4},{3,5},{4,2},{5,3},{6,0},{7,1},{8,14},{9,15},{10,... | collective-permute-start | bytes 1244168 | tf_op jit(solution)/shard_map/ppermute | solution.py:120
  28.8 0.6 collective-permute-start.1
  29.7 17.4 %all_gather.7 = bf16[128,2880]{1,0:T(8,128)(2,1)S(1)} all-gather(bf16[32,2880]{1,0:T(8,128)(2,1)S(1)} %copy-done.2), channel_id=1, replica_groups={{0,8,16,24},{1,9,17,25},{2,10,18,26},{3,11,19,27},{4,12,20,28},{5,13,21..., dimensions={0}, use_global_device_ids=true | all-gather | bytes 921600 | tf_op jit(solution)/shard_map/all_gather | solution.py:141
  47.6 1.6 %collective-permute-start.3 = (bf16[72,2880]{1,0:T(8,128)(2,1)S(1)}, bf16[72,2880]{1,0:T(8,128)(2,1)S(1)}, u32[]{:S(2)}, u32[]{:S(2)}) collective-permute-start(bf16[72,2880]{1,0:T(8,128)(2,1)S(1)} %fusion.13), channel_id=1, source_target_pairs={{0,4},{1,5},{2,6},{3,7},{4,0},{5,1},{6,2},{7,3},{8,12},{9,13},{10,... | collective-permute-start | bytes 1244168 | tf_op jit(solution)/shard_map/ppermute | solution.py:120
  49.1 1.4 %collective-permute-start.5 = (bf16[72,2880]{1,0:T(8,128)(2,1)S(1)}, bf16[72,2880]{1,0:T(8,128)(2,1)S(1)}, u32[]{:S(2)}, u32[]{:S(2)}) collective-permute-start(bf16[72,2880]{1,0:T(8,128)(2,1)S(1)} %fusion.13), channel_id=1, source_target_pairs={{0,6},{1,7},{2,4},{3,5},{4,2},{5,3},{6,0},{7,1},{8,14},{9,15},{10,... | collective-permute-start | bytes 1244168 | tf_op jit(solution)/shard_map/ppermute | solution.py:120
  50.9 0.6 collective-permute-start.4
  52.1 1.6 %fusion.90 = f32[288,720]{1,0:T(8,128)S(1)} fusion(bf16[288,2880]{1,0:T(8,128)(2,1)S(1)} %pad_maximum_fusion, bf16[720,2880]{1,0:T(8,128)(2,1)S(1)} %shard_map.111), kind=kOutput, calls=%fused_computation.156 | convolution fusion | flops 1194393600 | bytes 6635520 | tf_op jit(solution)/shard_map/dot_general | solution.py:195
  53.8 0.4 slice-done.2
  54.2 1.6 %fusion.4 = f32[288,720]{1,0:T(8,128)S(1)} fusion(bf16[288,2880]{1,0:T(8,128)(2,1)S(1)} %pad_maximum_fusion, bf16[1,2880,720]{1,2,0:T(8,128)(2,1)S(1)} %bitcast.82), kind=kOutput, calls=%fused_computation.4 | convolution fusion | flops 1194393600 | bytes 6635520 | tf_op jit(solution)/shard_map/dot_general | solution.py:196
  56.0 1.6 %fusion.2 = f32[288,720]{1,0:T(8,128)S(1)} fusion(bf16[288,2880]{1,0:T(8,128)(2,1)S(1)} %pad_maximum_fusion.1, bf16[1,2880,720]{1,2,0:T(8,128)(2,1)S(1)} %bitcast.82), kind=kOutput, calls=%fused_computation.2 | convolution fusion | flops 1194393600 | bytes 6635520 | tf_op jit(solution)/shard_map/dot_general | solution.py:196
  57.6 1.6 %fusion.91 = f32[288,720]{1,0:T(8,128)S(1)} fusion(bf16[288,2880]{1,0:T(8,128)(2,1)S(1)} %pad_maximum_fusion.1, bf16[720,2880]{1,0:T(8,128)(2,1)S(1)} %shard_map.111), kind=kOutput, calls=%fused_computation.157 | convolution fusion | flops 1194393600 | bytes 6635520 | tf_op jit(solution)/shard_map/dot_general | solution.py:195
  59.4 9.5 %collective-permute-done.3 = bf16[72,2880]{1,0:T(8,128)(2,1)S(1)} collective-permute-done((bf16[72,2880]{1,0:T(8,128)(2,1)S(1)}, bf16[72,2880]{1,0:T(8,128)(2,1)S(1)}, u32[]{:S(2)}, u32[]{:S(2)}) %collective-permute-start.3) | collective-permute-done | bytes 414752 | tf_op jit(solution)/shard_map/ppermute | solution.py:120
  68.9 1.2 collective-permute-done.4
  70.4 0.6 collective-permute-start.10
  71.0 0.5 shard_map.112
  71.7 1.0 collective-permute-done.8
  72.7 1.9 %multiply_convert_fusion.1 = (bf16[288,720]{1,0:T(8,128)(2,1)S(1)}, bf16[288,720]{1,0:T(8,128)(2,1)S(1)}, bf16[288,720]{1,0:T(8,128)(2,1)S(1)}) fusion(f32[288,720]{1,0:T(8,128)S(1)} %fusion.4, f32[288,720]{1,0:T(8,128)S(1)} %fusion.90, bf16[720,2880]{1,0:T(8,128)(2,1)S(1)} %shard_map.112, bf16[144,2880]{1,0:T(8,128)(2,1)S(1)} %collective-permute-done.8, ...), kind=kOutput, calls=%fused_computation.42 | convolution fusion | flops 1202895360 | bytes 8709120 | tf_op jit(solution)/shard_map/dot_general | solution.py:25
  74.5 1.6 %fusion.92 = f32[288,2880]{1,0:T(8,128)S(1)} fusion(bf16[288,720]{1,0:T(8,128)(2,1)S(1)} %get-tuple-element.73, bf16[720,2880]{1,0:T(8,128)(2,1)S(1)} %shard_map.111), kind=kOutput, calls=%fused_computation.158 | convolution fusion | flops 1194393600 | bytes 7879680 | tf_op jit(solution)/shard_map/dot_general | solution.py:25
  76.1 1.6 %fusion.9 = bf16[288,2880]{1,0:T(8,128)(2,1)S(1)} fusion(f32[288,2880]{1,0:T(8,128)S(1)} %fusion.92, bf16[288,720]{1,0:T(8,128)(2,1)S(1)} %get-tuple-element.74, bf16[1,2880,720]{1,2,0:T(8,128)(2,1)S(1)} %bitcast.82), kind=kOutput, calls=%fused_computation.7 | convolution fusion | flops 1196052480 | bytes 9538560 | tf_op jit(solution)/shard_map/dot_general | solution.py:25
  78.1 1.9 %multiply_convert_fusion = (bf16[288,720]{1,0:T(8,128)(2,1)S(1)}, bf16[288,720]{1,0:T(8,128)(2,1)S(1)}, bf16[288,720]{1,0:T(8,128)(2,1)S(1)}) fusion(f32[288,720]{1,0:T(8,128)S(1)} %fusion.2, f32[288,720]{1,0:T(8,128)S(1)} %fusion.91, bf16[288,2880]{1,0:T(8,128)(2,1)S(1)} %pad_maximum_fusion.2, bf16[720,2880]{1,0:T(8,128)(2,1)S(1)} %shard_map.112), kind=kOutput, calls=%fused_computation.41 | convolution fusion | flops 1197918720 | bytes 8709120 | tf_op jit(solution)/shard_map/dot_general | solution.py:25
  80.6 1.9 %collective-permute-done.9 = bf16[144,2880]{1,0:T(8,128)(2,1)S(1)} collective-permute-done((bf16[144,2880]{1,0:T(8,128)(2,1)S(1)}, bf16[144,2880]{1,0:T(8,128)(2,1)S(1)}, u32[]{:S(2)}, u32[]{:S(2)}) %collective-permute-start.9) | collective-permute-done | bytes 829472 | tf_op jit(solution)/shard_map/ppermute | solution.py:120
  82.7 0.8 fusion.16
  83.5 0.9 fusion.14
  84.7 0.8 fusion.20
  85.6 1.6 %collective-permute-start.14 = (bf16[72,2880]{1,0:T(8,128)(2,1)S(1)}, bf16[72,2880]{1,0:T(8,128)(2,1)S(1)}, u32[]{:S(2)}, u32[]{:S(2)}) collective-permute-start(bf16[72,2880]{1,0:T(8,128)(2,1)S(1)} %slice.183), channel_id=1, source_target_pairs={{0,4},{1,5},{2,6},{3,7},{4,0},{5,1},{6,2},{7,3},{8,12},{9,13},{10,... | collective-permute-start | bytes 1244168 | tf_op jit(solution)/shard_map/ppermute | solution.py:120
  87.1 0.9 fusion.15
  88.4 1.6 %collective-permute-start.12 = (bf16[72,1536]{1,0:T(8,128)(2,1)S(1)}, bf16[72,1536]{1,0:T(8,128)(2,1)S(1)}, u32[]{:S(2)}, u32[]{:S(2)}) collective-permute-start(bf16[72,1536]{1,0:T(8,128)(2,1)S(1)} %get-tuple-element.85), channel_id=1, source_target_pairs={{0,2},{1,3},{2,0},{3,1},{4,6},{5,7},{6,4},{7,5},{8,10},{9,11},{10,... | collective-permute-start | bytes 663560 | tf_op jit(solution)/shard_map/ppermute | solution.py:120
  89.9 0.5 collective-permute-start.13
  90.4 4.9 %shard_map.113 = bf16[720,2880]{1,0:T(8,128)(2,1)} custom-call(bf16[576,720]{1,0:T(8,128)(2,1)S(1)} %pad_maximum_fusion.3.left_ref, bf16[576,2880]{1,0:T(8,128)(2,1)S(1)} %constant_dynamic-update-slice_fusion.right_ref), custom_call_target="tpu_custom_call" | custom-call | flops 2388787200 | bytes 8294400 | tf_op jit(solution)/shard_map/pallas_call | solution.py:80
  95.5 1.6 %collective-permute-start.19 = (bf16[72,1344]{1,0:T(8,128)(2,1)S(1)}, bf16[72,1344]{1,0:T(8,128)(2,1)S(1)}, u32[]{:S(2)}, u32[]{:S(2)}) collective-permute-start(bf16[72,1344]{1,0:T(8,128)(2,1)S(1)} %get-tuple-element.87), channel_id=1, source_target_pairs={{0,2},{1,3},{2,0},{3,1},{4,6},{5,7},{6,4},{7,5},{8,10},{9,11},{10,... | collective-permute-start | bytes 580616 | tf_op jit(solution)/shard_map/ppermute | solution.py:120
  97.0 1.5 %collective-permute-start.20 = (bf16[72,1344]{1,0:T(8,128)(2,1)S(1)}, bf16[72,1344]{1,0:T(8,128)(2,1)S(1)}, u32[]{:S(2)}, u32[]{:S(2)}) collective-permute-start(bf16[72,1344]{1,0:T(8,128)(2,1)S(1)} %get-tuple-element.86), channel_id=1, source_target_pairs={{0,6},{1,7},{2,4},{3,5},{4,2},{5,3},{6,0},{7,1},{8,14},{9,15},{10,... | collective-permute-start | bytes 580616 | tf_op jit(solution)/shard_map/ppermute | solution.py:120
  98.5 2.9 %collective-permute-done.13 = bf16[72,1536]{1,0:T(8,128)(2,1)S(1)} collective-permute-done((bf16[72,1536]{1,0:T(8,128)(2,1)S(1)}, bf16[72,1536]{1,0:T(8,128)(2,1)S(1)}, u32[]{:S(2)}, u32[]{:S(2)}) %collective-permute-start.13) | collective-permute-done | bytes 221216 | tf_op jit(solution)/shard_map/ppermute | solution.py:120
  101.7 0.7 collective-permute-done.14
  102.9 2.1 %collective-permute-start.16 = (bf16[32,1536]{1,0:T(8,128)(2,1)S(1)}, bf16[32,1536]{1,0:T(8,128)(2,1)S(1)}, u32[]{:S(2)}, u32[]{:S(2)}) collective-permute-start(bf16[32,1536]{1,0:T(8,128)(2,1)S(1)} %get-tuple-element.79), channel_id=1, source_target_pairs={{0,16},{1,17},{2,18},{3,19},{4,20},{5,21},{6,22},{7,23},{8,24},{9,... | collective-permute-start | bytes 294920 | tf_op jit(solution)/shard_map/ppermute | solution.py:125
  104.9 1.8 %collective-permute-start.17 = (bf16[32,1536]{1,0:T(8,128)(2,1)S(1)}, bf16[32,1536]{1,0:T(8,128)(2,1)S(1)}, u32[]{:S(2)}, u32[]{:S(2)}) collective-permute-start(bf16[32,1536]{1,0:T(8,128)(2,1)S(1)} %get-tuple-element.78), channel_id=1, source_target_pairs={{0,24},{1,25},{2,26},{3,27},{4,28},{5,29},{6,30},{7,31},{8,0},{9,1... | collective-permute-start | bytes 294920 | tf_op jit(solution)/shard_map/ppermute | solution.py:125
  106.7 4.7 %shard_map.114 = bf16[720,2880]{1,0:T(8,128)(2,1)} custom-call(bf16[576,720]{1,0:T(8,128)(2,1)S(1)} %pad_maximum_fusion.4.left_ref, bf16[576,2880]{1,0:T(8,128)(2,1)S(1)} %constant_dynamic-update-slice_fusion.right_ref), custom_call_target="tpu_custom_call" | custom-call | flops 2388787200 | bytes 8294400 | tf_op jit(solution)/shard_map/pallas_call | solution.py:80
  111.4 1.9 %collective-permute-done.16 = bf16[32,1536]{1,0:T(8,128)(2,1)S(1)} collective-permute-done((bf16[32,1536]{1,0:T(8,128)(2,1)S(1)}, bf16[32,1536]{1,0:T(8,128)(2,1)S(1)}, u32[]{:S(2)}, u32[]{:S(2)}) %collective-permute-start.16) | collective-permute-done | bytes 98336 | tf_op jit(solution)/shard_map/ppermute | solution.py:125
  114.1 1.7 %collective-permute-start.21 = (bf16[32,1344]{1,0:T(8,128)(2,1)S(1)}, bf16[32,1344]{1,0:T(8,128)(2,1)S(1)}, u32[]{:S(2)}, u32[]{:S(2)}) collective-permute-start(bf16[32,1344]{1,0:T(8,128)(2,1)S(1)} %get-tuple-element.83), channel_id=1, source_target_pairs={{0,8},{1,9},{2,10},{3,11},{4,12},{5,13},{6,14},{7,15},{8,16},{9,17... | collective-permute-start | bytes 258056 | tf_op jit(solution)/shard_map/ppermute | solution.py:125
  115.8 1.1 collective-permute-start.22
  116.9 1.3 %collective-permute-start.23 = (bf16[32,1344]{1,0:T(8,128)(2,1)S(1)}, bf16[32,1344]{1,0:T(8,128)(2,1)S(1)}, u32[]{:S(2)}, u32[]{:S(2)}) collective-permute-start(bf16[32,1344]{1,0:T(8,128)(2,1)S(1)} %get-tuple-element.81), channel_id=1, source_target_pairs={{0,24},{1,25},{2,26},{3,27},{4,28},{5,29},{6,30},{7,31},{8,0},{9,1... | collective-permute-start | bytes 258056 | tf_op jit(solution)/shard_map/ppermute | solution.py:125
  118.3 4.7 %shard_map.115 = bf16[720,2880]{1,0:T(8,128)(2,1)} custom-call(bf16[576,720]{1,0:T(8,128)(2,1)S(1)} %pad_maximum_fusion.5.left_ref, bf16[576,2880]{1,0:T(8,128)(2,1)S(1)} %constant_dynamic-update-slice_fusion.4.right_ref), custom_call_target="tpu_custom_call" | custom-call | flops 2388787200 | bytes 8294400 | tf_op jit(solution)/shard_map/pallas_call | solution.py:80
  122.9 0.8 collective-permute-done.22
  124.1 0.8 fusion.42
  (101 shorter events, 7.1 us)
Async XLA Ops:
  0.6 29.1 %copy-start.2 = (bf16[32,2880]{1,0:T(8,128)(2,1)S(1)}, bf16[32,2880]{1,0:T(8,128)(2,1)}, u32[]{:S(2)}) copy-start(bf16[32,2880]{1,0:T(8,128)(2,1)} %param.12) | copy-start | bytes 552964
  25.4 21.7 %collective-permute-start = (bf16[72,2880]{1,0:T(8,128)(2,1)S(1)}, bf16[72,2880]{1,0:T(8,128)(2,1)S(1)}, u32[]{:S(2)}, u32[]{:S(2)}) collective-permute-start(bf16[72,2880]{1,0:T(8,128)(2,1)S(1)} %convolution_convert_fusion.1), channel_id=1, source_target_pairs={{0,4},{1,5},{2,6},{3,7},{4,0},{5,1},{6,2},{7,3},{8,12},{9,13},{10,... | collective-permute-start | bytes 1244168 | tf_op jit(solution)/shard_map/ppermute | solution.py:120
  26.9 20.2 %collective-permute-start.2 = (bf16[72,2880]{1,0:T(8,128)(2,1)S(1)}, bf16[72,2880]{1,0:T(8,128)(2,1)S(1)}, u32[]{:S(2)}, u32[]{:S(2)}) collective-permute-start(bf16[72,2880]{1,0:T(8,128)(2,1)S(1)} %convolution_convert_fusion.1), channel_id=1, source_target_pairs={{0,6},{1,7},{2,4},{3,5},{4,2},{5,3},{6,0},{7,1},{8,14},{9,15},{10,... | collective-permute-start | bytes 1244168 | tf_op jit(solution)/shard_map/ppermute | solution.py:120
  28.8 18.3 %collective-permute-start.1 = (bf16[72,2880]{1,0:T(8,128)(2,1)S(1)}, bf16[72,2880]{1,0:T(8,128)(2,1)S(1)}, u32[]{:S(2)}, u32[]{:S(2)}) collective-permute-start(bf16[72,2880]{1,0:T(8,128)(2,1)S(1)} %convolution_convert_fusion), channel_id=1, source_target_pairs={{0,2},{1,3},{2,0},{3,1},{4,6},{5,7},{6,4},{7,5},{8,10},{9,11},{10,... | collective-permute-start | bytes 1244168 | tf_op jit(solution)/shard_map/ppermute | solution.py:120
  29.6 21.9 %copy-start = (bf16[1,2880,720]{1,2,0:T(8,128)(2,1)S(1)}, bf16[1,2880,720]{1,2,0:T(8,128)(2,1)}, u32[]{:S(2)}) copy-start(bf16[1,2880,720]{1,2,0:T(8,128)(2,1)} %param.13) | copy-start | bytes 12441604
  47.2 4.8 %collective-permute-start.6 = (bf16[144,2880]{1,0:T(8,128)(2,1)S(1)}, bf16[144,2880]{1,0:T(8,128)(2,1)S(1)}, u32[]{:S(2)}, u32[]{:S(2)}) collective-permute-start(bf16[144,2880]{1,0:T(8,128)(2,1)S(1)} %pad_maximum_fusion.6), channel_id=1, source_target_pairs={{0,1},{1,0},{2,3},{3,2},{4,5},{5,4},{6,7},{7,6},{8,9},{9,8},{10,11... | collective-permute-start | bytes 2488328 | tf_op jit(solution)/shard_map/ppermute | solution.py:120
  47.6 21.3 %collective-permute-start.3 = (bf16[72,2880]{1,0:T(8,128)(2,1)S(1)}, bf16[72,2880]{1,0:T(8,128)(2,1)S(1)}, u32[]{:S(2)}, u32[]{:S(2)}) collective-permute-start(bf16[72,2880]{1,0:T(8,128)(2,1)S(1)} %fusion.13), channel_id=1, source_target_pairs={{0,4},{1,5},{2,6},{3,7},{4,0},{5,1},{6,2},{7,3},{8,12},{9,13},{10,... | collective-permute-start | bytes 1244168 | tf_op jit(solution)/shard_map/ppermute | solution.py:120
  49.1 19.8 %collective-permute-start.5 = (bf16[72,2880]{1,0:T(8,128)(2,1)S(1)}, bf16[72,2880]{1,0:T(8,128)(2,1)S(1)}, u32[]{:S(2)}, u32[]{:S(2)}) collective-permute-start(bf16[72,2880]{1,0:T(8,128)(2,1)S(1)} %fusion.13), channel_id=1, source_target_pairs={{0,6},{1,7},{2,4},{3,5},{4,2},{5,3},{6,0},{7,1},{8,14},{9,15},{10,... | collective-permute-start | bytes 1244168 | tf_op jit(solution)/shard_map/ppermute | solution.py:120
  50.9 19.3 %collective-permute-start.4 = (bf16[72,2880]{1,0:T(8,128)(2,1)S(1)}, bf16[72,2880]{1,0:T(8,128)(2,1)S(1)}, u32[]{:S(2)}, u32[]{:S(2)}) collective-permute-start(bf16[72,2880]{1,0:T(8,128)(2,1)S(1)} %get-tuple-element.92), channel_id=1, source_target_pairs={{0,2},{1,3},{2,0},{3,1},{4,6},{5,7},{6,4},{7,5},{8,10},{9,11},{10,... | collective-permute-start | bytes 1244168 | tf_op jit(solution)/shard_map/ppermute | solution.py:120
  51.9 3.9 %collective-permute-start.7 = (bf16[144,2880]{1,0:T(8,128)(2,1)S(1)}, bf16[144,2880]{1,0:T(8,128)(2,1)S(1)}, u32[]{:S(2)}, u32[]{:S(2)}) collective-permute-start(bf16[144,2880]{1,0:T(8,128)(2,1)S(1)} %pad_maximum_fusion.7), channel_id=1, source_target_pairs={{0,1},{1,0},{2,3},{3,2},{4,5},{5,4},{6,7},{7,6},{8,9},{9,8},{10,11... | collective-permute-start | bytes 2488328 | tf_op jit(solution)/shard_map/ppermute | solution.py:120
  52.0 2.2 %slice-start.2 = ((s8[4239360]{0:T(1024)(128)(4,1)}), s8[4194304]{0:T(1024)(128)(4,1)S(1)}, s32[]{:S(2)}) async-start(s8[4239360]{0:T(1024)(128)(4,1)} %bitcast.81), calls=%async_computation.2 | async-start | bytes 8388608
  52.1 2.0 %slice-start.3 = ((s8[4239360]{0:T(1024)(128)(4,1)}), s8[45056]{0:T(1024)(128)(4,1)S(1)}, s32[]{:S(2)}) async-start(s8[4239360]{0:T(1024)(128)(4,1)} %bitcast.81), calls=%async_computation.3 | async-start | bytes 90112
  56.0 15.0 %slice-start = ((s8[4239360]{0:T(1024)(128)(4,1)}), s8[4194304]{0:T(1024)(128)(4,1)S(1)}, s32[]{:S(2)}) async-start(s8[4239360]{0:T(1024)(128)(4,1)} %bitcast.74), calls=%async_computation | async-start | bytes 8388608
  57.6 13.4 %slice-start.1 = ((s8[4239360]{0:T(1024)(128)(4,1)}), s8[45056]{0:T(1024)(128)(4,1)S(1)}, s32[]{:S(2)}) async-start(s8[4239360]{0:T(1024)(128)(4,1)} %bitcast.74), calls=%async_computation.1 | async-start | bytes 90112
  70.2 2.4 %collective-permute-start.8 = (bf16[144,2880]{1,0:T(8,128)(2,1)S(1)}, bf16[144,2880]{1,0:T(8,128)(2,1)S(1)}, u32[]{:S(2)}, u32[]{:S(2)}) collective-permute-start(bf16[144,2880]{1,0:T(8,128)(2,1)S(1)} %pad_maximum_fusion.8), channel_id=1, source_target_pairs={{0,1},{1,0},{2,3},{3,2},{4,5},{5,4},{6,7},{7,6},{8,9},{9,8},{10,11... | collective-permute-start | bytes 2488328 | tf_op jit(solution)/shard_map/ppermute | solution.py:120
  70.4 7.6 %collective-permute-start.10 = (bf16[144,2880]{1,0:T(8,128)(2,1)S(1)}, bf16[144,2880]{1,0:T(8,128)(2,1)S(1)}, u32[]{:S(2)}, u32[]{:S(2)}) collective-permute-start(bf16[144,2880]{1,0:T(8,128)(2,1)S(1)} %pad_maximum_fusion.9), channel_id=1, source_target_pairs={{0,1},{1,0},{2,3},{3,2},{4,5},{5,4},{6,7},{7,6},{8,9},{9,8},{10,11... | collective-permute-start | bytes 2488328 | tf_op jit(solution)/shard_map/ppermute | solution.py:120
  80.1 2.4 %collective-permute-start.9 = (bf16[144,2880]{1,0:T(8,128)(2,1)S(1)}, bf16[144,2880]{1,0:T(8,128)(2,1)S(1)}, u32[]{:S(2)}, u32[]{:S(2)}) collective-permute-start(bf16[144,2880]{1,0:T(8,128)(2,1)S(1)} %slice.112), channel_id=1, source_target_pairs={{0,1},{1,0},{2,3},{3,2},{4,5},{5,4},{6,7},{7,6},{8,9},{9,8},{10,11... | collective-permute-start | bytes 2488328 | tf_op jit(solution)/shard_map/ppermute | solution.py:120
  84.5 3.7 %collective-permute-start.11 = (bf16[144,1536]{1,0:T(8,128)(2,1)S(1)}, bf16[144,1536]{1,0:T(8,128)(2,1)S(1)}, u32[]{:S(2)}, u32[]{:S(2)}) collective-permute-start(bf16[144,1536]{1,0:T(8,128)(2,1)S(1)} %slice.116), channel_id=1, source_target_pairs={{0,1},{1,0},{2,3},{3,2},{4,5},{5,4},{6,7},{7,6},{8,9},{9,8},{10,11... | collective-permute-start | bytes 1327112 | tf_op jit(solution)/shard_map/ppermute | solution.py:120
  85.6 16.9 %collective-permute-start.14 = (bf16[72,2880]{1,0:T(8,128)(2,1)S(1)}, bf16[72,2880]{1,0:T(8,128)(2,1)S(1)}, u32[]{:S(2)}, u32[]{:S(2)}) collective-permute-start(bf16[72,2880]{1,0:T(8,128)(2,1)S(1)} %slice.183), channel_id=1, source_target_pairs={{0,4},{1,5},{2,6},{3,7},{4,0},{5,1},{6,2},{7,3},{8,12},{9,13},{10,... | collective-permute-start | bytes 1244168 | tf_op jit(solution)/shard_map/ppermute | solution.py:120
  88.1 7.3 %collective-permute-start.18 = (bf16[144,1344]{1,0:T(8,128)(2,1)S(1)}, bf16[144,1344]{1,0:T(8,128)(2,1)S(1)}, u32[]{:S(2)}, u32[]{:S(2)}) collective-permute-start(bf16[144,1344]{1,0:T(8,128)(2,1)S(1)} %slice.123), channel_id=1, source_target_pairs={{0,1},{1,0},{2,3},{3,2},{4,5},{5,4},{6,7},{7,6},{8,9},{9,8},{10,11... | collective-permute-start | bytes 1161224 | tf_op jit(solution)/shard_map/ppermute | solution.py:120
  88.4 10.1 %collective-permute-start.12 = (bf16[72,1536]{1,0:T(8,128)(2,1)S(1)}, bf16[72,1536]{1,0:T(8,128)(2,1)S(1)}, u32[]{:S(2)}, u32[]{:S(2)}) collective-permute-start(bf16[72,1536]{1,0:T(8,128)(2,1)S(1)} %get-tuple-element.85), channel_id=1, source_target_pairs={{0,2},{1,3},{2,0},{3,1},{4,6},{5,7},{6,4},{7,5},{8,10},{9,11},{10,... | collective-permute-start | bytes 663560 | tf_op jit(solution)/shard_map/ppermute | solution.py:120
  89.9 11.5 %collective-permute-start.13 = (bf16[72,1536]{1,0:T(8,128)(2,1)S(1)}, bf16[72,1536]{1,0:T(8,128)(2,1)S(1)}, u32[]{:S(2)}, u32[]{:S(2)}) collective-permute-start(bf16[72,1536]{1,0:T(8,128)(2,1)S(1)} %get-tuple-element.84), channel_id=1, source_target_pairs={{0,6},{1,7},{2,4},{3,5},{4,2},{5,3},{6,0},{7,1},{8,14},{9,15},{10,... | collective-permute-start | bytes 663560 | tf_op jit(solution)/shard_map/ppermute | solution.py:120
  95.5 17.8 %collective-permute-start.19 = (bf16[72,1344]{1,0:T(8,128)(2,1)S(1)}, bf16[72,1344]{1,0:T(8,128)(2,1)S(1)}, u32[]{:S(2)}, u32[]{:S(2)}) collective-permute-start(bf16[72,1344]{1,0:T(8,128)(2,1)S(1)} %get-tuple-element.87), channel_id=1, source_target_pairs={{0,2},{1,3},{2,0},{3,1},{4,6},{5,7},{6,4},{7,5},{8,10},{9,11},{10,... | collective-permute-start | bytes 580616 | tf_op jit(solution)/shard_map/ppermute | solution.py:120
  97.0 16.3 %collective-permute-start.20 = (bf16[72,1344]{1,0:T(8,128)(2,1)S(1)}, bf16[72,1344]{1,0:T(8,128)(2,1)S(1)}, u32[]{:S(2)}, u32[]{:S(2)}) collective-permute-start(bf16[72,1344]{1,0:T(8,128)(2,1)S(1)} %get-tuple-element.86), channel_id=1, source_target_pairs={{0,6},{1,7},{2,4},{3,5},{4,2},{5,3},{6,0},{7,1},{8,14},{9,15},{10,... | collective-permute-start | bytes 580616 | tf_op jit(solution)/shard_map/ppermute | solution.py:120
  102.8 8.6 %collective-permute-start.15 = (bf16[32,1536]{1,0:T(8,128)(2,1)S(1)}, bf16[32,1536]{1,0:T(8,128)(2,1)S(1)}, u32[]{:S(2)}, u32[]{:S(2)}) collective-permute-start(bf16[32,1536]{1,0:T(8,128)(2,1)S(1)} %get-tuple-element.80), channel_id=1, source_target_pairs={{0,8},{1,9},{2,10},{3,11},{4,12},{5,13},{6,14},{7,15},{8,16},{9,17... | collective-permute-start | bytes 294920 | tf_op jit(solution)/shard_map/ppermute | solution.py:125
  102.9 10.4 %collective-permute-start.16 = (bf16[32,1536]{1,0:T(8,128)(2,1)S(1)}, bf16[32,1536]{1,0:T(8,128)(2,1)S(1)}, u32[]{:S(2)}, u32[]{:S(2)}) collective-permute-start(bf16[32,1536]{1,0:T(8,128)(2,1)S(1)} %get-tuple-element.79), channel_id=1, source_target_pairs={{0,16},{1,17},{2,18},{3,19},{4,20},{5,21},{6,22},{7,23},{8,24},{9,... | collective-permute-start | bytes 294920 | tf_op jit(solution)/shard_map/ppermute | solution.py:125
  104.9 8.4 %collective-permute-start.17 = (bf16[32,1536]{1,0:T(8,128)(2,1)S(1)}, bf16[32,1536]{1,0:T(8,128)(2,1)S(1)}, u32[]{:S(2)}, u32[]{:S(2)}) collective-permute-start(bf16[32,1536]{1,0:T(8,128)(2,1)S(1)} %get-tuple-element.78), channel_id=1, source_target_pairs={{0,24},{1,25},{2,26},{3,27},{4,28},{5,29},{6,30},{7,31},{8,0},{9,1... | collective-permute-start | bytes 294920 | tf_op jit(solution)/shard_map/ppermute | solution.py:125
  114.1 8.9 %collective-permute-start.21 = (bf16[32,1344]{1,0:T(8,128)(2,1)S(1)}, bf16[32,1344]{1,0:T(8,128)(2,1)S(1)}, u32[]{:S(2)}, u32[]{:S(2)}) collective-permute-start(bf16[32,1344]{1,0:T(8,128)(2,1)S(1)} %get-tuple-element.83), channel_id=1, source_target_pairs={{0,8},{1,9},{2,10},{3,11},{4,12},{5,13},{6,14},{7,15},{8,16},{9,17... | collective-permute-start | bytes 258056 | tf_op jit(solution)/shard_map/ppermute | solution.py:125
  115.8 8.0 %collective-permute-start.22 = (bf16[32,1344]{1,0:T(8,128)(2,1)S(1)}, bf16[32,1344]{1,0:T(8,128)(2,1)S(1)}, u32[]{:S(2)}, u32[]{:S(2)}) collective-permute-start(bf16[32,1344]{1,0:T(8,128)(2,1)S(1)} %get-tuple-element.82), channel_id=1, source_target_pairs={{0,16},{1,17},{2,18},{3,19},{4,20},{5,21},{6,22},{7,23},{8,24},{9,... | collective-permute-start | bytes 258056 | tf_op jit(solution)/shard_map/ppermute | solution.py:125
  116.9 6.9 %copy-start.1 = (bf16[32,2880]{1,0:T(8,128)(2,1)S(1)}, bf16[32,2880]{1,0:T(8,128)(2,1)}, u32[]{:S(2)}) copy-start(bf16[32,2880]{1,0:T(8,128)(2,1)} %param.8) | copy-start | bytes 552964
  116.9 7.0 %copy-start.3 = (f32[2880]{0:T(1024)S(1)}, f32[2880]{0:T(1024)}, u32[]{:S(2)}) copy-start(f32[2880]{0:T(1024)} %param.9) | copy-start | bytes 34564
  116.9 6.9 %collective-permute-start.23 = (bf16[32,1344]{1,0:T(8,128)(2,1)S(1)}, bf16[32,1344]{1,0:T(8,128)(2,1)S(1)}, u32[]{:S(2)}, u32[]{:S(2)}) collective-permute-start(bf16[32,1344]{1,0:T(8,128)(2,1)S(1)} %get-tuple-element.81), channel_id=1, source_target_pairs={{0,24},{1,25},{2,26},{3,27},{4,28},{5,29},{6,30},{7,31},{8,0},{9,1... | collective-permute-start | bytes 258056 | tf_op jit(solution)/shard_map/ppermute | solution.py:125

commit v5 on v2

--- a/solution.py
+++ b/solution.py
@@ -225,14 +225,15 @@
     chip_sum = chip_rows[:kept].astype(jnp.float32) + flip(chip_rows[kept:], CORE).astype(
         jnp.float32
     )
-    side_sum = flip(chip_sum[slots:].astype(jnp.bfloat16), SIDE)
+    side_ready = chip_sum[slots:].astype(jnp.bfloat16)
+    side_sum = flip(side_ready, SIDE)
 
     pair_core_dy = flip(pair_dy, CORE)
-    across_dy = behind(across_dy, (chip_rows, pair_forward))
+    across_dy = behind(across_dy, (chip_sum, pair_forward))
     pair_dy = jnp.concatenate([pair_dy, across_dy, pair_core_dy, flip(across_dy, CORE)], axis=0)
     pair_hid, pair_d_gate, pair_d_up = hidden(*pair_forward, pair_dy)
 
-    cut = -(-width // 2 // 256) * 256
+    cut = width // 2 // 128 * 128
     spans = [(0, cut), (cut, width)]
 
     def core_sum(rows, from_core):
@@ -242,11 +243,11 @@
     def to_pair(rows):
         return flip(rows[:slots], PAIR), flip(rows[slots:], PAIR | SIDE)
 
-    rows_first = row_gradient(*behind((pair_d_gate, pair_d_up), chip_sum), *spans[0])
+    rows_first = row_gradient(*behind((pair_d_gate, pair_d_up), side_ready), *spans[0])
     core_first = flip(rows_first[kept:], CORE)
     rows_second = row_gradient(*behind((pair_d_gate, pair_d_up), rows_first), *spans[1])
-    core_second = flip(rows_second[kept:], CORE)
     sum_first = core_sum(rows_first, core_first)
+    core_second = flip(behind(rows_second[kept:], sum_first), CORE)
     sent_first = to_pair(sum_first)
 
     x_in = jnp.concatenate([chip_x, pair_x], axis=0)
@@ -284,12 +285,13 @@
     grad_gate = weight_gradient(d_gate, x_in, (sum_first, rows_second, chip_sum))
     sum_second = core_sum(*behind((rows_second, core_second), grad_gate))
     sent_second = to_pair(sum_second)
-    d_column = to_column(spans[0], *behind(sent_first, grad_gate))
+    d_column = to_column(spans[0], *behind(sent_first, (grad_gate, sum_second)))
     first_half = to_tokens(d_column)
     grad_up = weight_gradient(d_up, x_in, d_column)
     first_half = added(*behind(first_half, grad_up))
-    second_half = to_tokens(to_column(spans[1], *behind(sent_second, first_half)))
-    grad_down = weight_gradient(hid, dy_e, first_half)
+    d_column = to_column(spans[1], *behind(sent_second, first_half))
+    second_half = to_tokens(d_column)
+    grad_down = weight_gradient(hid, dy_e, d_column)
     second_half = added(*behind(second_half, grad_down))
     grads = [grad_gate.T[None], grad_up.T[None], grad_down[None]]
     d_normed = jnp.concatenate([first_half, second_half], axis=1)

time: 117 us -> 114 us (0.974)
  waiting for transfers between devices: 10.1 us -> 8.08 us
    ppermute x19, waiting for transfers between devices: 7.31 us -> 6.07 us  [flip(): lax.ppermute(row_major(value), 'sq', [(i, i ^ bit) for i in range(devices)])]
  transfers between devices with their start and end apart: 25 -> 25, of which waited for: 6 -> 6; matrix products, arithmetic and copies ran while one was open for 16% -> 18% of each run, Pallas kernels for 13% -> 13%
where the time goes in v5:
time: 114 us
  blocking collectives  38.3 us (34%)
  starting transfers between devices  22.9 us (20%)
  matrix products  19.6 us (17%)
  Pallas kernels  14.9 us (13%)
  waiting for transfers between devices  8.08 us (7%)
  other arithmetic  5.57 us (5%)
  local copies, waits for them, and re-layouts  3.54 us (3%)
  between operations  1.38 us (1%)
    all_gather x2, blocking collectives, gather_column(): lax.all_gather(block, 'sq', axis=0, tiled=True, axis_index_groups=lines)  38.3 us
    ppermute x19, starting transfers between devices, flip(): lax.ppermute(row_major(value), 'sq', [(i, i ^ bit) for i in range(devices)])  14.9 us
    pallas_call x3, Pallas kernels, weight_product(): pl.pallas_call(product_kernel, in_specs=[pl.BlockSpec(memory_space=pltpu....  14 us
    dot_general x8, matrix products, contract_cols(): lax.dot_general(left, right, (((1,), (1,)), ((), ())), preferred_element_...  10.6 us
    ppermute x6, starting transfers between devices, shift(): return lax.ppermute(row_major(value), 'sq', pairs)  8.07 us
    ppermute x19, waiting for transfers between devices, flip(): lax.ppermute(row_major(value), 'sq', [(i, i ^ bit) for i in range(devices)])  6.07 us
    dot_general x2, matrix products, forward(): gate = jnp.dot(x_in, gate_w, preferred_element_type=jnp.float32)  3.3 us
    dot_general x2, matrix products, forward(): up = jnp.dot(x_in, up_w, preferred_element_type=jnp.float32)  3.29 us
  transfers between devices with their start and end apart: 25, of which 6 were waited for; matrix products, arithmetic and copies ran while one was open for 18% of the time, Pallas kernels for 13%

profile of v5, /device:TPU:0, one launch (start us, length us, event | category | flops | bytes accessed | tf_op | source)
XLA Modules:
  0.0 114.3 jit_solution(6088847898782068337)
XLA Ops:
  0.6 0.7 select_reduce_fusion.4
  1.5 1.1 fusion.45
  2.6 1.0 fusion.40
  3.8 20.9 %all_gather.6 = bf16[128,2904]{1,0:T(8,128)(2,1)S(1)} all-gather(bf16[32,2904]{1,0:T(8,128)(2,1)S(1)} %concatenate.47), channel_id=1, replica_groups={{0,8,16,24},{1,9,17,25},{2,10,18,26},{3,11,19,27},{4,12,20,28},{5,13,21..., dimensions={0}, use_global_device_ids=true | all-gather | bytes 929280 | tf_op jit(solution)/shard_map/all_gather | solution.py:141
  25.4 1.6 %collective-permute-start = (bf16[72,2880]{1,0:T(8,128)(2,1)S(1)}, bf16[72,2880]{1,0:T(8,128)(2,1)S(1)}, u32[]{:S(2)}, u32[]{:S(2)}) collective-permute-start(bf16[72,2880]{1,0:T(8,128)(2,1)S(1)} %convolution_convert_fusion.1), channel_id=1, source_target_pairs={{0,4},{1,5},{2,6},{3,7},{4,0},{5,1},{6,2},{7,3},{8,12},{9,13},{10,... | collective-permute-start | bytes 1244168 | tf_op jit(solution)/shard_map/ppermute | solution.py:120
  27.0 1.4 %collective-permute-start.2 = (bf16[72,2880]{1,0:T(8,128)(2,1)S(1)}, bf16[72,2880]{1,0:T(8,128)(2,1)S(1)}, u32[]{:S(2)}, u32[]{:S(2)}) collective-permute-start(bf16[72,2880]{1,0:T(8,128)(2,1)S(1)} %convolution_convert_fusion.1), channel_id=1, source_target_pairs={{0,6},{1,7},{2,4},{3,5},{4,2},{5,3},{6,0},{7,1},{8,14},{9,15},{10,... | collective-permute-start | bytes 1244168 | tf_op jit(solution)/shard_map/ppermute | solution.py:120
  28.8 0.6 collective-permute-start.1
  29.7 17.4 %all_gather.7 = bf16[128,2880]{1,0:T(8,128)(2,1)S(1)} all-gather(bf16[32,2880]{1,0:T(8,128)(2,1)S(1)} %copy-done.2), channel_id=1, replica_groups={{0,8,16,24},{1,9,17,25},{2,10,18,26},{3,11,19,27},{4,12,20,28},{5,13,21..., dimensions={0}, use_global_device_ids=true | all-gather | bytes 921600 | tf_op jit(solution)/shard_map/all_gather | solution.py:141
  47.7 1.6 %collective-permute-start.3 = (bf16[72,2880]{1,0:T(8,128)(2,1)S(1)}, bf16[72,2880]{1,0:T(8,128)(2,1)S(1)}, u32[]{:S(2)}, u32[]{:S(2)}) collective-permute-start(bf16[72,2880]{1,0:T(8,128)(2,1)S(1)} %fusion.13), channel_id=1, source_target_pairs={{0,4},{1,5},{2,6},{3,7},{4,0},{5,1},{6,2},{7,3},{8,12},{9,13},{10,... | collective-permute-start | bytes 1244168 | tf_op jit(solution)/shard_map/ppermute | solution.py:120
  49.3 1.5 %collective-permute-start.4 = (bf16[72,2880]{1,0:T(8,128)(2,1)S(1)}, bf16[72,2880]{1,0:T(8,128)(2,1)S(1)}, u32[]{:S(2)}, u32[]{:S(2)}) collective-permute-start(bf16[72,2880]{1,0:T(8,128)(2,1)S(1)} %get-tuple-element.104), channel_id=1, source_target_pairs={{0,2},{1,3},{2,0},{3,1},{4,6},{5,7},{6,4},{7,5},{8,10},{9,11},{10,... | collective-permute-start | bytes 1244168 | tf_op jit(solution)/shard_map/ppermute | solution.py:120
  51.0 0.4 shard_map.111
  51.4 1.7 %slice-done = s8[4194304]{0:T(1024)(128)(4,1)S(1)} async-done(((s8[4239360]{0:T(1024)(128)(4,1)}), s8[4194304]{0:T(1024)(128)(4,1)S(1)}, s32[]{:S(2)}) %slice-start) | async-done | bytes 4194328
  53.1 0.5 shard_map.112
  53.6 0.6 collective-permute-start.9
  54.6 1.6 %fusion.93 = f32[288,720]{1,0:T(8,128)S(1)} fusion(bf16[288,2880]{1,0:T(8,128)(2,1)S(1)} %get-tuple-element.85, bf16[720,2880]{1,0:T(8,128)(2,1)S(1)} %shard_map.111), kind=kOutput, calls=%fused_computation.163 | convolution fusion | flops 1194393600 | bytes 6635520 | tf_op jit(solution)/shard_map/dot_general | solution.py:195
  56.6 1.6 %fusion.4 = f32[288,720]{1,0:T(8,128)S(1)} fusion(bf16[288,2880]{1,0:T(8,128)(2,1)S(1)} %get-tuple-element.85, bf16[1,2880,720]{1,2,0:T(8,128)(2,1)S(1)} %bitcast.81), kind=kOutput, calls=%fused_computation.4 | convolution fusion | flops 1194393600 | bytes 6635520 | tf_op jit(solution)/shard_map/dot_general | solution.py:196
  58.2 0.6 collective-permute-start.8
  59.2 1.6 %fusion = f32[288,720]{1,0:T(8,128)S(1)} fusion(bf16[288,2880]{1,0:T(8,128)(2,1)S(1)} %pad_maximum_fusion.1, bf16[1,2880,720]{1,2,0:T(8,128)(2,1)S(1)} %bitcast.81), kind=kOutput, calls=%fused_computation | convolution fusion | flops 1194393600 | bytes 6635520 | tf_op jit(solution)/shard_map/dot_general | solution.py:196
  60.8 0.6 collective-permute-start.10
  61.6 1.7 %fusion.95 = f32[288,720]{1,0:T(8,128)S(1)} fusion(bf16[288,2880]{1,0:T(8,128)(2,1)S(1)} %pad_maximum_fusion.1, bf16[720,2880]{1,0:T(8,128)(2,1)S(1)} %shard_map.111), kind=kOutput, calls=%fused_computation.165 | convolution fusion | flops 1194393600 | bytes 6635520 | tf_op jit(solution)/shard_map/dot_general | solution.py:195
  63.2 1.9 %multiply_convert_fusion.1 = (bf16[288,720]{1,0:T(8,128)(2,1)S(1)}, bf16[288,720]{1,0:T(8,128)(2,1)S(1)}, bf16[288,720]{1,0:T(8,128)(2,1)S(1)}) fusion(f32[288,720]{1,0:T(8,128)S(1)} %fusion.4, f32[288,720]{1,0:T(8,128)S(1)} %fusion.93, bf16[720,2880]{1,0:T(8,128)(2,1)S(1)} %shard_map.112, bf16[144,2880]{1,0:T(8,128)(2,1)S(1)} %collective-permute-done.6, ...), kind=kOutput, calls=%fused_computation.43 | convolution fusion | flops 1202895360 | bytes 8709120 | tf_op jit(solution)/shard_map/dot_general | solution.py:25
  65.1 1.5 %fusion.94 = f32[288,2880]{1,0:T(8,128)S(1)} fusion(bf16[288,720]{1,0:T(8,128)(2,1)S(1)} %get-tuple-element.79, bf16[720,2880]{1,0:T(8,128)(2,1)S(1)} %shard_map.111), kind=kOutput, calls=%fused_computation.164 | convolution fusion | flops 1194393600 | bytes 7879680 | tf_op jit(solution)/shard_map/dot_general | solution.py:25
  66.7 1.6 %fusion.9 = bf16[288,2880]{1,0:T(8,128)(2,1)S(1)} fusion(f32[288,2880]{1,0:T(8,128)S(1)} %fusion.94, bf16[288,720]{1,0:T(8,128)(2,1)S(1)} %get-tuple-element.80, bf16[1,2880,720]{1,2,0:T(8,128)(2,1)S(1)} %bitcast.81), kind=kOutput, calls=%fused_computation.7 | convolution fusion | flops 1196052480 | bytes 9538560 | tf_op jit(solution)/shard_map/dot_general | solution.py:25
  68.6 2.2 %collective-permute-done.7 = bf16[144,2880]{1,0:T(8,128)(2,1)S(1)} collective-permute-done((bf16[144,2880]{1,0:T(8,128)(2,1)S(1)}, bf16[144,2880]{1,0:T(8,128)(2,1)S(1)}, u32[]{:S(2)}, u32[]{:S(2)}) %collective-permute-start.7) | collective-permute-done | bytes 829472 | tf_op jit(solution)/shard_map/ppermute | solution.py:120
  71.2 0.5 collective-permute-start.16
  71.8 1.0 collective-permute-done.11
  72.9 2.1 %multiply_convert_fusion = (bf16[288,720]{1,0:T(8,128)(2,1)S(1)}, bf16[288,720]{1,0:T(8,128)(2,1)S(1)}, bf16[288,720]{1,0:T(8,128)(2,1)S(1)}) fusion(f32[288,720]{1,0:T(8,128)S(1)} %fusion, f32[288,720]{1,0:T(8,128)S(1)} %fusion.95, bf16[720,2880]{1,0:T(8,128)(2,1)S(1)} %shard_map.112, bf16[72,2880]{1,0:T(8,128)(2,1)S(1)} %collective-permute-done.11, ...), kind=kOutput, calls=%fused_computation.42 | convolution fusion | flops 1204554240 | bytes 8709120 | tf_op jit(solution)/shard_map/dot_general | solution.py:25
  75.0 0.9 fusion.20
  75.8 0.9 fusion.15
  76.9 0.9 fusion.16
  78.0 0.9 fusion.14
  79.0 0.6 collective-permute-done.12
  80.0 1.5 %collective-permute-start.13 = (bf16[72,1408]{1,0:T(8,128)(2,1)S(1)}, bf16[72,1408]{1,0:T(8,128)(2,1)S(1)}, u32[]{:S(2)}, u32[]{:S(2)}) collective-permute-start(bf16[72,1408]{1,0:T(8,128)(2,1)S(1)} %get-tuple-element.99), channel_id=1, source_target_pairs={{0,2},{1,3},{2,0},{3,1},{4,6},{5,7},{6,4},{7,5},{8,10},{9,11},{10,... | collective-permute-start | bytes 608264 | tf_op jit(solution)/shard_map/ppermute | solution.py:120
  81.5 0.5 collective-permute-start.14
  82.0 4.7 %shard_map.113 = bf16[720,2880]{1,0:T(8,128)(2,1)} custom-call(bf16[576,720]{1,0:T(8,128)(2,1)S(1)} %pad_maximum_fusion.2.left_ref, bf16[576,2880]{1,0:T(8,128)(2,1)S(1)} %constant_dynamic-update-slice_fusion.3.right_ref), custom_call_target="tpu_custom_call" | custom-call | flops 2388787200 | bytes 8294400 | tf_op jit(solution)/shard_map/pallas_call | solution.py:80
  86.8 1.5 %collective-permute-start.20 = (bf16[72,1472]{1,0:T(8,128)(2,1)S(1)}, bf16[72,1472]{1,0:T(8,128)(2,1)S(1)}, u32[]{:S(2)}, u32[]{:S(2)}) collective-permute-start(bf16[72,1472]{1,0:T(8,128)(2,1)S(1)} %get-tuple-element.93), channel_id=1, source_target_pairs={{0,2},{1,3},{2,0},{3,1},{4,6},{5,7},{6,4},{7,5},{8,10},{9,11},{10,... | collective-permute-start | bytes 635912 | tf_op jit(solution)/shard_map/ppermute | solution.py:120
  88.4 1.5 %collective-permute-start.21 = (bf16[72,1472]{1,0:T(8,128)(2,1)S(1)}, bf16[72,1472]{1,0:T(8,128)(2,1)S(1)}, u32[]{:S(2)}, u32[]{:S(2)}) collective-permute-start(bf16[72,1472]{1,0:T(8,128)(2,1)S(1)} %get-tuple-element.92), channel_id=1, source_target_pairs={{0,6},{1,7},{2,4},{3,5},{4,2},{5,3},{6,0},{7,1},{8,14},{9,15},{10,... | collective-permute-start | bytes 635912 | tf_op jit(solution)/shard_map/ppermute | solution.py:120
  89.9 2.3 %collective-permute-done.14 = bf16[72,1408]{1,0:T(8,128)(2,1)S(1)} collective-permute-done((bf16[72,1408]{1,0:T(8,128)(2,1)S(1)}, bf16[72,1408]{1,0:T(8,128)(2,1)S(1)}, u32[]{:S(2)}, u32[]{:S(2)}) %collective-permute-start.14) | collective-permute-done | bytes 202784 | tf_op jit(solution)/shard_map/ppermute | solution.py:120
  93.0 2.1 %collective-permute-start.18 = (bf16[32,1408]{1,0:T(8,128)(2,1)S(1)}, bf16[32,1408]{1,0:T(8,128)(2,1)S(1)}, u32[]{:S(2)}, u32[]{:S(2)}) collective-permute-start(bf16[32,1408]{1,0:T(8,128)(2,1)S(1)} %get-tuple-element.90), channel_id=1, source_target_pairs={{0,16},{1,17},{2,18},{3,19},{4,20},{5,21},{6,22},{7,23},{8,24},{9,... | collective-permute-start | bytes 270344 | tf_op jit(solution)/shard_map/ppermute | solution.py:125
  95.0 1.8 %collective-permute-start.19 = (bf16[32,1408]{1,0:T(8,128)(2,1)S(1)}, bf16[32,1408]{1,0:T(8,128)(2,1)S(1)}, u32[]{:S(2)}, u32[]{:S(2)}) collective-permute-start(bf16[32,1408]{1,0:T(8,128)(2,1)S(1)} %get-tuple-element.89), channel_id=1, source_target_pairs={{0,24},{1,25},{2,26},{3,27},{4,28},{5,29},{6,30},{7,31},{8,0},{9,1... | collective-permute-start | bytes 270344 | tf_op jit(solution)/shard_map/ppermute | solution.py:125
  96.8 4.7 %shard_map.114 = bf16[720,2880]{1,0:T(8,128)(2,1)} custom-call(bf16[576,720]{1,0:T(8,128)(2,1)S(1)} %pad_maximum_fusion.3.left_ref, bf16[576,2880]{1,0:T(8,128)(2,1)S(1)} %constant_dynamic-update-slice_fusion.3.right_ref), custom_call_target="tpu_custom_call" | custom-call | flops 2388787200 | bytes 8294400 | tf_op jit(solution)/shard_map/pallas_call | solution.py:80
  101.5 0.8 collective-permute-done.18
  103.1 1.6 %collective-permute-start.22 = (bf16[32,1472]{1,0:T(8,128)(2,1)S(1)}, bf16[32,1472]{1,0:T(8,128)(2,1)S(1)}, u32[]{:S(2)}, u32[]{:S(2)}) collective-permute-start(bf16[32,1472]{1,0:T(8,128)(2,1)S(1)} %get-tuple-element.88), channel_id=1, source_target_pairs={{0,8},{1,9},{2,10},{3,11},{4,12},{5,13},{6,14},{7,15},{8,16},{9,17... | collective-permute-start | bytes 282632 | tf_op jit(solution)/shard_map/ppermute | solution.py:125
  104.7 1.6 %collective-permute-start.23 = (bf16[32,1472]{1,0:T(8,128)(2,1)S(1)}, bf16[32,1472]{1,0:T(8,128)(2,1)S(1)}, u32[]{:S(2)}, u32[]{:S(2)}) collective-permute-start(bf16[32,1472]{1,0:T(8,128)(2,1)S(1)} %get-tuple-element.87), channel_id=1, source_target_pairs={{0,16},{1,17},{2,18},{3,19},{4,20},{5,21},{6,22},{7,23},{8,24},{9,... | collective-permute-start | bytes 282632 | tf_op jit(solution)/shard_map/ppermute | solution.py:125
  106.3 1.0 collective-permute-start.24
  107.3 4.7 %shard_map.115 = bf16[720,2880]{1,0:T(8,128)(2,1)} custom-call(bf16[576,720]{1,0:T(8,128)(2,1)S(1)} %pad_maximum_fusion.4.left_ref, bf16[576,2880]{1,0:T(8,128)(2,1)S(1)} %constant_dynamic-update-slice_fusion.9.right_ref), custom_call_target="tpu_custom_call" | custom-call | flops 2388787200 | bytes 8294400 | tf_op jit(solution)/shard_map/pallas_call | solution.py:80
  112.0 1.2 %collective-permute-done.23 = bf16[32,1472]{1,0:T(8,128)(2,1)S(1)} collective-permute-done((bf16[32,1472]{1,0:T(8,128)(2,1)S(1)}, bf16[32,1472]{1,0:T(8,128)(2,1)S(1)}, u32[]{:S(2)}, u32[]{:S(2)}) %collective-permute-start.23) | collective-permute-done | bytes 94240 | tf_op jit(solution)/shard_map/ppermute | solution.py:125
  113.4 0.8 fusion.44
  (103 shorter events, 7.0 us)
Async XLA Ops:
  0.6 29.1 %copy-start.2 = (bf16[32,2880]{1,0:T(8,128)(2,1)S(1)}, bf16[32,2880]{1,0:T(8,128)(2,1)}, u32[]{:S(2)}) copy-start(bf16[32,2880]{1,0:T(8,128)(2,1)} %param.12) | copy-start | bytes 552964
  25.4 21.7 %collective-permute-start = (bf16[72,2880]{1,0:T(8,128)(2,1)S(1)}, bf16[72,2880]{1,0:T(8,128)(2,1)S(1)}, u32[]{:S(2)}, u32[]{:S(2)}) collective-permute-start(bf16[72,2880]{1,0:T(8,128)(2,1)S(1)} %convolution_convert_fusion.1), channel_id=1, source_target_pairs={{0,4},{1,5},{2,6},{3,7},{4,0},{5,1},{6,2},{7,3},{8,12},{9,13},{10,... | collective-permute-start | bytes 1244168 | tf_op jit(solution)/shard_map/ppermute | solution.py:120
  27.0 20.2 %collective-permute-start.2 = (bf16[72,2880]{1,0:T(8,128)(2,1)S(1)}, bf16[72,2880]{1,0:T(8,128)(2,1)S(1)}, u32[]{:S(2)}, u32[]{:S(2)}) collective-permute-start(bf16[72,2880]{1,0:T(8,128)(2,1)S(1)} %convolution_convert_fusion.1), channel_id=1, source_target_pairs={{0,6},{1,7},{2,4},{3,5},{4,2},{5,3},{6,0},{7,1},{8,14},{9,15},{10,... | collective-permute-start | bytes 1244168 | tf_op jit(solution)/shard_map/ppermute | solution.py:120
  28.8 18.3 %collective-permute-start.1 = (bf16[72,2880]{1,0:T(8,128)(2,1)S(1)}, bf16[72,2880]{1,0:T(8,128)(2,1)S(1)}, u32[]{:S(2)}, u32[]{:S(2)}) collective-permute-start(bf16[72,2880]{1,0:T(8,128)(2,1)S(1)} %convolution_convert_fusion), channel_id=1, source_target_pairs={{0,2},{1,3},{2,0},{3,1},{4,6},{5,7},{6,4},{7,5},{8,10},{9,11},{10,... | collective-permute-start | bytes 1244168 | tf_op jit(solution)/shard_map/ppermute | solution.py:120
  29.7 21.3 %copy-start = (bf16[1,2880,720]{1,2,0:T(8,128)(2,1)S(1)}, bf16[1,2880,720]{1,2,0:T(8,128)(2,1)}, u32[]{:S(2)}) copy-start(bf16[1,2880,720]{1,2,0:T(8,128)(2,1)} %param.13) | copy-start | bytes 12441604
  47.7 10.5 %collective-permute-start.3 = (bf16[72,2880]{1,0:T(8,128)(2,1)S(1)}, bf16[72,2880]{1,0:T(8,128)(2,1)S(1)}, u32[]{:S(2)}, u32[]{:S(2)}) collective-permute-start(bf16[72,2880]{1,0:T(8,128)(2,1)S(1)} %fusion.13), channel_id=1, source_target_pairs={{0,4},{1,5},{2,6},{3,7},{4,0},{5,1},{6,2},{7,3},{8,12},{9,13},{10,... | collective-permute-start | bytes 1244168 | tf_op jit(solution)/shard_map/ppermute | solution.py:120
  49.3 9.0 %collective-permute-start.4 = (bf16[72,2880]{1,0:T(8,128)(2,1)S(1)}, bf16[72,2880]{1,0:T(8,128)(2,1)S(1)}, u32[]{:S(2)}, u32[]{:S(2)}) collective-permute-start(bf16[72,2880]{1,0:T(8,128)(2,1)S(1)} %get-tuple-element.104), channel_id=1, source_target_pairs={{0,2},{1,3},{2,0},{3,1},{4,6},{5,7},{6,4},{7,5},{8,10},{9,11},{10,... | collective-permute-start | bytes 1244168 | tf_op jit(solution)/shard_map/ppermute | solution.py:120
  50.8 3.5 %collective-permute-start.5 = (bf16[144,2880]{1,0:T(8,128)(2,1)S(1)}, bf16[144,2880]{1,0:T(8,128)(2,1)S(1)}, u32[]{:S(2)}, u32[]{:S(2)}) collective-permute-start(bf16[144,2880]{1,0:T(8,128)(2,1)S(1)} %pad_maximum_fusion.5), channel_id=1, source_target_pairs={{0,1},{1,0},{2,3},{3,2},{4,5},{5,4},{6,7},{7,6},{8,9},{9,8},{10,11... | collective-permute-start | bytes 2488328 | tf_op jit(solution)/shard_map/ppermute | solution.py:120
  50.9 2.2 %slice-start = ((s8[4239360]{0:T(1024)(128)(4,1)}), s8[4194304]{0:T(1024)(128)(4,1)S(1)}, s32[]{:S(2)}) async-start(s8[4239360]{0:T(1024)(128)(4,1)} %bitcast.73), calls=%async_computation | async-start | bytes 8388608
  51.0 2.1 %slice-start.1 = ((s8[4239360]{0:T(1024)(128)(4,1)}), s8[45056]{0:T(1024)(128)(4,1)S(1)}, s32[]{:S(2)}) async-start(s8[4239360]{0:T(1024)(128)(4,1)} %bitcast.73), calls=%async_computation.1 | async-start | bytes 90112
  53.6 5.4 %collective-permute-start.9 = (bf16[144,2880]{1,0:T(8,128)(2,1)S(1)}, bf16[144,2880]{1,0:T(8,128)(2,1)S(1)}, u32[]{:S(2)}, u32[]{:S(2)}) collective-permute-start(bf16[144,2880]{1,0:T(8,128)(2,1)S(1)} %pad_maximum_fusion.7), channel_id=1, source_target_pairs={{0,1},{1,0},{2,3},{3,2},{4,5},{5,4},{6,7},{7,6},{8,9},{9,8},{10,11... | collective-permute-start | bytes 2488328 | tf_op jit(solution)/shard_map/ppermute | solution.py:120
  54.4 2.2 %slice-start.2 = ((s8[4239360]{0:T(1024)(128)(4,1)}), s8[4194304]{0:T(1024)(128)(4,1)S(1)}, s32[]{:S(2)}) async-start(s8[4239360]{0:T(1024)(128)(4,1)} %bitcast.80), calls=%async_computation.2 | async-start | bytes 8388608
  54.6 2.0 %slice-start.3 = ((s8[4239360]{0:T(1024)(128)(4,1)}), s8[45056]{0:T(1024)(128)(4,1)S(1)}, s32[]{:S(2)}) async-start(s8[4239360]{0:T(1024)(128)(4,1)} %bitcast.80), calls=%async_computation.3 | async-start | bytes 90112
  58.2 12.8 %collective-permute-start.8 = (bf16[72,2880]{1,0:T(8,128)(2,1)S(1)}, bf16[72,2880]{1,0:T(8,128)(2,1)S(1)}, u32[]{:S(2)}, u32[]{:S(2)}) collective-permute-start(bf16[72,2880]{1,0:T(8,128)(2,1)S(1)} %collective-permute-done.3), channel_id=1, source_target_pairs={{0,2},{1,3},{2,0},{3,1},{4,6},{5,7},{6,4},{7,5},{8,10},{9,11},{10,... | collective-permute-start | bytes 1244168 | tf_op jit(solution)/shard_map/ppermute | solution.py:120
  58.9 4.3 %collective-permute-start.6 = (bf16[144,2880]{1,0:T(8,128)(2,1)S(1)}, bf16[144,2880]{1,0:T(8,128)(2,1)S(1)}, u32[]{:S(2)}, u32[]{:S(2)}) collective-permute-start(bf16[144,2880]{1,0:T(8,128)(2,1)S(1)} %pad_maximum_fusion.6), channel_id=1, source_target_pairs={{0,1},{1,0},{2,3},{3,2},{4,5},{5,4},{6,7},{7,6},{8,9},{9,8},{10,11... | collective-permute-start | bytes 2488328 | tf_op jit(solution)/shard_map/ppermute | solution.py:120
  60.8 11.0 %collective-permute-start.10 = (bf16[72,2880]{1,0:T(8,128)(2,1)S(1)}, bf16[72,2880]{1,0:T(8,128)(2,1)S(1)}, u32[]{:S(2)}, u32[]{:S(2)}) collective-permute-start(bf16[72,2880]{1,0:T(8,128)(2,1)S(1)} %collective-permute-done.4), channel_id=1, source_target_pairs={{0,1},{1,0},{2,3},{3,2},{4,5},{5,4},{6,7},{7,6},{8,9},{9,8},{10,11... | collective-permute-start | bytes 1244168 | tf_op jit(solution)/shard_map/ppermute | solution.py:120
  68.3 2.4 %collective-permute-start.7 = (bf16[144,2880]{1,0:T(8,128)(2,1)S(1)}, bf16[144,2880]{1,0:T(8,128)(2,1)S(1)}, u32[]{:S(2)}, u32[]{:S(2)}) collective-permute-start(bf16[144,2880]{1,0:T(8,128)(2,1)S(1)} %slice.112), channel_id=1, source_target_pairs={{0,1},{1,0},{2,3},{3,2},{4,5},{5,4},{6,7},{7,6},{8,9},{9,8},{10,11... | collective-permute-start | bytes 2488328 | tf_op jit(solution)/shard_map/ppermute | solution.py:120
  71.0 1.8 %collective-permute-start.11 = (bf16[72,2880]{1,0:T(8,128)(2,1)S(1)}, bf16[72,2880]{1,0:T(8,128)(2,1)S(1)}, u32[]{:S(2)}, u32[]{:S(2)}) collective-permute-start(bf16[72,2880]{1,0:T(8,128)(2,1)S(1)} %collective-permute-done.8), channel_id=1, source_target_pairs={{0,1},{1,0},{2,3},{3,2},{4,5},{5,4},{6,7},{7,6},{8,9},{9,8},{10,11... | collective-permute-start | bytes 1244168 | tf_op jit(solution)/shard_map/ppermute | solution.py:120
  71.2 21.3 %collective-permute-start.16 = (bf16[72,2880]{1,0:T(8,128)(2,1)S(1)}, bf16[72,2880]{1,0:T(8,128)(2,1)S(1)}, u32[]{:S(2)}, u32[]{:S(2)}) collective-permute-start(bf16[72,2880]{1,0:T(8,128)(2,1)S(1)} %slice.183), channel_id=1, source_target_pairs={{0,4},{1,5},{2,6},{3,7},{4,0},{5,1},{6,2},{7,3},{8,12},{9,13},{10,... | collective-permute-start | bytes 1244168 | tf_op jit(solution)/shard_map/ppermute | solution.py:120
  77.8 1.8 %collective-permute-start.12 = (bf16[144,1408]{1,0:T(8,128)(2,1)S(1)}, bf16[144,1408]{1,0:T(8,128)(2,1)S(1)}, u32[]{:S(2)}, u32[]{:S(2)}) collective-permute-start(bf16[144,1408]{1,0:T(8,128)(2,1)S(1)} %slice.117), channel_id=1, source_target_pairs={{0,1},{1,0},{2,3},{3,2},{4,5},{5,4},{6,7},{7,6},{8,9},{9,8},{10,11... | collective-permute-start | bytes 1216520 | tf_op jit(solution)/shard_map/ppermute | solution.py:120
  79.7 7.0 %collective-permute-start.15 = (bf16[144,1472]{1,0:T(8,128)(2,1)S(1)}, bf16[144,1472]{1,0:T(8,128)(2,1)S(1)}, u32[]{:S(2)}, u32[]{:S(2)}) collective-permute-start(bf16[144,1472]{1,0:T(8,128)(2,1)S(1)} %slice.121), channel_id=1, source_target_pairs={{0,1},{1,0},{2,3},{3,2},{4,5},{5,4},{6,7},{7,6},{8,9},{9,8},{10,11... | collective-permute-start | bytes 1271816 | tf_op jit(solution)/shard_map/ppermute | solution.py:120
  80.0 9.9 %collective-permute-start.13 = (bf16[72,1408]{1,0:T(8,128)(2,1)S(1)}, bf16[72,1408]{1,0:T(8,128)(2,1)S(1)}, u32[]{:S(2)}, u32[]{:S(2)}) collective-permute-start(bf16[72,1408]{1,0:T(8,128)(2,1)S(1)} %get-tuple-element.99), channel_id=1, source_target_pairs={{0,2},{1,3},{2,0},{3,1},{4,6},{5,7},{6,4},{7,5},{8,10},{9,11},{10,... | collective-permute-start | bytes 608264 | tf_op jit(solution)/shard_map/ppermute | solution.py:120
  81.5 10.7 %collective-permute-start.14 = (bf16[72,1408]{1,0:T(8,128)(2,1)S(1)}, bf16[72,1408]{1,0:T(8,128)(2,1)S(1)}, u32[]{:S(2)}, u32[]{:S(2)}) collective-permute-start(bf16[72,1408]{1,0:T(8,128)(2,1)S(1)} %get-tuple-element.98), channel_id=1, source_target_pairs={{0,6},{1,7},{2,4},{3,5},{4,2},{5,3},{6,0},{7,1},{8,14},{9,15},{10,... | collective-permute-start | bytes 608264 | tf_op jit(solution)/shard_map/ppermute | solution.py:120
  86.8 15.5 %collective-permute-start.20 = (bf16[72,1472]{1,0:T(8,128)(2,1)S(1)}, bf16[72,1472]{1,0:T(8,128)(2,1)S(1)}, u32[]{:S(2)}, u32[]{:S(2)}) collective-permute-start(bf16[72,1472]{1,0:T(8,128)(2,1)S(1)} %get-tuple-element.93), channel_id=1, source_target_pairs={{0,2},{1,3},{2,0},{3,1},{4,6},{5,7},{6,4},{7,5},{8,10},{9,11},{10,... | collective-permute-start | bytes 635912 | tf_op jit(solution)/shard_map/ppermute | solution.py:120
  88.4 14.0 %collective-permute-start.21 = (bf16[72,1472]{1,0:T(8,128)(2,1)S(1)}, bf16[72,1472]{1,0:T(8,128)(2,1)S(1)}, u32[]{:S(2)}, u32[]{:S(2)}) collective-permute-start(bf16[72,1472]{1,0:T(8,128)(2,1)S(1)} %get-tuple-element.92), channel_id=1, source_target_pairs={{0,6},{1,7},{2,4},{3,5},{4,2},{5,3},{6,0},{7,1},{8,14},{9,15},{10,... | collective-permute-start | bytes 635912 | tf_op jit(solution)/shard_map/ppermute | solution.py:120
  92.9 8.6 %collective-permute-start.17 = (bf16[32,1408]{1,0:T(8,128)(2,1)S(1)}, bf16[32,1408]{1,0:T(8,128)(2,1)S(1)}, u32[]{:S(2)}, u32[]{:S(2)}) collective-permute-start(bf16[32,1408]{1,0:T(8,128)(2,1)S(1)} %get-tuple-element.91), channel_id=1, source_target_pairs={{0,8},{1,9},{2,10},{3,11},{4,12},{5,13},{6,14},{7,15},{8,16},{9,17... | collective-permute-start | bytes 270344 | tf_op jit(solution)/shard_map/ppermute | solution.py:125
  93.0 9.3 %collective-permute-start.18 = (bf16[32,1408]{1,0:T(8,128)(2,1)S(1)}, bf16[32,1408]{1,0:T(8,128)(2,1)S(1)}, u32[]{:S(2)}, u32[]{:S(2)}) collective-permute-start(bf16[32,1408]{1,0:T(8,128)(2,1)S(1)} %get-tuple-element.90), channel_id=1, source_target_pairs={{0,16},{1,17},{2,18},{3,19},{4,20},{5,21},{6,22},{7,23},{8,24},{9,... | collective-permute-start | bytes 270344 | tf_op jit(solution)/shard_map/ppermute | solution.py:125
  95.0 7.3 %collective-permute-start.19 = (bf16[32,1408]{1,0:T(8,128)(2,1)S(1)}, bf16[32,1408]{1,0:T(8,128)(2,1)S(1)}, u32[]{:S(2)}, u32[]{:S(2)}) collective-permute-start(bf16[32,1408]{1,0:T(8,128)(2,1)S(1)} %get-tuple-element.89), channel_id=1, source_target_pairs={{0,24},{1,25},{2,26},{3,27},{4,28},{5,29},{6,30},{7,31},{8,0},{9,1... | collective-permute-start | bytes 270344 | tf_op jit(solution)/shard_map/ppermute | solution.py:125
  103.1 8.9 %collective-permute-start.22 = (bf16[32,1472]{1,0:T(8,128)(2,1)S(1)}, bf16[32,1472]{1,0:T(8,128)(2,1)S(1)}, u32[]{:S(2)}, u32[]{:S(2)}) collective-permute-start(bf16[32,1472]{1,0:T(8,128)(2,1)S(1)} %get-tuple-element.88), channel_id=1, source_target_pairs={{0,8},{1,9},{2,10},{3,11},{4,12},{5,13},{6,14},{7,15},{8,16},{9,17... | collective-permute-start | bytes 282632 | tf_op jit(solution)/shard_map/ppermute | solution.py:125
  104.7 8.5 %collective-permute-start.23 = (bf16[32,1472]{1,0:T(8,128)(2,1)S(1)}, bf16[32,1472]{1,0:T(8,128)(2,1)S(1)}, u32[]{:S(2)}, u32[]{:S(2)}) collective-permute-start(bf16[32,1472]{1,0:T(8,128)(2,1)S(1)} %get-tuple-element.87), channel_id=1, source_target_pairs={{0,16},{1,17},{2,18},{3,19},{4,20},{5,21},{6,22},{7,23},{8,24},{9,... | collective-permute-start | bytes 282632 | tf_op jit(solution)/shard_map/ppermute | solution.py:125
  106.3 6.9 %copy-start.1 = (bf16[32,2880]{1,0:T(8,128)(2,1)S(1)}, bf16[32,2880]{1,0:T(8,128)(2,1)}, u32[]{:S(2)}) copy-start(bf16[32,2880]{1,0:T(8,128)(2,1)} %param.8) | copy-start | bytes 552964
  106.3 6.9 %copy-start.3 = (f32[2880]{0:T(1024)S(1)}, f32[2880]{0:T(1024)}, u32[]{:S(2)}) copy-start(f32[2880]{0:T(1024)} %param.9) | copy-start | bytes 34564
  106.3 6.9 %collective-permute-start.24 = (bf16[32,1472]{1,0:T(8,128)(2,1)S(1)}, bf16[32,1472]{1,0:T(8,128)(2,1)S(1)}, u32[]{:S(2)}, u32[]{:S(2)}) collective-permute-start(bf16[32,1472]{1,0:T(8,128)(2,1)S(1)} %get-tuple-element.86), channel_id=1, source_target_pairs={{0,24},{1,25},{2,26},{3,27},{4,28},{5,29},{6,30},{7,31},{8,0},{9,1... | collective-permute-start | bytes 282632 | tf_op jit(solution)/shard_map/ppermute | solution.py:125

commit v6 on v5

--- a/solution.py
+++ b/solution.py
@@ -189,7 +189,6 @@
 
     gate_w = fast_copy(behind(w_gate[0], (own_dy, far_dy)).T).T
     up_w = w_up[0]
-    down_w = fast_copy(behind(w_down[0], gate_w))
 
     def forward(x_in):
         gate = jnp.dot(x_in, gate_w, preferred_element_type=jnp.float32)
@@ -218,6 +217,7 @@
     chip_forward = forward(chip_x)
     side_dy, pair_dy = behind((side_dy, pair_dy), chip_forward)
     across_dy = flip(side_dy, PAIR)
+    down_w = fast_copy(behind(w_down[0], side_dy))
     chip_dy = both_cores(own_dy, side_dy)
     pair_forward = forward(behind(pair_x, chip_dy))
     chip_hid, chip_d_gate, chip_d_up = hidden(*chip_forward, chip_dy)

time: 114 us -> 118 us (1.035)
  waiting for transfers between devices: 8.08 us -> 13.5 us
  local copies, waits for them, and re-layouts: 3.54 us -> 1.77 us
    ppermute x19, waiting for transfers between devices: 6.07 us -> 9.44 us  [flip(): lax.ppermute(row_major(value), 'sq', [(i, i ^ bit) for i in range(devices)])]
    ppermute x6, waiting for transfers between devices: 2.02 us -> 4.06 us  [shift(): return lax.ppermute(row_major(value), 'sq', pairs)]
    unnamed x26 -> x28, local copies, waits for them, and re-layouts: 2.74 us -> 0.97 us
    ppermute x6, starting transfers between devices: 8.07 us -> 6.81 us  [shift(): return lax.ppermute(row_major(value), 'sq', pairs)]
  transfers between devices with their start and end apart: 25 -> 25, of which waited for: 6 -> 9; matrix products, arithmetic and copies ran while one was open for 18% -> 18% of each run, Pallas kernels for 13% -> 13%
where the time goes in v6:
time: 118 us
  blocking collectives  38.3 us (32%)
  starting transfers between devices  22.1 us (19%)
  matrix products  20.3 us (17%)
  Pallas kernels  15.1 us (13%)
  waiting for transfers between devices  13.5 us (11%)
  other arithmetic  5.57 us (5%)
  local copies, waits for them, and re-layouts  1.77 us (2%)
  between operations  1.32 us (1%)
    all_gather x2, blocking collectives, gather_column(): lax.all_gather(block, 'sq', axis=0, tiled=True, axis_index_groups=lines)  38.3 us
    ppermute x19, starting transfers between devices, flip(): lax.ppermute(row_major(value), 'sq', [(i, i ^ bit) for i in range(devices)])  15.3 us
    pallas_call x3, Pallas kernels, weight_product(): pl.pallas_call(product_kernel, in_specs=[pl.BlockSpec(memory_space=pltpu....  14.2 us
    dot_general x8, matrix products, contract_cols(): lax.dot_general(left, right, (((1,), (1,)), ((), ())), preferred_element_...  10.4 us
    ppermute x19, waiting for transfers between devices, flip(): lax.ppermute(row_major(value), 'sq', [(i, i ^ bit) for i in range(devices)])  9.44 us
    ppermute x6, starting transfers between devices, shift(): return lax.ppermute(row_major(value), 'sq', pairs)  6.81 us
    dot_general x2, matrix products, forward(): gate = jnp.dot(x_in, gate_w, preferred_element_type=jnp.float32)  4.21 us
    ppermute x6, waiting for transfers between devices, shift(): return lax.ppermute(row_major(value), 'sq', pairs)  4.06 us
  transfers between devices with their start and end apart: 25, of which 9 were waited for; matrix products, arithmetic and copies ran while one was open for 18% of the time, Pallas kernels for 13%

profile of v6, /device:TPU:0, one launch (start us, length us, event | category | flops | bytes accessed | tf_op | source)
XLA Modules:
  0.0 118.0 jit_solution(12603129783306059237)
XLA Ops:
  0.6 0.7 select_reduce_fusion.4
  1.5 1.1 fusion.45
  2.7 1.0 fusion.40
  3.8 20.9 %all_gather.6 = bf16[128,2904]{1,0:T(8,128)(2,1)S(1)} all-gather(bf16[32,2904]{1,0:T(8,128)(2,1)S(1)} %concatenate.47), channel_id=1, replica_groups={{0,8,16,24},{1,9,17,25},{2,10,18,26},{3,11,19,27},{4,12,20,28},{5,13,21..., dimensions={0}, use_global_device_ids=true | all-gather | bytes 929280 | tf_op jit(solution)/shard_map/all_gather | solution.py:141
  25.4 1.6 %collective-permute-start = (bf16[72,2880]{1,0:T(8,128)(2,1)S(1)}, bf16[72,2880]{1,0:T(8,128)(2,1)S(1)}, u32[]{:S(2)}, u32[]{:S(2)}) collective-permute-start(bf16[72,2880]{1,0:T(8,128)(2,1)S(1)} %convolution_convert_fusion.1), channel_id=1, source_target_pairs={{0,4},{1,5},{2,6},{3,7},{4,0},{5,1},{6,2},{7,3},{8,12},{9,13},{10,... | collective-permute-start | bytes 1244168 | tf_op jit(solution)/shard_map/ppermute | solution.py:120
  27.0 1.4 %collective-permute-start.2 = (bf16[72,2880]{1,0:T(8,128)(2,1)S(1)}, bf16[72,2880]{1,0:T(8,128)(2,1)S(1)}, u32[]{:S(2)}, u32[]{:S(2)}) collective-permute-start(bf16[72,2880]{1,0:T(8,128)(2,1)S(1)} %convolution_convert_fusion.1), channel_id=1, source_target_pairs={{0,6},{1,7},{2,4},{3,5},{4,2},{5,3},{6,0},{7,1},{8,14},{9,15},{10,... | collective-permute-start | bytes 1244168 | tf_op jit(solution)/shard_map/ppermute | solution.py:120
  28.8 0.6 collective-permute-start.1
  29.7 17.4 %all_gather.7 = bf16[128,2880]{1,0:T(8,128)(2,1)S(1)} all-gather(bf16[32,2880]{1,0:T(8,128)(2,1)S(1)} %copy-done.2), channel_id=1, replica_groups={{0,8,16,24},{1,9,17,25},{2,10,18,26},{3,11,19,27},{4,12,20,28},{5,13,21..., dimensions={0}, use_global_device_ids=true | all-gather | bytes 921600 | tf_op jit(solution)/shard_map/all_gather | solution.py:141
  47.4 1.6 %collective-permute-start.3 = (bf16[72,2880]{1,0:T(8,128)(2,1)S(1)}, bf16[72,2880]{1,0:T(8,128)(2,1)S(1)}, u32[]{:S(2)}, u32[]{:S(2)}) collective-permute-start(bf16[72,2880]{1,0:T(8,128)(2,1)S(1)} %fusion.13), channel_id=1, source_target_pairs={{0,4},{1,5},{2,6},{3,7},{4,0},{5,1},{6,2},{7,3},{8,12},{9,13},{10,... | collective-permute-start | bytes 1244168 | tf_op jit(solution)/shard_map/ppermute | solution.py:120
  49.3 1.6 %collective-permute-start.4 = (bf16[72,2880]{1,0:T(8,128)(2,1)S(1)}, bf16[72,2880]{1,0:T(8,128)(2,1)S(1)}, u32[]{:S(2)}, u32[]{:S(2)}) collective-permute-start(bf16[72,2880]{1,0:T(8,128)(2,1)S(1)} %get-tuple-element.104), channel_id=1, source_target_pairs={{0,2},{1,3},{2,0},{3,1},{4,6},{5,7},{6,4},{7,5},{8,10},{9,11},{10,... | collective-permute-start | bytes 1244168 | tf_op jit(solution)/shard_map/ppermute | solution.py:120
  51.0 0.6 collective-permute-start.9
  52.1 1.2 %collective-permute-done.5 = bf16[144,2880]{1,0:T(8,128)(2,1)S(1)} collective-permute-done((bf16[144,2880]{1,0:T(8,128)(2,1)S(1)}, bf16[144,2880]{1,0:T(8,128)(2,1)S(1)}, u32[]{:S(2)}, u32[]{:S(2)}) %collective-permute-start.5) | collective-permute-done | bytes 829472 | tf_op jit(solution)/shard_map/ppermute | solution.py:120
  53.8 1.6 %fusion.4 = f32[288,720]{1,0:T(8,128)S(1)} fusion(bf16[288,2880]{1,0:T(8,128)(2,1)S(1)} %get-tuple-element.85, bf16[1,2880,720]{1,2,0:T(8,128)(2,1)S(1)} %bitcast.81), kind=kOutput, calls=%fused_computation.4 | convolution fusion | flops 1194393600 | bytes 6635520 | tf_op jit(solution)/shard_map/dot_general | solution.py:195
  55.4 2.6 %fusion.93 = f32[288,720]{1,0:T(8,128)} fusion(bf16[288,2880]{1,0:T(8,128)(2,1)S(1)} %get-tuple-element.85, bf16[720,2880]{1,0:T(8,128)(2,1)S(1)} %shard_map.111), kind=kOutput, calls=%fused_computation.163 | convolution fusion | flops 1194393600 | bytes 6635520 | tf_op jit(solution)/shard_map/dot_general | solution.py:194
  58.0 0.9 collective-permute-start.8
  59.2 1.7 %fusion = f32[288,720]{1,0:T(8,128)S(1)} fusion(bf16[288,2880]{1,0:T(8,128)(2,1)S(1)} %pad_maximum_fusion.1, bf16[1,2880,720]{1,2,0:T(8,128)(2,1)S(1)} %bitcast.81), kind=kOutput, calls=%fused_computation | convolution fusion | flops 1194393600 | bytes 6635520 | tf_op jit(solution)/shard_map/dot_general | solution.py:195
  61.0 0.5 collective-permute-start.6
  61.5 0.5 shard_map.112
  62.2 1.7 %fusion.95 = f32[288,720]{1,0:T(8,128)S(1)} fusion(bf16[288,2880]{1,0:T(8,128)(2,1)S(1)} %pad_maximum_fusion.1, bf16[720,2880]{1,0:T(8,128)(2,1)S(1)} %shard_map.111), kind=kOutput, calls=%fused_computation.165 | convolution fusion | flops 1194393600 | bytes 6635520 | tf_op jit(solution)/shard_map/dot_general | solution.py:194
  64.0 1.9 %multiply_convert_fusion.1 = (bf16[288,720]{1,0:T(8,128)(2,1)S(1)}, bf16[288,720]{1,0:T(8,128)(2,1)S(1)}, bf16[288,720]{1,0:T(8,128)(2,1)S(1)}) fusion(f32[288,720]{1,0:T(8,128)S(1)} %fusion.4, f32[288,720]{1,0:T(8,128)S(1)} %copy-done.4, bf16[720,2880]{1,0:T(8,128)(2,1)S(1)} %shard_map.112, bf16[144,2880]{1,0:T(8,128)(2,1)S(1)} %collective-permute-done.6, ...), kind=kOutput, calls=%fused_computation.43 | convolution fusion | flops 1202895360 | bytes 8709120 | tf_op jit(solution)/shard_map/dot_general | solution.py:25
  65.9 1.5 %fusion.94 = f32[288,2880]{1,0:T(8,128)S(1)} fusion(bf16[288,720]{1,0:T(8,128)(2,1)S(1)} %get-tuple-element.79, bf16[720,2880]{1,0:T(8,128)(2,1)S(1)} %shard_map.111), kind=kOutput, calls=%fused_computation.164 | convolution fusion | flops 1194393600 | bytes 7879680 | tf_op jit(solution)/shard_map/dot_general | solution.py:25
  67.4 1.6 %fusion.9 = bf16[288,2880]{1,0:T(8,128)(2,1)S(1)} fusion(f32[288,2880]{1,0:T(8,128)S(1)} %fusion.94, bf16[288,720]{1,0:T(8,128)(2,1)S(1)} %get-tuple-element.80, bf16[1,2880,720]{1,2,0:T(8,128)(2,1)S(1)} %bitcast.81), kind=kOutput, calls=%fused_computation.7 | convolution fusion | flops 1196052480 | bytes 9538560 | tf_op jit(solution)/shard_map/dot_general | solution.py:25
  69.5 2.0 %collective-permute-done.7 = bf16[144,2880]{1,0:T(8,128)(2,1)S(1)} collective-permute-done((bf16[144,2880]{1,0:T(8,128)(2,1)S(1)}, bf16[144,2880]{1,0:T(8,128)(2,1)S(1)}, u32[]{:S(2)}, u32[]{:S(2)}) %collective-permute-start.7) | collective-permute-done | bytes 829472 | tf_op jit(solution)/shard_map/ppermute | solution.py:120
  72.0 0.6 collective-permute-start.16
  72.7 0.9 collective-permute-done.11
  73.6 1.9 %multiply_convert_fusion = (bf16[288,720]{1,0:T(8,128)(2,1)S(1)}, bf16[288,720]{1,0:T(8,128)(2,1)S(1)}, bf16[288,720]{1,0:T(8,128)(2,1)S(1)}) fusion(f32[288,720]{1,0:T(8,128)S(1)} %fusion, f32[288,720]{1,0:T(8,128)S(1)} %fusion.95, bf16[720,2880]{1,0:T(8,128)(2,1)S(1)} %shard_map.112, bf16[72,2880]{1,0:T(8,128)(2,1)S(1)} %collective-permute-done.11, ...), kind=kOutput, calls=%fused_computation.42 | convolution fusion | flops 1204554240 | bytes 8709120 | tf_op jit(solution)/shard_map/dot_general | solution.py:25
  75.6 0.9 fusion.20
  76.5 0.9 fusion.15
  77.4 0.9 fusion.16
  78.5 0.9 fusion.14
  79.5 0.5 collective-permute-done.12
  80.4 1.2 %collective-permute-start.14 = (bf16[72,1408]{1,0:T(8,128)(2,1)S(1)}, bf16[72,1408]{1,0:T(8,128)(2,1)S(1)}, u32[]{:S(2)}, u32[]{:S(2)}) collective-permute-start(bf16[72,1408]{1,0:T(8,128)(2,1)S(1)} %get-tuple-element.98), channel_id=1, source_target_pairs={{0,6},{1,7},{2,4},{3,5},{4,2},{5,3},{6,0},{7,1},{8,14},{9,15},{10,... | collective-permute-start | bytes 608264 | tf_op jit(solution)/shard_map/ppermute | solution.py:120
  81.7 0.9 collective-permute-start.13
  82.6 4.9 %shard_map.113 = bf16[720,2880]{1,0:T(8,128)(2,1)} custom-call(bf16[576,720]{1,0:T(8,128)(2,1)S(1)} %pad_maximum_fusion.2.left_ref, bf16[576,2880]{1,0:T(8,128)(2,1)S(1)} %constant_dynamic-update-slice_fusion.3.right_ref), custom_call_target="tpu_custom_call" | custom-call | flops 2388787200 | bytes 8294400 | tf_op jit(solution)/shard_map/pallas_call | solution.py:80
  87.6 1.6 %collective-permute-done.14 = bf16[72,1408]{1,0:T(8,128)(2,1)S(1)} collective-permute-done((bf16[72,1408]{1,0:T(8,128)(2,1)S(1)}, bf16[72,1408]{1,0:T(8,128)(2,1)S(1)}, u32[]{:S(2)}, u32[]{:S(2)}) %collective-permute-start.14) | collective-permute-done | bytes 202784 | tf_op jit(solution)/shard_map/ppermute | solution.py:120
  89.3 3.0 %collective-permute-done.13 = bf16[72,1408]{1,0:T(8,128)(2,1)S(1)} collective-permute-done((bf16[72,1408]{1,0:T(8,128)(2,1)S(1)}, bf16[72,1408]{1,0:T(8,128)(2,1)S(1)}, u32[]{:S(2)}, u32[]{:S(2)}) %collective-permute-start.13) | collective-permute-done | bytes 202784 | tf_op jit(solution)/shard_map/ppermute | solution.py:120
  92.2 1.9 %collective-permute-start.21 = (bf16[72,1472]{1,0:T(8,128)(2,1)S(1)}, bf16[72,1472]{1,0:T(8,128)(2,1)S(1)}, u32[]{:S(2)}, u32[]{:S(2)}) collective-permute-start(bf16[72,1472]{1,0:T(8,128)(2,1)S(1)} %get-tuple-element.92), channel_id=1, source_target_pairs={{0,6},{1,7},{2,4},{3,5},{4,2},{5,3},{6,0},{7,1},{8,14},{9,15},{10,... | collective-permute-start | bytes 635912 | tf_op jit(solution)/shard_map/ppermute | solution.py:120
  94.1 0.9 collective-permute-start.20
  95.8 1.6 %collective-permute-start.19 = (bf16[32,1408]{1,0:T(8,128)(2,1)S(1)}, bf16[32,1408]{1,0:T(8,128)(2,1)S(1)}, u32[]{:S(2)}, u32[]{:S(2)}) collective-permute-start(bf16[32,1408]{1,0:T(8,128)(2,1)S(1)} %get-tuple-element.89), channel_id=1, source_target_pairs={{0,24},{1,25},{2,26},{3,27},{4,28},{5,29},{6,30},{7,31},{8,0},{9,1... | collective-permute-start | bytes 270344 | tf_op jit(solution)/shard_map/ppermute | solution.py:125
  97.4 1.3 %collective-permute-start.17 = (bf16[32,1408]{1,0:T(8,128)(2,1)S(1)}, bf16[32,1408]{1,0:T(8,128)(2,1)S(1)}, u32[]{:S(2)}, u32[]{:S(2)}) collective-permute-start(bf16[32,1408]{1,0:T(8,128)(2,1)S(1)} %get-tuple-element.91), channel_id=1, source_target_pairs={{0,8},{1,9},{2,10},{3,11},{4,12},{5,13},{6,14},{7,15},{8,16},{9,17... | collective-permute-start | bytes 270344 | tf_op jit(solution)/shard_map/ppermute | solution.py:125
  98.7 4.7 %shard_map.114 = bf16[720,2880]{1,0:T(8,128)(2,1)} custom-call(bf16[576,720]{1,0:T(8,128)(2,1)S(1)} %pad_maximum_fusion.3.left_ref, bf16[576,2880]{1,0:T(8,128)(2,1)S(1)} %constant_dynamic-update-slice_fusion.3.right_ref), custom_call_target="tpu_custom_call" | custom-call | flops 2388787200 | bytes 8294400 | tf_op jit(solution)/shard_map/pallas_call | solution.py:80
  103.4 1.9 %collective-permute-done.18 = bf16[32,1408]{1,0:T(8,128)(2,1)S(1)} collective-permute-done((bf16[32,1408]{1,0:T(8,128)(2,1)S(1)}, bf16[32,1408]{1,0:T(8,128)(2,1)S(1)}, u32[]{:S(2)}, u32[]{:S(2)}) %collective-permute-start.18) | collective-permute-done | bytes 90144 | tf_op jit(solution)/shard_map/ppermute | solution.py:125
  106.1 1.4 %collective-permute-start.24 = (bf16[32,1472]{1,0:T(8,128)(2,1)S(1)}, bf16[32,1472]{1,0:T(8,128)(2,1)S(1)}, u32[]{:S(2)}, u32[]{:S(2)}) collective-permute-start(bf16[32,1472]{1,0:T(8,128)(2,1)S(1)} %get-tuple-element.86), channel_id=1, source_target_pairs={{0,24},{1,25},{2,26},{3,27},{4,28},{5,29},{6,30},{7,31},{8,0},{9,1... | collective-permute-start | bytes 282632 | tf_op jit(solution)/shard_map/ppermute | solution.py:125
  107.5 0.5 collective-permute-start.23
  108.1 1.9 %collective-permute-start.22 = (bf16[32,1472]{1,0:T(8,128)(2,1)S(1)}, bf16[32,1472]{1,0:T(8,128)(2,1)S(1)}, u32[]{:S(2)}, u32[]{:S(2)}) collective-permute-start(bf16[32,1472]{1,0:T(8,128)(2,1)S(1)} %get-tuple-element.88), channel_id=1, source_target_pairs={{0,8},{1,9},{2,10},{3,11},{4,12},{5,13},{6,14},{7,15},{8,16},{9,17... | collective-permute-start | bytes 282632 | tf_op jit(solution)/shard_map/ppermute | solution.py:125
  110.0 4.7 %shard_map.115 = bf16[720,2880]{1,0:T(8,128)(2,1)} custom-call(bf16[576,720]{1,0:T(8,128)(2,1)S(1)} %pad_maximum_fusion.4.left_ref, bf16[576,2880]{1,0:T(8,128)(2,1)S(1)} %constant_dynamic-update-slice_fusion.9.right_ref), custom_call_target="tpu_custom_call" | custom-call | flops 2388787200 | bytes 8294400 | tf_op jit(solution)/shard_map/pallas_call | solution.py:80
  114.7 2.1 %collective-permute-done.23 = bf16[32,1472]{1,0:T(8,128)(2,1)S(1)} collective-permute-done((bf16[32,1472]{1,0:T(8,128)(2,1)S(1)}, bf16[32,1472]{1,0:T(8,128)(2,1)S(1)}, u32[]{:S(2)}, u32[]{:S(2)}) %collective-permute-start.23) | collective-permute-done | bytes 94240 | tf_op jit(solution)/shard_map/ppermute | solution.py:125
  117.1 0.8 fusion.44
  (105 shorter events, 7.5 us)
Async XLA Ops:
  0.6 29.1 %copy-start.2 = (bf16[32,2880]{1,0:T(8,128)(2,1)S(1)}, bf16[32,2880]{1,0:T(8,128)(2,1)}, u32[]{:S(2)}) copy-start(bf16[32,2880]{1,0:T(8,128)(2,1)} %param.12) | copy-start | bytes 552964
  25.4 21.7 %collective-permute-start = (bf16[72,2880]{1,0:T(8,128)(2,1)S(1)}, bf16[72,2880]{1,0:T(8,128)(2,1)S(1)}, u32[]{:S(2)}, u32[]{:S(2)}) collective-permute-start(bf16[72,2880]{1,0:T(8,128)(2,1)S(1)} %convolution_convert_fusion.1), channel_id=1, source_target_pairs={{0,4},{1,5},{2,6},{3,7},{4,0},{5,1},{6,2},{7,3},{8,12},{9,13},{10,... | collective-permute-start | bytes 1244168 | tf_op jit(solution)/shard_map/ppermute | solution.py:120
  27.0 20.2 %collective-permute-start.2 = (bf16[72,2880]{1,0:T(8,128)(2,1)S(1)}, bf16[72,2880]{1,0:T(8,128)(2,1)S(1)}, u32[]{:S(2)}, u32[]{:S(2)}) collective-permute-start(bf16[72,2880]{1,0:T(8,128)(2,1)S(1)} %convolution_convert_fusion.1), channel_id=1, source_target_pairs={{0,6},{1,7},{2,4},{3,5},{4,2},{5,3},{6,0},{7,1},{8,14},{9,15},{10,... | collective-permute-start | bytes 1244168 | tf_op jit(solution)/shard_map/ppermute | solution.py:120
  28.8 18.3 %collective-permute-start.1 = (bf16[72,2880]{1,0:T(8,128)(2,1)S(1)}, bf16[72,2880]{1,0:T(8,128)(2,1)S(1)}, u32[]{:S(2)}, u32[]{:S(2)}) collective-permute-start(bf16[72,2880]{1,0:T(8,128)(2,1)S(1)} %convolution_convert_fusion), channel_id=1, source_target_pairs={{0,2},{1,3},{2,0},{3,1},{4,6},{5,7},{6,4},{7,5},{8,10},{9,11},{10,... | collective-permute-start | bytes 1244168 | tf_op jit(solution)/shard_map/ppermute | solution.py:120
  29.7 21.9 %copy-start = (bf16[1,2880,720]{1,2,0:T(8,128)(2,1)S(1)}, bf16[1,2880,720]{1,2,0:T(8,128)(2,1)}, u32[]{:S(2)}) copy-start(bf16[1,2880,720]{1,2,0:T(8,128)(2,1)} %param.13) | copy-start | bytes 12441604
  47.4 10.6 %collective-permute-start.3 = (bf16[72,2880]{1,0:T(8,128)(2,1)S(1)}, bf16[72,2880]{1,0:T(8,128)(2,1)S(1)}, u32[]{:S(2)}, u32[]{:S(2)}) collective-permute-start(bf16[72,2880]{1,0:T(8,128)(2,1)S(1)} %fusion.13), channel_id=1, source_target_pairs={{0,4},{1,5},{2,6},{3,7},{4,0},{5,1},{6,2},{7,3},{8,12},{9,13},{10,... | collective-permute-start | bytes 1244168 | tf_op jit(solution)/shard_map/ppermute | solution.py:120
  49.3 8.7 %collective-permute-start.4 = (bf16[72,2880]{1,0:T(8,128)(2,1)S(1)}, bf16[72,2880]{1,0:T(8,128)(2,1)S(1)}, u32[]{:S(2)}, u32[]{:S(2)}) collective-permute-start(bf16[72,2880]{1,0:T(8,128)(2,1)S(1)} %get-tuple-element.104), channel_id=1, source_target_pairs={{0,2},{1,3},{2,0},{3,1},{4,6},{5,7},{6,4},{7,5},{8,10},{9,11},{10,... | collective-permute-start | bytes 1244168 | tf_op jit(solution)/shard_map/ppermute | solution.py:120
  50.9 2.4 %collective-permute-start.5 = (bf16[144,2880]{1,0:T(8,128)(2,1)S(1)}, bf16[144,2880]{1,0:T(8,128)(2,1)S(1)}, u32[]{:S(2)}, u32[]{:S(2)}) collective-permute-start(bf16[144,2880]{1,0:T(8,128)(2,1)S(1)} %pad_maximum_fusion.5), channel_id=1, source_target_pairs={{0,1},{1,0},{2,3},{3,2},{4,5},{5,4},{6,7},{7,6},{8,9},{9,8},{10,11... | collective-permute-start | bytes 2488328 | tf_op jit(solution)/shard_map/ppermute | solution.py:120
  51.0 8.0 %collective-permute-start.9 = (bf16[144,2880]{1,0:T(8,128)(2,1)S(1)}, bf16[144,2880]{1,0:T(8,128)(2,1)S(1)}, u32[]{:S(2)}, u32[]{:S(2)}) collective-permute-start(bf16[144,2880]{1,0:T(8,128)(2,1)S(1)} %pad_maximum_fusion.7), channel_id=1, source_target_pairs={{0,1},{1,0},{2,3},{3,2},{4,5},{5,4},{6,7},{7,6},{8,9},{9,8},{10,11... | collective-permute-start | bytes 2488328 | tf_op jit(solution)/shard_map/ppermute | solution.py:120
  51.6 2.2 %slice-start.2 = ((s8[4239360]{0:T(1024)(128)(4,1)}), s8[4194304]{0:T(1024)(128)(4,1)S(1)}, s32[]{:S(2)}) async-start(s8[4239360]{0:T(1024)(128)(4,1)} %bitcast.80), calls=%async_computation.2 | async-start | bytes 8388608
  51.6 2.2 %slice-start.3 = ((s8[4239360]{0:T(1024)(128)(4,1)}), s8[45056]{0:T(1024)(128)(4,1)S(1)}, s32[]{:S(2)}) async-start(s8[4239360]{0:T(1024)(128)(4,1)} %bitcast.80), calls=%async_computation.3 | async-start | bytes 90112
  58.0 13.7 %collective-permute-start.8 = (bf16[72,2880]{1,0:T(8,128)(2,1)S(1)}, bf16[72,2880]{1,0:T(8,128)(2,1)S(1)}, u32[]{:S(2)}, u32[]{:S(2)}) collective-permute-start(bf16[72,2880]{1,0:T(8,128)(2,1)S(1)} %collective-permute-done.3), channel_id=1, source_target_pairs={{0,2},{1,3},{2,0},{3,1},{4,6},{5,7},{6,4},{7,5},{8,10},{9,11},{10,... | collective-permute-start | bytes 1244168 | tf_op jit(solution)/shard_map/ppermute | solution.py:120
  59.0 2.5 %slice-start = ((s8[4239360]{0:T(1024)(128)(4,1)}), s8[4194304]{0:T(1024)(128)(4,1)S(1)}, s32[]{:S(2)}) async-start(s8[4239360]{0:T(1024)(128)(4,1)} %bitcast.73), calls=%async_computation | async-start | bytes 8388608
  59.2 2.3 %slice-start.1 = ((s8[4239360]{0:T(1024)(128)(4,1)}), s8[45056]{0:T(1024)(128)(4,1)S(1)}, s32[]{:S(2)}) async-start(s8[4239360]{0:T(1024)(128)(4,1)} %bitcast.73), calls=%async_computation.1 | async-start | bytes 90112
  60.9 11.7 %collective-permute-start.10 = (bf16[72,2880]{1,0:T(8,128)(2,1)S(1)}, bf16[72,2880]{1,0:T(8,128)(2,1)S(1)}, u32[]{:S(2)}, u32[]{:S(2)}) collective-permute-start(bf16[72,2880]{1,0:T(8,128)(2,1)S(1)} %collective-permute-done.4), channel_id=1, source_target_pairs={{0,1},{1,0},{2,3},{3,2},{4,5},{5,4},{6,7},{7,6},{8,9},{9,8},{10,11... | collective-permute-start | bytes 1244168 | tf_op jit(solution)/shard_map/ppermute | solution.py:120
  61.0 3.0 %collective-permute-start.6 = (bf16[144,2880]{1,0:T(8,128)(2,1)S(1)}, bf16[144,2880]{1,0:T(8,128)(2,1)S(1)}, u32[]{:S(2)}, u32[]{:S(2)}) collective-permute-start(bf16[144,2880]{1,0:T(8,128)(2,1)S(1)} %pad_maximum_fusion.6), channel_id=1, source_target_pairs={{0,1},{1,0},{2,3},{3,2},{4,5},{5,4},{6,7},{7,6},{8,9},{9,8},{10,11... | collective-permute-start | bytes 2488328 | tf_op jit(solution)/shard_map/ppermute | solution.py:120
  62.2 1.8 %copy-start.4 = (f32[288,720]{1,0:T(8,128)S(1)}, f32[288,720]{1,0:T(8,128)}, u32[]{:S(2)}) copy-start(f32[288,720]{1,0:T(8,128)} %fusion.93) | copy-start | bytes 2488324
  69.1 2.4 %collective-permute-start.7 = (bf16[144,2880]{1,0:T(8,128)(2,1)S(1)}, bf16[144,2880]{1,0:T(8,128)(2,1)S(1)}, u32[]{:S(2)}, u32[]{:S(2)}) collective-permute-start(bf16[144,2880]{1,0:T(8,128)(2,1)S(1)} %slice.112), channel_id=1, source_target_pairs={{0,1},{1,0},{2,3},{3,2},{4,5},{5,4},{6,7},{7,6},{8,9},{9,8},{10,11... | collective-permute-start | bytes 2488328 | tf_op jit(solution)/shard_map/ppermute | solution.py:120
  71.7 1.8 %collective-permute-start.11 = (bf16[72,2880]{1,0:T(8,128)(2,1)S(1)}, bf16[72,2880]{1,0:T(8,128)(2,1)S(1)}, u32[]{:S(2)}, u32[]{:S(2)}) collective-permute-start(bf16[72,2880]{1,0:T(8,128)(2,1)S(1)} %collective-permute-done.8), channel_id=1, source_target_pairs={{0,1},{1,0},{2,3},{3,2},{4,5},{5,4},{6,7},{7,6},{8,9},{9,8},{10,11... | collective-permute-start | bytes 1244168 | tf_op jit(solution)/shard_map/ppermute | solution.py:120
  72.0 23.4 %collective-permute-start.16 = (bf16[72,2880]{1,0:T(8,128)(2,1)S(1)}, bf16[72,2880]{1,0:T(8,128)(2,1)S(1)}, u32[]{:S(2)}, u32[]{:S(2)}) collective-permute-start(bf16[72,2880]{1,0:T(8,128)(2,1)S(1)} %slice.183), channel_id=1, source_target_pairs={{0,4},{1,5},{2,6},{3,7},{4,0},{5,1},{6,2},{7,3},{8,12},{9,13},{10,... | collective-permute-start | bytes 1244168 | tf_op jit(solution)/shard_map/ppermute | solution.py:120
  78.3 1.8 %collective-permute-start.12 = (bf16[144,1408]{1,0:T(8,128)(2,1)S(1)}, bf16[144,1408]{1,0:T(8,128)(2,1)S(1)}, u32[]{:S(2)}, u32[]{:S(2)}) collective-permute-start(bf16[144,1408]{1,0:T(8,128)(2,1)S(1)} %slice.117), channel_id=1, source_target_pairs={{0,1},{1,0},{2,3},{3,2},{4,5},{5,4},{6,7},{7,6},{8,9},{9,8},{10,11... | collective-permute-start | bytes 1216520 | tf_op jit(solution)/shard_map/ppermute | solution.py:120
  80.2 7.3 %collective-permute-start.15 = (bf16[144,1472]{1,0:T(8,128)(2,1)S(1)}, bf16[144,1472]{1,0:T(8,128)(2,1)S(1)}, u32[]{:S(2)}, u32[]{:S(2)}) collective-permute-start(bf16[144,1472]{1,0:T(8,128)(2,1)S(1)} %slice.121), channel_id=1, source_target_pairs={{0,1},{1,0},{2,3},{3,2},{4,5},{5,4},{6,7},{7,6},{8,9},{9,8},{10,11... | collective-permute-start | bytes 1271816 | tf_op jit(solution)/shard_map/ppermute | solution.py:120
  80.4 8.8 %collective-permute-start.14 = (bf16[72,1408]{1,0:T(8,128)(2,1)S(1)}, bf16[72,1408]{1,0:T(8,128)(2,1)S(1)}, u32[]{:S(2)}, u32[]{:S(2)}) collective-permute-start(bf16[72,1408]{1,0:T(8,128)(2,1)S(1)} %get-tuple-element.98), channel_id=1, source_target_pairs={{0,6},{1,7},{2,4},{3,5},{4,2},{5,3},{6,0},{7,1},{8,14},{9,15},{10,... | collective-permute-start | bytes 608264 | tf_op jit(solution)/shard_map/ppermute | solution.py:120
  81.7 10.5 %collective-permute-start.13 = (bf16[72,1408]{1,0:T(8,128)(2,1)S(1)}, bf16[72,1408]{1,0:T(8,128)(2,1)S(1)}, u32[]{:S(2)}, u32[]{:S(2)}) collective-permute-start(bf16[72,1408]{1,0:T(8,128)(2,1)S(1)} %get-tuple-element.99), channel_id=1, source_target_pairs={{0,2},{1,3},{2,0},{3,1},{4,6},{5,7},{6,4},{7,5},{8,10},{9,11},{10,... | collective-permute-start | bytes 608264 | tf_op jit(solution)/shard_map/ppermute | solution.py:120
  92.2 13.2 %collective-permute-start.21 = (bf16[72,1472]{1,0:T(8,128)(2,1)S(1)}, bf16[72,1472]{1,0:T(8,128)(2,1)S(1)}, u32[]{:S(2)}, u32[]{:S(2)}) collective-permute-start(bf16[72,1472]{1,0:T(8,128)(2,1)S(1)} %get-tuple-element.92), channel_id=1, source_target_pairs={{0,6},{1,7},{2,4},{3,5},{4,2},{5,3},{6,0},{7,1},{8,14},{9,15},{10,... | collective-permute-start | bytes 635912 | tf_op jit(solution)/shard_map/ppermute | solution.py:120
  94.1 11.3 %collective-permute-start.20 = (bf16[72,1472]{1,0:T(8,128)(2,1)S(1)}, bf16[72,1472]{1,0:T(8,128)(2,1)S(1)}, u32[]{:S(2)}, u32[]{:S(2)}) collective-permute-start(bf16[72,1472]{1,0:T(8,128)(2,1)S(1)} %get-tuple-element.93), channel_id=1, source_target_pairs={{0,2},{1,3},{2,0},{3,1},{4,6},{5,7},{6,4},{7,5},{8,10},{9,11},{10,... | collective-permute-start | bytes 635912 | tf_op jit(solution)/shard_map/ppermute | solution.py:120
  95.8 7.6 %collective-permute-start.19 = (bf16[32,1408]{1,0:T(8,128)(2,1)S(1)}, bf16[32,1408]{1,0:T(8,128)(2,1)S(1)}, u32[]{:S(2)}, u32[]{:S(2)}) collective-permute-start(bf16[32,1408]{1,0:T(8,128)(2,1)S(1)} %get-tuple-element.89), channel_id=1, source_target_pairs={{0,24},{1,25},{2,26},{3,27},{4,28},{5,29},{6,30},{7,31},{8,0},{9,1... | collective-permute-start | bytes 270344 | tf_op jit(solution)/shard_map/ppermute | solution.py:125
  97.4 8.0 %collective-permute-start.18 = (bf16[32,1408]{1,0:T(8,128)(2,1)S(1)}, bf16[32,1408]{1,0:T(8,128)(2,1)S(1)}, u32[]{:S(2)}, u32[]{:S(2)}) collective-permute-start(bf16[32,1408]{1,0:T(8,128)(2,1)S(1)} %get-tuple-element.90), channel_id=1, source_target_pairs={{0,16},{1,17},{2,18},{3,19},{4,20},{5,21},{6,22},{7,23},{8,24},{9,... | collective-permute-start | bytes 270344 | tf_op jit(solution)/shard_map/ppermute | solution.py:125
  97.4 8.0 %collective-permute-start.17 = (bf16[32,1408]{1,0:T(8,128)(2,1)S(1)}, bf16[32,1408]{1,0:T(8,128)(2,1)S(1)}, u32[]{:S(2)}, u32[]{:S(2)}) collective-permute-start(bf16[32,1408]{1,0:T(8,128)(2,1)S(1)} %get-tuple-element.91), channel_id=1, source_target_pairs={{0,8},{1,9},{2,10},{3,11},{4,12},{5,13},{6,14},{7,15},{8,16},{9,17... | collective-permute-start | bytes 270344 | tf_op jit(solution)/shard_map/ppermute | solution.py:125
  106.1 8.6 %collective-permute-start.24 = (bf16[32,1472]{1,0:T(8,128)(2,1)S(1)}, bf16[32,1472]{1,0:T(8,128)(2,1)S(1)}, u32[]{:S(2)}, u32[]{:S(2)}) collective-permute-start(bf16[32,1472]{1,0:T(8,128)(2,1)S(1)} %get-tuple-element.86), channel_id=1, source_target_pairs={{0,24},{1,25},{2,26},{3,27},{4,28},{5,29},{6,30},{7,31},{8,0},{9,1... | collective-permute-start | bytes 282632 | tf_op jit(solution)/shard_map/ppermute | solution.py:125
  107.5 9.3 %collective-permute-start.23 = (bf16[32,1472]{1,0:T(8,128)(2,1)S(1)}, bf16[32,1472]{1,0:T(8,128)(2,1)S(1)}, u32[]{:S(2)}, u32[]{:S(2)}) collective-permute-start(bf16[32,1472]{1,0:T(8,128)(2,1)S(1)} %get-tuple-element.87), channel_id=1, source_target_pairs={{0,16},{1,17},{2,18},{3,19},{4,20},{5,21},{6,22},{7,23},{8,24},{9,... | collective-permute-start | bytes 282632 | tf_op jit(solution)/shard_map/ppermute | solution.py:125
  108.1 8.8 %copy-start.1 = (bf16[32,2880]{1,0:T(8,128)(2,1)S(1)}, bf16[32,2880]{1,0:T(8,128)(2,1)}, u32[]{:S(2)}) copy-start(bf16[32,2880]{1,0:T(8,128)(2,1)} %param.8) | copy-start | bytes 552964
  108.1 8.8 %copy-start.3 = (f32[2880]{0:T(1024)S(1)}, f32[2880]{0:T(1024)}, u32[]{:S(2)}) copy-start(f32[2880]{0:T(1024)} %param.9) | copy-start | bytes 34564
  108.1 8.7 %collective-permute-start.22 = (bf16[32,1472]{1,0:T(8,128)(2,1)S(1)}, bf16[32,1472]{1,0:T(8,128)(2,1)S(1)}, u32[]{:S(2)}, u32[]{:S(2)}) collective-permute-start(bf16[32,1472]{1,0:T(8,128)(2,1)S(1)} %get-tuple-element.88), channel_id=1, source_target_pairs={{0,8},{1,9},{2,10},{3,11},{4,12},{5,13},{6,14},{7,15},{8,16},{9,17... | collective-permute-start | bytes 282632 | tf_op jit(solution)/shard_map/ppermute | solution.py:125
